TPU v7x, 32 devices: a whole 2x2x4 slice. The times are simulated.
32 devices in a mesh: grp: 2 (over y), lat: 8 (over z, x), row: 2 (over core).
Axes of the slice: x: 2, y: 2, z: 4, core: 2. Of those that a mesh axis runs over, the one named last changes fastest.
Arguments:
- activations: bfloat16 [32, 128, 4096], P(('grp', 'row'), 'lat'), parts along dimension 0, may hold values from -6 to 6
- act_blocks: int32 [32, 4], P('grp'), parts along dimension 0, may hold values from -1 to 7, as said below
- dictionary: bfloat16 [4096, 4096], P(('grp', 'lat', 'row')), parts along dimension 0, may hold values from -0.09375 to 0.09375
- enc_bias: bfloat16 [4096], P(('grp', 'lat', 'row')), parts along dimension 0, may hold values from -1 to 1
- dec_bias: bfloat16 [8192], P('grp'), parts along dimension 0, may hold values from -3 to 3
Outputs:
- dict_grad: bfloat16 [4096, 4096], P(('grp', 'lat', 'row')), parts along dimension 0
There are 2 independent parts, one for each index of `grp`. A program takes and returns all parts, laid end to end along the dimension named above; each array names one. Nothing has to cross between parts.
Inputs may be any that keep to these rules, and one draw needn't show every extreme that they name: `act_blocks`: each row lists 1 to 4 distinct latent blocks first and -1 after them. Among the row blocks of either half (the first 8 and the rest) no latent block is listed by more than 4 of them, and in every draw some latent block is listed by exactly 4 row blocks of one half.
All inputs are finite; a program needn't handle non-finite values.
Results may differ from a plain program's by a relative error of at most 0.005.
Values may be sent and summed in bfloat16 or wider, within the bound.
No kernel may reach another device: no remote copies, remote signals or barrier semaphores. Data moves between devices by JAX's collectives and lax.ppermute only.
A program may use at most 128 MiB of HBM per device.

v0:
```python
from functools import partial

import jax
import jax.numpy as jnp
from jax import lax
from jax.sharding import PartitionSpec as P


def slot_tables(lists, block_count, slot_count):
    row_total = lists.shape[0]
    labels = jnp.arange(block_count, dtype=jnp.int32)
    matches = jnp.sum((lists[:, :, None] == labels[None, None, :]).astype(jnp.int32), axis=1)
    position = jnp.cumsum(matches, axis=0) - 1
    places = jnp.arange(slot_count, dtype=jnp.int32)
    hits = ((matches[:, :, None] == 1) & (position[:, :, None] == places[None, None, :])).astype(
        jnp.int32
    )
    row_ids = jnp.arange(row_total, dtype=jnp.int32)
    table = jnp.sum(hits * row_ids[:, None, None], axis=0)
    filled = jnp.sum(hits, axis=0)
    return (table, filled)


def encode_slot(dict_full, bias_full, slot_rows, is_filled):
    latent_width = dict_full.shape[0]

    def encode_active(inputs):
        preacts = jnp.einsum("rd,ld->rl", inputs, dict_full, preferred_element_type=jnp.float32)
        preacts = preacts + bias_full.astype(jnp.float32)
        latent_codes = jax.nn.softplus(preacts).astype(jnp.bfloat16)
        pieces = jnp.einsum(
            "rl,ld->rd", latent_codes, dict_full, preferred_element_type=jnp.float32
        )
        return (latent_codes, jax.nn.sigmoid(preacts), pieces.astype(jnp.bfloat16))

    def encode_vacant(inputs):
        return (
            jnp.zeros((inputs.shape[0], latent_width), jnp.bfloat16),
            jnp.zeros((inputs.shape[0], latent_width), jnp.float32),
            jnp.zeros_like(inputs),
        )

    return lax.cond(is_filled > 0, encode_active, encode_vacant, slot_rows)


def slope_slot(dict_full, err_rows, sigmas, is_filled):

    def slope_active(err_in, sig_in):
        code_grads = jnp.einsum("rd,ld->rl", err_in, dict_full, preferred_element_type=jnp.float32)
        return (code_grads * sig_in).astype(jnp.bfloat16)

    def slope_vacant(err_in, sig_in):
        return jnp.zeros(sig_in.shape, jnp.bfloat16)

    return lax.cond(is_filled > 0, slope_active, slope_vacant, err_rows, sigmas)


def body(activations, act_blocks, dictionary, enc_bias, dec_bias):
    lat_count = lax.axis_size("lat")
    row_count = lax.axis_size("row")
    lat_index = lax.axis_index("lat")
    row_index = lax.axis_index("row")
    half_blocks, rows_each, feature_dim = activations.shape
    list_width = act_blocks.shape[1]
    slot_count = list_width * half_blocks // lat_count
    block_rows = rows_each * lat_count
    flat_width = rows_each * feature_dim
    dict_full, bias_full = (
        lax.all_gather(dictionary, "row", axis=0, tiled=True),
        lax.all_gather(enc_bias, "row", axis=0, tiled=True),
    )
    flat_acts = activations.reshape(half_blocks, flat_width)
    bias_flat = jnp.tile(dec_bias.astype(jnp.float32), rows_each)
    centred = (flat_acts.astype(jnp.float32) - bias_flat[None, :]).astype(jnp.bfloat16)
    lists = act_blocks.reshape(row_count, half_blocks, list_width)
    tables, filled = jax.vmap(partial(slot_tables, block_count=lat_count, slot_count=slot_count))(
        lists
    )
    own_table = lax.dynamic_index_in_dim(tables, row_index, 0, keepdims=False)
    own_filled = lax.dynamic_index_in_dim(filled, row_index, 0, keepdims=False)
    mine_filled = lax.dynamic_index_in_dim(filled, lat_index, 1, keepdims=False)
    send_rows = own_table.T
    send_live = own_filled.T
    slot_flags = lax.dynamic_index_in_dim(mine_filled, row_index, 0, keepdims=False)
    wire_shape = (slot_count, block_rows, feature_dim)
    mask_bf = send_live.astype(jnp.bfloat16)[..., None]
    mask_f = send_live.astype(jnp.float32)[..., None]
    back_shape = send_rows.shape + (flat_width,)
    outgoing = (centred[send_rows] * mask_bf).reshape(wire_shape)
    items = lax.all_to_all(outgoing, "lat", split_axis=1, concat_axis=1, tiled=True)
    latent_codes, sigmas, pieces = lax.map(
        lambda bundle: encode_slot(dict_full, bias_full, bundle[0], bundle[1]), (items, slot_flags)
    )
    returned = lax.all_to_all(pieces, "lat", split_axis=1, concat_axis=1, tiled=True)
    returned = returned.reshape(back_shape).astype(jnp.float32) * mask_f
    rebuilt = jnp.zeros((half_blocks, flat_width), jnp.float32).at[send_rows].add(returned)
    errors = (rebuilt - centred.astype(jnp.float32)).astype(jnp.bfloat16)
    err_out = (errors[send_rows] * mask_bf).reshape(wire_shape)
    err_items = lax.all_to_all(err_out, "lat", split_axis=1, concat_axis=1, tiled=True)
    slopes = lax.map(
        lambda bundle: slope_slot(dict_full, bundle[0], bundle[1], bundle[2]),
        (err_items, sigmas, slot_flags),
    )
    total = jnp.einsum("srl,srd->ld", latent_codes, err_items, preferred_element_type=jnp.float32)
    total = total + jnp.einsum("srl,srd->ld", slopes, items, preferred_element_type=jnp.float32)
    grads = lax.psum_scatter(total / block_rows, "row", scatter_dimension=0, tiled=True)
    return grads.astype(jnp.bfloat16)


def solution(mesh):
    in_specs = (
        P(("grp", "row"), "lat", None),
        P("grp", None),
        P(("grp", "lat", "row"), None),
        P(("grp", "lat", "row")),
        P("grp"),
    )
    out_specs = P(("grp", "lat", "row"), None)
    return jax.shard_map(body, mesh=mesh, in_specs=in_specs, out_specs=out_specs, check_vma=False)
```

profile of v0, /device:TPU:0, one launch (start us, length us, event | category | flops | bytes accessed | tf_op | source)
XLA Modules:
  0.0 498.6 jit_solution(12925900510257038202)
XLA Ops:
  11.8 5.3 %gather_fusion = bf16[32,65536]{1,0:T(8,128)(2,1)} fusion(bf16[8,65536]{1,0:T(8,128)(2,1)S(1)} %subtract_convert_fusion.1, s32[1024]{0:T(1024)S(1)} %pad_clamp_fusion), kind=kCustom, calls=%fused_computation | custom fusion | bytes 8388736 | tf_op jit(solution)/shard_map/gather | solution.py:89
  17.1 5.6 %gather.11 = bf16[4,128,4096]{2,1,0:T(8,128)(2,1)} reshape(bf16[32,65536]{1,0:T(8,128)(2,1)} %gather_fusion) | data formatting | bytes 8388608 | tf_op jit(solution)/shard_map/gather | solution.py:89
  22.8 7.6 %copy_multiply_fusion.1 = bf16[4,128,4096]{2,0,1:T(4,128)(2,1)} fusion(bf16[4,128,4096]{2,1,0:T(8,128)(2,1)} %gather.11, bf16[4,128]{0,1:T(8,128)(2,1)S(1)} %bitcast.64), kind=kLoop, calls=%fused_computation.30 | loop fusion | flops 2097152 | bytes 8389632 | tf_op jit(solution)/shard_map/mul | solution.py:89
  30.5 7.4 %all-to-all-start = ((bf16[4,128,4096]{2,0,1:T(4,128)(2,1)}), bf16[4,128,4096]{2,0,1:T(4,128)(2,1)}, u32[]{:S(2)}, u32[]{:S(2)}) async-start(bf16[4,128,4096]{2,0,1:T(4,128)(2,1)} %copy_multiply_fusion.1), calls=%async_computation | async-start | bytes 8388608 | tf_op jit(solution)/shard_map/all_to_all | solution.py:90
  38.8 2.2 all-gather
  41.1 90.0 %all-to-all-done = bf16[4,128,4096]{2,0,1:T(4,128)(2,1)} async-done(((bf16[4,128,4096]{2,0,1:T(4,128)(2,1)}), bf16[4,128,4096]{2,0,1:T(4,128)(2,1)}, u32[]{:S(2)}, u32[]{:S(2)}) %all-to-all-start) | async-done | bytes 4194336 | tf_op jit(solution)/shard_map/all_to_all | solution.py:90
  131.1 6.4 %copy.50 = bf16[4,128,4096]{2,1,0:T(8,128)(2,1)} copy(bf16[4,128,4096]{2,0,1:T(4,128)(2,1)} %all-to-all-done) | data formatting | bytes 8388608 | tf_op jit(solution)/shard_map/while | solution.py:91
  137.6 26.5 %while.24 = (s32[]{:T(128)}, bf16[4,128,256]{2,1,0:T(8,128)(2,1)S(1)}, f32[4,128,256]{2,1,0:T(8,128)}, bf16[4,128,4096]{2,1,0:T(8,128)(2,1)}, s32[4]{0:T(128)S(1...) while((s32[]{:T(128)}, ...), condition=%wide.region_7.8_spmd, body=%wide.region_4.7_spmd.sunk | while | flops 537985280 | bytes 17764568 | solution.py:91
  138.9 3.5 conditional.4
  139.0 2.9 convolution_add_fusion
  145.5 3.5 conditional.4
  145.6 2.9 convolution_add_fusion
  152.2 3.5 conditional.4
  152.2 2.9 convolution_add_fusion
  158.8 3.5 conditional.4
  158.9 2.9 convolution_add_fusion
  164.1 5.5 %copy.51 = bf16[4,128,4096]{2,0,1:T(4,128)(2,1)S(1)} copy(bf16[4,128,4096]{2,1,0:T(8,128)(2,1)} %get-tuple-element.154) | data formatting | bytes 8388608 | tf_op jit(solution)/shard_map/while | solution.py:91
  169.7 90.6 %all_to_all.15 = bf16[4,128,4096]{2,0,1:T(4,128)(2,1)S(1)} all-to-all(bf16[4,128,4096]{2,0,1:T(4,128)(2,1)S(1)} %copy.51), channel_id=1, replica_groups=mesh['grp'=2,'lat'=8,'row'=2] {'lat'}, dimensions={1} | all-to-all | bytes 8388608 | tf_op jit(solution)/shard_map/all_to_all | solution.py:94
  260.3 5.7 %copy_convert_fusion = f32[4,128,4096]{2,1,0:T(8,128)} fusion(bf16[4,128,4096]{2,0,1:T(4,128)(2,1)S(1)} %all_to_all.15), kind=kLoop, calls=%fused_computation.29 | loop fusion | flops 2097152 | bytes 12582912 | tf_op jit(solution)/shard_map/convert_element_type | solution.py:95
  266.0 7.5 %reshape.44 = f32[4,8,65536]{2,1,0:T(8,128)} reshape(f32[4,128,4096]{2,1,0:T(8,128)} %copy_convert_fusion) | data formatting | bytes 16777216 | tf_op jit(solution)/shard_map/convert_element_type | solution.py:95
  273.5 7.2 %multiply_bitcast_fusion = f32[32,65536]{1,0:T(8,128)} fusion(f32[4,8,65536]{2,1,0:T(8,128)} %reshape.44, f32[4,8]{1,0:T(4,128)S(1)} %get-tuple-element.245), kind=kLoop, calls=%fused_computation.23 | loop fusion | flops 2097152 | bytes 16777344 | tf_op jit(solution)/shard_map/mul | solution.py:95
  280.8 46.9 %scatter_fusion = f32[8,65536]{1,0:T(8,128)S(1)} fusion(f32[8,65536]{1,0:T(8,128)S(1)} %broadcast_in_dim.61, s32[32]{0:T(128)S(1)} %reshape.47, f32[32,65536]{1,0:T(8,128)} %multiply_bitcast_fusion), kind=kCustom, calls=%fused_computation.2 | custom fusion | flops 2097152 | bytes 25165952 | tf_op jit(solution)/shard_map/scatter-add | solution.py:96
  329.6 5.3 %gather_fusion.1 = bf16[32,65536]{1,0:T(8,128)(2,1)} fusion(bf16[8,65536]{1,0:T(8,128)(2,1)S(1)} %subtract_convert_fusion, s32[1024]{0:T(1024)S(1)} %pad_clamp_fusion), kind=kCustom, calls=%fused_computation.1 | custom fusion | bytes 8388736 | tf_op jit(solution)/shard_map/gather | solution.py:98
  334.8 5.8 %gather.13 = bf16[4,128,4096]{2,1,0:T(8,128)(2,1)} reshape(bf16[32,65536]{1,0:T(8,128)(2,1)} %gather_fusion.1) | data formatting | bytes 8388608 | tf_op jit(solution)/shard_map/gather | solution.py:98
  340.7 5.7 %copy_multiply_fusion = bf16[4,128,4096]{2,0,1:T(4,128)(2,1)S(1)} fusion(bf16[4,128,4096]{2,1,0:T(8,128)(2,1)} %gather.13, bf16[4,128]{0,1:T(8,128)(2,1)S(1)} %bitcast.65), kind=kLoop, calls=%fused_computation.28 | loop fusion | flops 2097152 | bytes 8389632 | tf_op jit(solution)/shard_map/mul | solution.py:98
  346.4 94.1 %all_to_all.16 = bf16[4,128,4096]{2,0,1:T(4,128)(2,1)S(1)} all-to-all(bf16[4,128,4096]{2,0,1:T(4,128)(2,1)S(1)} %copy_multiply_fusion), channel_id=1, replica_groups=mesh['grp'=2,'lat'=8,'row'=2] {'lat'}, dimensions={1} | all-to-all | bytes 8388608 | tf_op jit(solution)/shard_map/all_to_all | solution.py:99
  440.4 4.3 copy.55
  444.7 14.1 %while.25 = (s32[]{:T(128)}, bf16[4,128,256]{2,1,0:T(8,128)(2,1)S(1)}, s32[4]{0:T(128)S(1)}, bf16[4,128,4096]{2,1,0:T(8,128)(2,1)}, bf16[256,4096]{1,0:T(8,128)(...) while((s32[]{:T(128)}, bf16[4,128,256]{2,1,0:T(8,128)(2,1)S(1)}, s32[4]{0:T(128)S(1)}, ...), condition=%wide.region_12.13_spmd, body=%wide.region_9.12_spmd.sunk | while | flops 268500992 | bytes 3474587 | solution.py:100
  458.9 7.4 %convolution_bitcast_fusion = f32[256,4096]{1,0:T(8,128)S(1)} fusion(bf16[4,128,256]{2,1,0:T(8,128)(2,1)S(1)} %get-tuple-element.156, bf16[4,128,4096]{2,0,1:T(4,128)(2,1)} %all-to-all-done), kind=kOutput, calls=%fused_computation.24 | convolution fusion | flops 1073741824 | bytes 8650752 | tf_op jit(solution)/shard_map/srl,srd->ld/dot_general | solution.py:105
  466.3 7.2 %fusion.13 = f32[256,4096]{1,0:T(8,128)} fusion(f32[256,4096]{1,0:T(8,128)S(1)} %convolution_bitcast_fusion, bf16[4,128,256]{2,1,0:T(8,128)(2,1)S(1)} %copy-done.6, bf16[4,128,4096]{2,0,1:T(4,128)(2,1)S(1)} %copy-done.3), kind=kOutput, calls=%fused_computation.27 | convolution fusion | flops 1075838976 | bytes 12845056 | tf_op jit(solution)/shard_map/srl,srd->ld/dot_general | solution.py:104
  473.6 15.1 %reduce-scatter.2.cloned.1.call-done = f32[128,4096]{1,0:T(8,128)} async-done(((f32[256,4096]{1,0:T(8,128)}), f32[128,4096]{1,0:T(8,128)}) %reduce-scatter.2.cloned.1.call-update) | async-done | bytes 2097168 | tf_op jit(solution)/shard_map/reduce_scatter | solution.py:106
  488.6 2.7 convert_element_type.96
  (100 shorter events, 39.6 us)
Async XLA Ops:
  6.5 3.7 copy-start.7
  10.3 1.3 copy-start.4
  30.5 8.4 %copy-start.8 = (bf16[128]{0:T(256)(128)(2,1)S(1)}, bf16[128]{0:T(256)(128)(2,1)}, u32[]{:S(2)}) copy-start(bf16[128]{0:T(256)(128)(2,1)} %param.16) | copy-start | bytes 772
  30.5 100.7 %all-to-all-start = ((bf16[4,128,4096]{2,0,1:T(4,128)(2,1)}), bf16[4,128,4096]{2,0,1:T(4,128)(2,1)}, u32[]{:S(2)}, u32[]{:S(2)}) async-start(bf16[4,128,4096]{2,0,1:T(4,128)(2,1)} %copy_multiply_fusion.1), calls=%async_computation | async-start | bytes 8388608 | tf_op jit(solution)/shard_map/all_to_all | solution.py:90
  37.8 99.7 %all-gather.3.cloned.1.call-start = ((), (), s32[]{:S(2)}) async-start(), calls=%async_computation.4 | async-start | bytes 3145728 | tf_op jit(solution)/shard_map/all_gather | solution.py:69
  38.6 450.1 %reduce-scatter.2.cloned.1.call-start = ((), (), s32[]{:S(2)}) async-start(), calls=%async_computation.5 | async-start | bytes 6291456 | tf_op jit(solution)/shard_map/reduce_scatter | solution.py:106
  138.9 2.9 copy-start
  145.6 2.9 copy-start
  152.2 2.9 copy-start
  158.8 2.9 copy-start
  164.1 5.5 %copy-start.5 = (bf16[4,128,256]{2,1,0:T(8,128)(2,1)}, bf16[4,128,256]{2,1,0:T(8,128)(2,1)S(1)}, u32[]{:S(2)}) copy-start(bf16[4,128,256]{2,1,0:T(8,128)(2,1)S(1)} %get-tuple-element.153) | copy-start | bytes 786436
  440.4 4.3 copy-start.2
  440.4 4.3 copy-start.1
  458.9 7.4 %copy-start.3 = (bf16[4,128,4096]{2,0,1:T(4,128)(2,1)S(1)}, bf16[4,128,4096]{2,0,1:T(4,128)(2,1)}, u32[]{:S(2)}) copy-start(bf16[4,128,4096]{2,0,1:T(4,128)(2,1)} %copy-done.2) | copy-start | bytes 12582916
  458.9 7.4 %copy-start.6 = (bf16[4,128,256]{2,1,0:T(8,128)(2,1)S(1)}, bf16[4,128,256]{2,1,0:T(8,128)(2,1)}, u32[]{:S(2)}) copy-start(bf16[4,128,256]{2,1,0:T(8,128)(2,1)} %copy-done.5) | copy-start | bytes 786436
Sparse Core Ops, SparseCore 0:
  40.2 11.9 all-gather.2
  473.7 14.9 reduce-scatter.1
where the time goes:
time: 506 us; the launch traced here: 499 us
  blocking collectives  187 us (37%)
  waiting for transfers between devices  106 us (21%)
  other arithmetic  79.9 us (16%)
  local copies, waits for them, and re-layouts  61.9 us (12%)
  matrix products  36.4 us (7%)
  between operations  14.1 us (3%)
  starting transfers between devices  7.46 us (1%)
  loops' own time  6.22 us (1%)
    all_to_all x1, blocking collectives, body(): lax.all_to_all(err_out, 'lat', split_axis=1, concat_axis=1, tiled=True)  94.1 us
    all_to_all x1, blocking collectives, body(): lax.all_to_all(pieces, 'lat', split_axis=1, concat_axis=1, tiled=True)  90.6 us
    all_to_all x1, waiting for transfers between devices, body(): lax.all_to_all(outgoing, 'lat', split_axis=1, concat_axis=1, tiled=True)  90 us
    scatter-add x1, other arithmetic, body(): jnp.zeros((half_blocks, flat_width), jnp.float32).at[send_rows]  46.9 us
    reduce_scatter x1, waiting for transfers between devices, body(): lax.psum_scatter(total / block_rows, 'row', scatter_dimension=0, tiled=True)  15.1 us
    while x2, local copies, waits for them, and re-layouts, body(): lax.map(lambda bundle: encode_slot(dict_full, bias_full, bundle[0], bundl...  11.9 us
    dot_general x4, matrix products, encode_active(): jnp.einsum('rd,ld->rl', inputs, dict_full, preferred_element_type=jnp.flo...  11.6 us
    gather x2, local copies, waits for them, and re-layouts, body(): err_out = (errors[send_rows] * mask_bf).reshape(wire_shape)  11.1 us
  transfers between devices with their start and end apart: 3, of which 2 were waited for; matrix products, arithmetic and copies ran while one was open for 1% of the time, Pallas kernels for 0%

commit v1 on v0

--- a/solution.py
+++ b/solution.py
@@ -4,6 +4,8 @@
 import jax.numpy as jnp
 from jax import lax
 from jax.sharding import PartitionSpec as P
+
+GATHER_LIMIT = 32 * 2**20
 
 
 def slot_tables(lists, block_count, slot_count):
@@ -55,7 +57,7 @@
     return lax.cond(is_filled > 0, slope_active, slope_vacant, err_rows, sigmas)
 
 
-def body(activations, act_blocks, dictionary, enc_bias, dec_bias):
+def exchange_body(activations, act_blocks, dictionary, enc_bias, dec_bias):
     lat_count = lax.axis_size("lat")
     row_count = lax.axis_size("row")
     lat_index = lax.axis_index("lat")
@@ -107,6 +109,102 @@
     return grads.astype(jnp.bfloat16)
 
 
+def ring_body(activations, act_blocks, dictionary, enc_bias, dec_bias):
+    count = lax.axis_size("lat")
+    lat_index = lax.axis_index("lat")
+    row_index = lax.axis_index("row")
+    half_blocks, rows_each, width = activations.shape
+    latents = dictionary.shape[0]
+    cut = latents // 2
+    block_rows = rows_each * count
+    half = count // 2
+
+    order = list(range(0, count, 2)) + list(range(count - 1, 0, -2))
+    place_of = [order.index(i) for i in range(count)]
+    order_table = jnp.array(order, jnp.int32)
+    place = jnp.array(place_of, jnp.int32)[lat_index]
+    right_pairs = [(order[i], order[(i + 1) % count]) for i in range(count)]
+    left_pairs = [(b, a) for a, b in right_pairs]
+
+    def to_right(x):
+        return lax.ppermute(x, "lat", right_pairs)
+
+    def to_left(x):
+        return lax.ppermute(x, "lat", left_pairs)
+
+    def to_core(x):
+        return lax.ppermute(x, "row", [(0, 1), (1, 0)])
+
+    def owner(step):
+        return order_table[(place + step) % count]
+
+    words = {0: dictionary}
+    for step in range(1, half):
+        words[-step] = to_right(words[1 - step])
+        words[step] = to_left(words[step - 1])
+    words[half] = jnp.concatenate([to_right(words[1 - half][:cut]), to_left(words[half - 1][cut:])])
+
+    centred = (activations.astype(jnp.float32) - dec_bias.astype(jnp.float32)).astype(jnp.bfloat16)
+    centred = centred.reshape(half_blocks * rows_each, width)
+    rows = jnp.concatenate([centred, to_core(centred)])
+    biases = lax.all_gather(enc_bias, "lat", axis=0).astype(jnp.float32)
+    lists = act_blocks.reshape(2, half_blocks, act_blocks.shape[1])
+    lists = jnp.where(row_index == 0, lists, lists[::-1]).reshape(2 * half_blocks, -1)
+
+    steps = [0] + [s for t in range(1, half) for s in (-t, t)] + [half]
+    codes, sigmas = {}, {}
+    rebuilt = None
+    for step in steps:
+        block = owner(step)
+        bias = lax.dynamic_index_in_dim(biases, block, 0, keepdims=False)
+        listed = jnp.repeat(jnp.any(lists == block, axis=1), rows_each)[:, None]
+        preacts = jnp.einsum("rd,ld->rl", rows, words[step], preferred_element_type=jnp.float32)
+        preacts = preacts + bias
+        codes[step] = jnp.where(listed, jax.nn.softplus(preacts), 0.0).astype(jnp.bfloat16)
+        sigmas[step] = jnp.where(listed, jax.nn.sigmoid(preacts), 0.0)
+        pieces = jnp.einsum(
+            "rl,ld->rd", codes[step], words[step], preferred_element_type=jnp.float32
+        )
+        rebuilt = pieces if rebuilt is None else rebuilt + pieces
+    rebuilt = rebuilt.astype(jnp.bfloat16)
+    swapped = to_core(rebuilt)
+    middle = half_blocks * rows_each
+    swapped = jnp.concatenate([swapped[middle:], swapped[:middle]])
+    errors = rebuilt.astype(jnp.float32) + swapped.astype(jnp.float32) - rows.astype(jnp.float32)
+    errors = errors.astype(jnp.bfloat16)
+
+    def grads_of(step):
+        slopes = jnp.einsum("rd,ld->rl", errors, words[step], preferred_element_type=jnp.float32)
+        slopes = (slopes * sigmas[step]).astype(jnp.bfloat16)
+        total = jnp.einsum("rl,rd->ld", codes[step], errors, preferred_element_type=jnp.float32)
+        return total + jnp.einsum("rl,rd->ld", slopes, rows, preferred_element_type=jnp.float32)
+
+    def send(x):
+        return x.astype(jnp.bfloat16)
+
+    far = grads_of(half)
+    up = (to_right(send(far[:cut])), None)
+    down = (None, to_left(send(far[cut:])))
+    for step in range(half - 1, 0, -1):
+        ahead, behind = grads_of(step), grads_of(-step)
+        parts = []
+        for total, came in ((ahead, up), (behind, down)):
+            pieces = (total[:cut], total[cut:])
+            parts.append(
+                [send(p if c is None else p + c.astype(jnp.float32)) for p, c in zip(pieces, came)]
+            )
+        up = tuple(to_right(p) for p in parts[0])
+        down = tuple(to_left(p) for p in parts[1])
+    own = grads_of(0)
+    halves = []
+    for i, part in enumerate((own[:cut], own[cut:])):
+        for came in (up[i], down[i]):
+            if came is not None:
+                part = part + came.astype(jnp.float32)
+        halves.append(part)
+    return (jnp.concatenate(halves) / block_rows).astype(jnp.bfloat16)
+
+
 def solution(mesh):
     in_specs = (
         P(("grp", "row"), "lat", None),
@@ -116,4 +214,12 @@
         P("grp"),
     )
     out_specs = P(("grp", "lat", "row"), None)
+    lat_count, row_count = mesh.shape["lat"], mesh.shape["row"]
+
+    def body(activations, act_blocks, dictionary, enc_bias, dec_bias):
+        gathered = lat_count * dictionary.size * dictionary.dtype.itemsize
+        fits = row_count == 2 and lat_count % 2 == 0 and gathered <= GATHER_LIMIT
+        step = ring_body if fits else exchange_body
+        return step(activations, act_blocks, dictionary, enc_bias, dec_bias)
+
     return jax.shard_map(body, mesh=mesh, in_specs=in_specs, out_specs=out_specs, check_vma=False)

time: 506 us -> 260 us (0.51); the launches traced: 499 us -> 259 us
  blocking collectives: 187 us -> 21.1 us
  other arithmetic: 79.9 us -> 20 us
  local copies, waits for them, and re-layouts: 61.9 us -> 11.7 us
  matrix products: 36.4 us -> 74.6 us
  waiting for transfers between devices: 106 us -> 85.4 us
  starting transfers between devices: 7.46 us -> 24.2 us
  between operations: 14.1 us -> 22.2 us
  loops' own time: 6.22 us -> 0 us
    all_to_all x2 -> x0, blocking collectives: 185 us -> none  [the longest x1 94.1 us: body(): lax.all_to_all(err_out, 'lat', split_axis=1, concat_axis=1, tiled=True)]
    all_to_all x1 -> x0, waiting for transfers between devices: 90 us -> none  [body(): lax.all_to_all(outgoing, 'lat', split_axis=1, concat_axis=1, tiled=True)]
    ppermute x0 -> x24, waiting for transfers between devices: none -> 85.4 us  [the longest x11 63.1 us: to_right(): return lax.ppermute(x, 'lat', right_pairs)]
    scatter-add x1 -> x0, other arithmetic: 46.9 us -> none  [body(): jnp.zeros((half_blocks, flat_width), jnp.float32).at[send_rows]]
    dot_general x14 -> x32, matrix products: 36.4 us -> 74.6 us  [the longest x8 41.9 us: grads_of(): jnp.einsum('rl,rd->ld', slopes, rows, preferred_element_type=jnp.float32)]
    ppermute x0 -> x24, starting transfers between devices: none -> 24.2 us  [the longest x11 18.9 us: to_left(): return lax.ppermute(x, 'lat', left_pairs)]
    gather x4 -> x0, local copies, waits for them, and re-layouts: 22 us -> none  [the longest x2 11.1 us: body(): err_out = (errors[send_rows] * mask_bf).reshape(wire_shape)]
    mul x3 -> x0, other arithmetic: 20.5 us -> none  [the longest x1 7.61 us: body(): outgoing = (centred[send_rows] * mask_bf).reshape(wire_shape)]
  transfers between devices with their start and end apart: 3 -> 24, of which waited for: 2 -> 11; matrix products, arithmetic and copies ran while one was open for 1% -> 31% of each run, Pallas kernels for 0% -> 0%
where the time goes in v1:
time: 260 us; the launch traced here: 259 us
  waiting for transfers between devices  85.4 us (33%)
  matrix products  74.6 us (29%)
  starting transfers between devices  24.2 us (9%)
  between operations  22.2 us (9%)
  blocking collectives  21.1 us (8%)
  other arithmetic  20 us (8%)
  local copies, waits for them, and re-layouts  11.7 us (4%)
    ppermute x11, waiting for transfers between devices, to_right(): return lax.ppermute(x, 'lat', right_pairs)  63.1 us
    dot_general x8, matrix products, grads_of(): jnp.einsum('rl,rd->ld', slopes, rows, preferred_element_type=jnp.float32)  41.9 us
    all_gather x1, blocking collectives, ring_body(): biases = lax.all_gather(enc_bias, 'lat', axis=0).astype(jnp.float32)  21.1 us
    ppermute x11, starting transfers between devices, to_left(): return lax.ppermute(x, 'lat', left_pairs)  18.9 us
    ppermute x11, waiting for transfers between devices, to_left(): return lax.ppermute(x, 'lat', left_pairs)  18.2 us
    dot_general x8, matrix products, grads_of(): jnp.einsum('rl,rd->ld', codes[step], errors, preferred_element_type=jnp.f...  15.5 us
    dot_general x8, matrix products, ring_body(): jnp.einsum('rl,ld->rd', codes[step], words[step], preferred_element_type=...  8.86 us
    dot_general x8, matrix products, ring_body(): jnp.einsum('rd,ld->rl', rows, words[step], preferred_element_type=jnp.flo...  8.37 us
  transfers between devices with their start and end apart: 24, of which 11 were waited for; matrix products, arithmetic and copies ran while one was open for 31% of the time, Pallas kernels for 0%

profile of v1, /device:TPU:0, one launch (start us, length us, event | category | flops | bytes accessed | tf_op | source)
XLA Modules:
  0.0 259.2 jit_solution(3312329710484709068)
XLA Ops:
  0.0 3.1 %collective-permute-start.1 = (bf16[128,4096]{1,0:T(8,128)(2,1)}, bf16[128,4096]{1,0:T(8,128)(2,1)}, u32[]{:S(2)}, u32[]{:S(2)}) collective-permute-start(bf16[128,4096]{1,0:T(8,128)(2,1)} %param.9), channel_id=1, source_target_pairs={{0,4},{4,8},{8,12},{12,14},{14,10},{10,6},{6,2},{2,0},{1,5},{5,9},... | collective-permute-start | bytes 3145736 | tf_op jit(solution)/shard_map/ppermute | solution.py:130
  13.5 5.0 %compare_reduce_fusion.2 = (pred[2,8]{1,0:T(4,128)(4,1)S(1)}, pred[2,8]{1,0:T(4,128)(4,1)S(1)}, pred[2,8]{1,0:T(4,128)(4,1)S(1)}, pred[2,8]{1,0:T(4,128)(4,1)S(1...) fusion(s32[]{:T(128)} %bitcast.13, s32[]{:T(128)} %bitcast.17, ...), kind=kLoop, calls=%fused_computation.162 | loop fusion | flops 960 | bytes 673 | tf_op jit(solution)/shard_map/reduce_or | solution.py:160
  28.5 21.1 %all-gather.1 = bf16[8,1,128]{2,1,0:T(2,128)(2,1)S(1)} all-gather(bf16[1,1,128]{2,1,0:T(2,128)(2,1)S(1)} %bitcast.87), channel_id=2, replica_groups=mesh['grp'=2,'lat'=8,'row'=2] {'lat'}, dimensions={0}, use_global_device_ids=true | all-gather | bytes 2304 | tf_op jit(solution)/shard_map/all_gather | solution.py:150
  61.5 2.0 collective-permute-start.4
  63.5 2.0 convolution_add_fusion.3
  67.5 2.0 convolution_add_fusion.2
  69.5 15.5 %collective-permute-done.4 = bf16[128,4096]{1,0:T(8,128)(2,1)S(1)} collective-permute-done((bf16[128,4096]{1,0:T(8,128)(2,1)}, bf16[128,4096]{1,0:T(8,128)(2,1)S(1)}, u32[]{:S(2)}, u32[]{:S(2)}) %collective-permute-start.4) | collective-permute-done | bytes 1048608 | tf_op jit(solution)/shard_map/ppermute | solution.py:133
  85.1 2.0 collective-permute-start.6
  90.4 20.7 %collective-permute-done.5 = bf16[128,4096]{1,0:T(8,128)(2,1)S(1)} collective-permute-done((bf16[128,4096]{1,0:T(8,128)(2,1)S(1)}, bf16[128,4096]{1,0:T(8,128)(2,1)S(1)}, u32[]{:S(2)}, u32[]{:S(2)}) %collective-permute-start.5) | collective-permute-done | bytes 1048608 | tf_op jit(solution)/shard_map/ppermute | solution.py:130
  111.3 2.2 collective-permute-start.8
  115.8 4.6 %collective-permute-done.7 = bf16[64,4096]{1,0:T(8,128)(2,1)S(1)} collective-permute-done((bf16[64,4096]{1,0:T(8,128)(2,1)S(1)}, bf16[64,4096]{1,0:T(8,128)(2,1)S(1)}, u32[]{:S(2)}, u32[]{:S(2)}) %collective-permute-start.7) | collective-permute-done | bytes 524320 | tf_op jit(solution)/shard_map/ppermute | solution.py:130
  123.5 4.1 %collective-permute-done.9 = bf16[256,4096]{1,0:T(8,128)(2,1)S(1)} collective-permute-done((bf16[256,4096]{1,0:T(8,128)(2,1)S(1)}, bf16[256,4096]{1,0:T(8,128)(2,1)S(1)}, u32[]{:S(2)}, u32[]{:S(2)}) %collective-permute-start.9) | collective-permute-done | bytes 2097184 | tf_op jit(solution)/shard_map/ppermute | solution.py:136
  140.6 4.9 %fusion.4 = bf16[128,4096]{1,0:T(8,128)(2,1)} fusion(f32[128,4096]{1,0:T(8,128)} %fusion.130, bf16[256,4096]{1,0:T(8,128)(2,1)S(1)} %subtract_convert_fusion, bf16[128,4096]{1,0:T(8,128)(2,1)} %copy-done.8, f32[256,128]{1,0:T(8,128)} %copy-done.17, pred[256]{0:T(512)(128)(4,1)S(1)} %broadcast_in_dim.155, bf16[128,4096]{1,0:T(8,128)(2,1)} %copy-done, ...), kind=kOutput, calls=%fused_computation.16 | convolution fusion | flops 542310400 | bytes 8519936 | tf_op jit(solution)/shard_map/rl,rd->ld/dot_general | solution.py:180
  145.5 2.3 fusion.159
  147.9 5.3 %convolution_add_fusion.8 = f32[128,4096]{1,0:T(8,128)} fusion(f32[128,4096]{1,0:T(8,128)} %fusion.134, bf16[256,4096]{1,0:T(8,128)(2,1)S(1)} %subtract_convert_fusion, bf16[128,4096]{1,0:T(8,128)(2,1)} %copy-done.7, f32[256,128]{1,0:T(8,128)} %copy-done.16, pred[256]{0:T(512)(128)(4,1)S(1)} %broadcast_in_dim.152, bf16[128,4096]{1,0:T(8,128)(2,1)} %copy-done, ...), kind=kOutput, calls=%fused_computation.12 | convolution fusion | flops 541786112 | bytes 9568512 | tf_op jit(solution)/shard_map/rl,rd->ld/dot_general | solution.py:180
  153.2 2.1 slice.142
  155.2 2.0 collective-permute-start.20
  157.3 5.4 %convolution_add_fusion.4 = f32[128,4096]{1,0:T(8,128)} fusion(f32[128,4096]{1,0:T(8,128)} %fusion.138, bf16[256,4096]{1,0:T(8,128)(2,1)S(1)} %subtract_convert_fusion, bf16[128,4096]{1,0:T(8,128)(2,1)} %copy-done.6, f32[256,128]{1,0:T(8,128)} %copy-done.12, pred[256]{0:T(512)(128)(4,1)S(1)} %copy-done.20, bf16[128,4096]{1,0:T(8,128)(2,1)} %copy-done, ...), kind=kOutput, calls=%fused_computation.8 | convolution fusion | flops 541786112 | bytes 9568512 | tf_op jit(solution)/shard_map/rl,rd->ld/dot_general | solution.py:180
  162.6 2.1 slice.143
  166.7 5.3 %convolution_add_fusion.9 = f32[128,4096]{1,0:T(8,128)} fusion(f32[128,4096]{1,0:T(8,128)} %fusion.141, bf16[256,4096]{1,0:T(8,128)(2,1)S(1)} %subtract_convert_fusion, bf16[128,4096]{1,0:T(8,128)(2,1)} %copy-done.10, f32[256,128]{1,0:T(8,128)} %copy-done.15, pred[256]{0:T(512)(128)(4,1)S(1)} %broadcast_in_dim.146, bf16[128,4096]{1,0:T(8,128)(2,1)} %copy-done, ...), kind=kOutput, calls=%fused_computation.13 | convolution fusion | flops 541786112 | bytes 9568512 | tf_op jit(solution)/shard_map/rl,rd->ld/dot_general | solution.py:180
  172.0 5.2 %convolution_add_fusion.10 = f32[128,4096]{1,0:T(8,128)} fusion(f32[128,4096]{1,0:T(8,128)} %fusion.148, bf16[256,4096]{1,0:T(8,128)(2,1)S(1)} %subtract_convert_fusion, bf16[128,4096]{1,0:T(8,128)(2,1)} %collective-permute-done.2, f32[256,128]{1,0:T(8,128)S(1)} %convolution_add_fusion.17, pred[256]{0:T(512)(128)(4,1)S(1)} %copy-done.25, ...), kind=kOutput, calls=%fused_computation.14 | convolution fusion | flops 541786112 | bytes 9568512 | tf_op jit(solution)/shard_map/rl,rd->ld/dot_general | solution.py:180
  177.3 5.3 %convolution_add_fusion.5 = f32[128,4096]{1,0:T(8,128)} fusion(f32[128,4096]{1,0:T(8,128)} %fusion.145, bf16[256,4096]{1,0:T(8,128)(2,1)S(1)} %subtract_convert_fusion, bf16[128,4096]{1,0:T(8,128)(2,1)} %copy-done.11, f32[256,128]{1,0:T(8,128)S(1)} %convolution_add_fusion.16, pred[256]{0:T(512)(128)(4,1)S(1)} %copy-done.27, bf16[128,4096]{1,0:T(8,128)(2,1)} %copy-done, ...), kind=kOutput, calls=%fused_computation.9 | convolution fusion | flops 541786112 | bytes 9568512 | tf_op jit(solution)/shard_map/rl,rd->ld/dot_general | solution.py:180
  184.5 5.3 %convolution_add_fusion.6 = f32[128,4096]{1,0:T(8,128)} fusion(f32[128,4096]{1,0:T(8,128)} %fusion.151, bf16[256,4096]{1,0:T(8,128)(2,1)S(1)} %subtract_convert_fusion, bf16[128,4096]{1,0:T(8,128)(2,1)} %collective-permute-done.1, f32[256,128]{1,0:T(8,128)S(1)} %convolution_add_fusion.18, pred[256]{0:T(512)(128)(4,1)S(1)} %copy-done.22, ...), kind=kOutput, calls=%fused_computation.10 | convolution fusion | flops 541786112 | bytes 9568512 | tf_op jit(solution)/shard_map/rl,rd->ld/dot_general | solution.py:180
  192.9 2.0 collective-permute-start.21
  195.0 9.5 %collective-permute-done.11 = bf16[64,4096]{1,0:T(8,128)(2,1)S(1)} collective-permute-done((bf16[64,4096]{1,0:T(8,128)(2,1)S(1)}, bf16[64,4096]{1,0:T(8,128)(2,1)S(1)}, u32[]{:S(2)}, u32[]{:S(2)}) %collective-permute-start.11) | collective-permute-done | bytes 524320 | tf_op jit(solution)/shard_map/ppermute | solution.py:130
  211.4 9.3 %collective-permute-done.12 = bf16[64,4096]{1,0:T(8,128)(2,1)S(1)} collective-permute-done((bf16[64,4096]{1,0:T(8,128)(2,1)S(1)}, bf16[64,4096]{1,0:T(8,128)(2,1)S(1)}, u32[]{:S(2)}, u32[]{:S(2)}) %collective-permute-start.12) | collective-permute-done | bytes 524320 | tf_op jit(solution)/shard_map/ppermute | solution.py:130
  220.7 8.6 %collective-permute-done.18 = bf16[64,4096]{1,0:T(8,128)(2,1)S(1)} collective-permute-done((bf16[64,4096]{1,0:T(8,128)(2,1)S(1)}, bf16[64,4096]{1,0:T(8,128)(2,1)S(1)}, u32[]{:S(2)}, u32[]{:S(2)}) %collective-permute-start.18) | collective-permute-done | bytes 524320 | tf_op jit(solution)/shard_map/ppermute | solution.py:130
  237.6 5.2 %convolution_add_fusion.11 = f32[128,4096]{1,0:T(8,128)} fusion(f32[128,4096]{1,0:T(8,128)} %fusion.154, bf16[256,4096]{1,0:T(8,128)(2,1)S(1)} %subtract_convert_fusion, bf16[128,4096]{1,0:T(8,128)(2,1)} %param.9, f32[256,128]{1,0:T(8,128)S(1)} %copy-done.14, pred[256]{0:T(512)(128)(4,1)S(1)} %broadcast_in_dim.134, bf16[128,4096]{1,0:T(8,128)(2,1)} %copy-done, ...), kind=kOutput, calls=%fused_computation.15 | convolution fusion | flops 541786112 | bytes 9568512 | tf_op jit(solution)/shard_map/rl,rd->ld/dot_general | solution.py:180
  242.9 2.7 %collective-permute-done.13 = bf16[64,4096]{1,0:T(8,128)(2,1)} collective-permute-done((bf16[64,4096]{1,0:T(8,128)(2,1)}, bf16[64,4096]{1,0:T(8,128)(2,1)}, u32[]{:S(2)}, u32[]{:S(2)}) %collective-permute-start.13) | collective-permute-done | bytes 524320 | tf_op jit(solution)/shard_map/ppermute | solution.py:130
  245.6 7.6 %collective-permute-done.19 = bf16[64,4096]{1,0:T(8,128)(2,1)} collective-permute-done((bf16[64,4096]{1,0:T(8,128)(2,1)}, bf16[64,4096]{1,0:T(8,128)(2,1)}, u32[]{:S(2)}, u32[]{:S(2)}) %collective-permute-start.19) | collective-permute-done | bytes 524320 | tf_op jit(solution)/shard_map/ppermute | solution.py:130
  253.3 2.3 collective-permute-done.23
  255.6 2.5 fusion.25
  (161 shorter events, 57.5 us)
Async XLA Ops:
  0.0 28.5 %copy-start.29 = (bf16[128]{0:T(256)(128)(2,1)S(1)}, bf16[128]{0:T(256)(128)(2,1)}, u32[]{:S(2)}) copy-start(bf16[128]{0:T(256)(128)(2,1)} %param.10) | copy-start | bytes 772
  0.0 57.8 %collective-permute-start.1 = (bf16[128,4096]{1,0:T(8,128)(2,1)}, bf16[128,4096]{1,0:T(8,128)(2,1)}, u32[]{:S(2)}, u32[]{:S(2)}) collective-permute-start(bf16[128,4096]{1,0:T(8,128)(2,1)} %param.9), channel_id=1, source_target_pairs={{0,4},{4,8},{8,12},{12,14},{14,10},{10,6},{6,2},{2,0},{1,5},{5,9},... | collective-permute-start | bytes 3145736 | tf_op jit(solution)/shard_map/ppermute | solution.py:130
  5.2 52.7 %collective-permute-start = (bf16[128,4096]{1,0:T(8,128)(2,1)S(1)}, bf16[128,4096]{1,0:T(8,128)(2,1)S(1)}, u32[]{:S(2)}, u32[]{:S(2)}) collective-permute-start(bf16[128,4096]{1,0:T(8,128)(2,1)S(1)} %bitcast.69), channel_id=1, source_target_pairs={{0,1},{1,0},{2,3},{3,2},{4,5},{5,4},{6,7},{7,6},{8,9},{9,8},{10,11... | collective-permute-start | bytes 3145736 | tf_op jit(solution)/shard_map/ppermute | solution.py:136
  5.3 56.1 %collective-permute-start.2 = (bf16[128,4096]{1,0:T(8,128)(2,1)S(1)}, bf16[128,4096]{1,0:T(8,128)(2,1)}, u32[]{:S(2)}, u32[]{:S(2)}) collective-permute-start(bf16[128,4096]{1,0:T(8,128)(2,1)S(1)} %copy-done.9), channel_id=1, source_target_pairs={{4,0},{8,4},{12,8},{14,12},{10,14},{6,10},{2,6},{0,2},{5,1},{9,5},... | collective-permute-start | bytes 3145736 | tf_op jit(solution)/shard_map/ppermute | solution.py:133
  50.4 17.1 %copy-start.23 = (pred[256]{0:T(512)(128)(4,1)}, pred[256]{0:T(512)(128)(4,1)S(1)}, u32[]{:S(2)}) copy-start(pred[256]{0:T(512)(128)(4,1)S(1)} %broadcast_in_dim.140) | copy-start | bytes 772
  57.9 29.9 %collective-permute-start.3 = (bf16[128,4096]{1,0:T(8,128)(2,1)}, bf16[128,4096]{1,0:T(8,128)(2,1)S(1)}, u32[]{:S(2)}, u32[]{:S(2)}) collective-permute-start(bf16[128,4096]{1,0:T(8,128)(2,1)} %collective-permute-done.1), channel_id=1, source_target_pairs={{0,4},{4,8},{8,12},{12,14},{14,10},{10,6},{6,2},{2,0},{1,5},{5,9},... | collective-permute-start | bytes 3145736 | tf_op jit(solution)/shard_map/ppermute | solution.py:130
  57.9 62.8 %copy-start = (bf16[128,4096]{1,0:T(8,128)(2,1)}, bf16[128,4096]{1,0:T(8,128)(2,1)S(1)}, u32[]{:S(2)}) copy-start(bf16[128,4096]{1,0:T(8,128)(2,1)S(1)} %collective-permute-done) | copy-start | bytes 3145732
  61.5 23.6 %collective-permute-start.4 = (bf16[128,4096]{1,0:T(8,128)(2,1)}, bf16[128,4096]{1,0:T(8,128)(2,1)S(1)}, u32[]{:S(2)}, u32[]{:S(2)}) collective-permute-start(bf16[128,4096]{1,0:T(8,128)(2,1)} %collective-permute-done.2), channel_id=1, source_target_pairs={{4,0},{8,4},{12,8},{14,12},{10,14},{6,10},{2,6},{0,2},{5,1},{9,5},... | collective-permute-start | bytes 3145736 | tf_op jit(solution)/shard_map/ppermute | solution.py:133
  85.1 26.2 %collective-permute-start.6 = (bf16[128,4096]{1,0:T(8,128)(2,1)S(1)}, bf16[128,4096]{1,0:T(8,128)(2,1)S(1)}, u32[]{:S(2)}, u32[]{:S(2)}) collective-permute-start(bf16[128,4096]{1,0:T(8,128)(2,1)S(1)} %collective-permute-done.4), channel_id=1, source_target_pairs={{4,0},{8,4},{12,8},{14,12},{10,14},{6,10},{2,6},{0,2},{5,1},{9,5},... | collective-permute-start | bytes 3145736 | tf_op jit(solution)/shard_map/ppermute | solution.py:133
  87.8 45.1 %copy-start.15 = (f32[256,128]{1,0:T(8,128)}, f32[256,128]{1,0:T(8,128)S(1)}, u32[]{:S(2)}) copy-start(f32[256,128]{1,0:T(8,128)S(1)} %convolution_add_fusion.15) | copy-start | bytes 393220
  87.8 23.3 %collective-permute-start.5 = (bf16[128,4096]{1,0:T(8,128)(2,1)S(1)}, bf16[128,4096]{1,0:T(8,128)(2,1)S(1)}, u32[]{:S(2)}, u32[]{:S(2)}) collective-permute-start(bf16[128,4096]{1,0:T(8,128)(2,1)S(1)} %collective-permute-done.3), channel_id=1, source_target_pairs={{0,4},{4,8},{8,12},{12,14},{14,10},{10,6},{6,2},{2,0},{1,5},{5,9},... | collective-permute-start | bytes 3145736 | tf_op jit(solution)/shard_map/ppermute | solution.py:130
  111.2 9.2 %collective-permute-start.7 = (bf16[64,4096]{1,0:T(8,128)(2,1)S(1)}, bf16[64,4096]{1,0:T(8,128)(2,1)S(1)}, u32[]{:S(2)}, u32[]{:S(2)}) collective-permute-start(bf16[64,4096]{1,0:T(8,128)(2,1)S(1)} %slice.84), channel_id=1, source_target_pairs={{0,4},{4,8},{8,12},{12,14},{14,10},{10,6},{6,2},{2,0},{1,5},{5,9},... | collective-permute-start | bytes 1572872 | tf_op jit(solution)/shard_map/ppermute | solution.py:130
  111.3 9.4 %collective-permute-start.8 = (bf16[64,4096]{1,0:T(8,128)(2,1)S(1)}, bf16[64,4096]{1,0:T(8,128)(2,1)S(1)}, u32[]{:S(2)}, u32[]{:S(2)}) collective-permute-start(bf16[64,4096]{1,0:T(8,128)(2,1)S(1)} %slice.85), channel_id=1, source_target_pairs={{4,0},{8,4},{12,8},{14,12},{10,14},{6,10},{2,6},{0,2},{5,1},{9,5},... | collective-permute-start | bytes 1572872 | tf_op jit(solution)/shard_map/ppermute | solution.py:133
  115.8 20.9 %copy-start.12 = (f32[256,128]{1,0:T(8,128)}, f32[256,128]{1,0:T(8,128)S(1)}, u32[]{:S(2)}) copy-start(f32[256,128]{1,0:T(8,128)S(1)} %convolution_add_fusion.14) | copy-start | bytes 393220
  123.4 4.2 %collective-permute-start.9 = (bf16[256,4096]{1,0:T(8,128)(2,1)S(1)}, bf16[256,4096]{1,0:T(8,128)(2,1)S(1)}, u32[]{:S(2)}, u32[]{:S(2)}) collective-permute-start(bf16[256,4096]{1,0:T(8,128)(2,1)S(1)} %fusion.3), channel_id=1, source_target_pairs={{0,1},{1,0},{2,3},{3,2},{4,5},{5,4},{6,7},{7,6},{8,9},{9,8},{10,11... | collective-permute-start | bytes 6291464 | tf_op jit(solution)/shard_map/ppermute | solution.py:136
  147.8 41.9 %collective-permute-start.10 = (bf16[64,4096]{1,0:T(8,128)(2,1)}, bf16[64,4096]{1,0:T(8,128)(2,1)}, u32[]{:S(2)}, u32[]{:S(2)}) collective-permute-start(bf16[64,4096]{1,0:T(8,128)(2,1)} %get-tuple-element.25), channel_id=1, source_target_pairs={{0,4},{4,8},{8,12},{12,14},{14,10},{10,6},{6,2},{2,0},{1,5},{5,9},... | collective-permute-start | bytes 1572872 | tf_op jit(solution)/shard_map/ppermute | solution.py:130
  155.2 39.7 %collective-permute-start.17 = (bf16[64,4096]{1,0:T(8,128)(2,1)}, bf16[64,4096]{1,0:T(8,128)(2,1)}, u32[]{:S(2)}, u32[]{:S(2)}) collective-permute-start(bf16[64,4096]{1,0:T(8,128)(2,1)} %slice.142), channel_id=1, source_target_pairs={{0,4},{4,8},{8,12},{12,14},{14,10},{10,6},{6,2},{2,0},{1,5},{5,9},... | collective-permute-start | bytes 1572872 | tf_op jit(solution)/shard_map/ppermute | solution.py:130
  155.2 36.2 %collective-permute-start.20 = (bf16[64,4096]{1,0:T(8,128)(2,1)}, bf16[64,4096]{1,0:T(8,128)(2,1)}, u32[]{:S(2)}, u32[]{:S(2)}) collective-permute-start(bf16[64,4096]{1,0:T(8,128)(2,1)} %get-tuple-element.26), channel_id=1, source_target_pairs={{4,0},{8,4},{12,8},{14,12},{10,14},{6,10},{2,6},{0,2},{5,1},{9,5},... | collective-permute-start | bytes 1572872 | tf_op jit(solution)/shard_map/ppermute | solution.py:133
  164.7 41.7 %collective-permute-start.14 = (bf16[64,4096]{1,0:T(8,128)(2,1)}, bf16[64,4096]{1,0:T(8,128)(2,1)}, u32[]{:S(2)}, u32[]{:S(2)}) collective-permute-start(bf16[64,4096]{1,0:T(8,128)(2,1)} %slice.143), channel_id=1, source_target_pairs={{4,0},{8,4},{12,8},{14,12},{10,14},{6,10},{2,6},{0,2},{5,1},{9,5},... | collective-permute-start | bytes 1572872 | tf_op jit(solution)/shard_map/ppermute | solution.py:133
  189.7 14.8 %copy-start.5 = (f32[128,4096]{1,0:T(8,128)S(1)}, f32[128,4096]{1,0:T(8,128)}, u32[]{:S(2)}) copy-start(f32[128,4096]{1,0:T(8,128)} %convolution_add_fusion.9) | copy-start | bytes 6291460
  191.3 13.2 %collective-permute-start.11 = (bf16[64,4096]{1,0:T(8,128)(2,1)S(1)}, bf16[64,4096]{1,0:T(8,128)(2,1)S(1)}, u32[]{:S(2)}, u32[]{:S(2)}) collective-permute-start(bf16[64,4096]{1,0:T(8,128)(2,1)S(1)} %fusion.22), channel_id=1, source_target_pairs={{0,4},{4,8},{8,12},{12,14},{14,10},{10,6},{6,2},{2,0},{1,5},{5,9},... | collective-permute-start | bytes 1572872 | tf_op jit(solution)/shard_map/ppermute | solution.py:130
  192.9 13.5 %collective-permute-start.21 = (bf16[64,4096]{1,0:T(8,128)(2,1)S(1)}, bf16[64,4096]{1,0:T(8,128)(2,1)S(1)}, u32[]{:S(2)}, u32[]{:S(2)}) collective-permute-start(bf16[64,4096]{1,0:T(8,128)(2,1)S(1)} %fusion.14), channel_id=1, source_target_pairs={{4,0},{8,4},{12,8},{14,12},{10,14},{6,10},{2,6},{0,2},{5,1},{9,5},... | collective-permute-start | bytes 1572872 | tf_op jit(solution)/shard_map/ppermute | solution.py:133
  205.8 14.9 %collective-permute-start.12 = (bf16[64,4096]{1,0:T(8,128)(2,1)S(1)}, bf16[64,4096]{1,0:T(8,128)(2,1)S(1)}, u32[]{:S(2)}, u32[]{:S(2)}) collective-permute-start(bf16[64,4096]{1,0:T(8,128)(2,1)S(1)} %get-tuple-element.17), channel_id=1, source_target_pairs={{0,4},{4,8},{8,12},{12,14},{14,10},{10,6},{6,2},{2,0},{1,5},{5,9},... | collective-permute-start | bytes 1572872 | tf_op jit(solution)/shard_map/ppermute | solution.py:130
  206.1 23.1 %copy-start.3 = (f32[128,4096]{1,0:T(8,128)S(1)}, f32[128,4096]{1,0:T(8,128)}, u32[]{:S(2)}) copy-start(f32[128,4096]{1,0:T(8,128)} %convolution_add_fusion.10) | copy-start | bytes 6291460
  206.1 23.1 %collective-permute-start.18 = (bf16[64,4096]{1,0:T(8,128)(2,1)S(1)}, bf16[64,4096]{1,0:T(8,128)(2,1)S(1)}, u32[]{:S(2)}, u32[]{:S(2)}) collective-permute-start(bf16[64,4096]{1,0:T(8,128)(2,1)S(1)} %get-tuple-element.18), channel_id=1, source_target_pairs={{0,4},{4,8},{8,12},{12,14},{14,10},{10,6},{6,2},{2,0},{1,5},{5,9},... | collective-permute-start | bytes 1572872 | tf_op jit(solution)/shard_map/ppermute | solution.py:130
  207.8 23.7 %collective-permute-start.15 = (bf16[64,4096]{1,0:T(8,128)(2,1)S(1)}, bf16[64,4096]{1,0:T(8,128)(2,1)S(1)}, u32[]{:S(2)}, u32[]{:S(2)}) collective-permute-start(bf16[64,4096]{1,0:T(8,128)(2,1)S(1)} %get-tuple-element.21), channel_id=1, source_target_pairs={{4,0},{8,4},{12,8},{14,12},{10,14},{6,10},{2,6},{0,2},{5,1},{9,5},... | collective-permute-start | bytes 1572872 | tf_op jit(solution)/shard_map/ppermute | solution.py:133
  209.6 22.0 %copy-start.2 = (f32[128,4096]{1,0:T(8,128)S(1)}, f32[128,4096]{1,0:T(8,128)}, u32[]{:S(2)}) copy-start(f32[128,4096]{1,0:T(8,128)} %convolution_add_fusion.6) | copy-start | bytes 6291460
  209.6 22.0 %collective-permute-start.22 = (bf16[64,4096]{1,0:T(8,128)(2,1)S(1)}, bf16[64,4096]{1,0:T(8,128)(2,1)S(1)}, u32[]{:S(2)}, u32[]{:S(2)}) collective-permute-start(bf16[64,4096]{1,0:T(8,128)(2,1)S(1)} %get-tuple-element.22), channel_id=1, source_target_pairs={{4,0},{8,4},{12,8},{14,12},{10,14},{6,10},{2,6},{0,2},{5,1},{9,5},... | collective-permute-start | bytes 1572872 | tf_op jit(solution)/shard_map/ppermute | solution.py:133
  230.4 15.2 %collective-permute-start.13 = (bf16[64,4096]{1,0:T(8,128)(2,1)}, bf16[64,4096]{1,0:T(8,128)(2,1)}, u32[]{:S(2)}, u32[]{:S(2)}) collective-permute-start(bf16[64,4096]{1,0:T(8,128)(2,1)} %get-tuple-element.15), channel_id=1, source_target_pairs={{0,4},{4,8},{8,12},{12,14},{14,10},{10,6},{6,2},{2,0},{1,5},{5,9},... | collective-permute-start | bytes 1572872 | tf_op jit(solution)/shard_map/ppermute | solution.py:130
  231.0 22.3 %collective-permute-start.19 = (bf16[64,4096]{1,0:T(8,128)(2,1)}, bf16[64,4096]{1,0:T(8,128)(2,1)}, u32[]{:S(2)}, u32[]{:S(2)}) collective-permute-start(bf16[64,4096]{1,0:T(8,128)(2,1)} %get-tuple-element.16), channel_id=1, source_target_pairs={{0,4},{4,8},{8,12},{12,14},{14,10},{10,6},{6,2},{2,0},{1,5},{5,9},... | collective-permute-start | bytes 1572872 | tf_op jit(solution)/shard_map/ppermute | solution.py:130
  232.8 20.5 %collective-permute-start.16 = (bf16[64,4096]{1,0:T(8,128)(2,1)}, bf16[64,4096]{1,0:T(8,128)(2,1)}, u32[]{:S(2)}, u32[]{:S(2)}) collective-permute-start(bf16[64,4096]{1,0:T(8,128)(2,1)} %get-tuple-element.19), channel_id=1, source_target_pairs={{4,0},{8,4},{12,8},{14,12},{10,14},{6,10},{2,6},{0,2},{5,1},{9,5},... | collective-permute-start | bytes 1572872 | tf_op jit(solution)/shard_map/ppermute | solution.py:133
  234.2 21.4 %collective-permute-start.23 = (bf16[64,4096]{1,0:T(8,128)(2,1)}, bf16[64,4096]{1,0:T(8,128)(2,1)}, u32[]{:S(2)}, u32[]{:S(2)}) collective-permute-start(bf16[64,4096]{1,0:T(8,128)(2,1)} %get-tuple-element.20), channel_id=1, source_target_pairs={{4,0},{8,4},{12,8},{14,12},{10,14},{6,10},{2,6},{0,2},{5,1},{9,5},... | collective-permute-start | bytes 1572872 | tf_op jit(solution)/shard_map/ppermute | solution.py:133
  (23 other events, 149.4 us)

commit v2 on v1

--- a/solution.py
+++ b/solution.py
@@ -3,9 +3,12 @@
 import jax
 import jax.numpy as jnp
 from jax import lax
+from jax.experimental import pallas as pl
+from jax.experimental.pallas import tpu as pltpu
 from jax.sharding import PartitionSpec as P
 
 GATHER_LIMIT = 32 * 2**20
+LANES = 128
 
 
 def slot_tables(lists, block_count, slot_count):
@@ -109,6 +112,23 @@
     return grads.astype(jnp.bfloat16)
 
 
+def after(values, token):
+    anywhere = pl.BlockSpec(memory_space=pl.ANY)
+
+    def nothing(*refs):
+        del refs
+
+    return pl.pallas_call(
+        nothing,
+        out_shape=[jax.ShapeDtypeStruct(v.shape, v.dtype) for v in values],
+        in_specs=[anywhere] * (len(values) + 1),
+        out_specs=[anywhere] * len(values),
+        input_output_aliases={i: i for i in range(len(values))},
+        compiler_params=pltpu.CompilerParams(vmem_limit_bytes=2**20),
+        cost_estimate=pl.CostEstimate(flops=0, bytes_accessed=0, transcendentals=0),
+    )(*values, token)
+
+
 def ring_body(activations, act_blocks, dictionary, enc_bias, dec_bias):
     count = lax.axis_size("lat")
     lat_index = lax.axis_index("lat")
@@ -120,11 +140,9 @@
     half = count // 2
 
     order = list(range(0, count, 2)) + list(range(count - 1, 0, -2))
-    place_of = [order.index(i) for i in range(count)]
-    order_table = jnp.array(order, jnp.int32)
-    place = jnp.array(place_of, jnp.int32)[lat_index]
     right_pairs = [(order[i], order[(i + 1) % count]) for i in range(count)]
     left_pairs = [(b, a) for a, b in right_pairs]
+    place = jnp.where(lat_index % 2 == 0, lat_index // 2, count - 1 - lat_index // 2)
 
     def to_right(x):
         return lax.ppermute(x, "lat", right_pairs)
@@ -136,34 +154,43 @@
         return lax.ppermute(x, "row", [(0, 1), (1, 0)])
 
     def owner(step):
-        return order_table[(place + step) % count]
-
-    words = {0: dictionary}
+        at = (place + step + count) % count
+        return jnp.where(at < half, 2 * at, 2 * (count - 1 - at) + 1)
+
+    first = jnp.arange(LANES) == 0
+    tail = jnp.where(first, enc_bias[:, None], jnp.zeros((), enc_bias.dtype))
+    own_words = jnp.concatenate([dictionary, tail], axis=1)
+    words = {0: own_words}
+    from_left = from_right = (own_words[:cut], own_words[cut:])
     for step in range(1, half):
-        words[-step] = to_right(words[1 - step])
-        words[step] = to_left(words[step - 1])
-    words[half] = jnp.concatenate([to_right(words[1 - half][:cut]), to_left(words[half - 1][cut:])])
+        from_left = tuple(to_right(x) for x in from_left)
+        from_right = tuple(to_left(x) for x in from_right[::-1])[::-1]
+        words[-step], words[step] = jnp.concatenate(from_left), jnp.concatenate(from_right)
+    words[half] = jnp.concatenate([to_right(from_left[0]), to_left(from_right[1])])
 
     centred = (activations.astype(jnp.float32) - dec_bias.astype(jnp.float32)).astype(jnp.bfloat16)
     centred = centred.reshape(half_blocks * rows_each, width)
     rows = jnp.concatenate([centred, to_core(centred)])
-    biases = lax.all_gather(enc_bias, "lat", axis=0).astype(jnp.float32)
+    ones = jnp.broadcast_to(first.astype(rows.dtype), (rows.shape[0], LANES))
+    rows_one = jnp.concatenate([rows, ones], axis=1)
     lists = act_blocks.reshape(2, half_blocks, act_blocks.shape[1])
     lists = jnp.where(row_index == 0, lists, lists[::-1]).reshape(2 * half_blocks, -1)
 
     steps = [0] + [s for t in range(1, half) for s in (-t, t)] + [half]
+    owners = jnp.stack([owner(s) for s in steps])
+    listed = jnp.any(lists[:, :, None] == owners, axis=1).astype(jnp.float32)
+    listed = lax.optimization_barrier(jnp.repeat(listed, rows_each, axis=0))
+
     codes, sigmas = {}, {}
     rebuilt = None
-    for step in steps:
-        block = owner(step)
-        bias = lax.dynamic_index_in_dim(biases, block, 0, keepdims=False)
-        listed = jnp.repeat(jnp.any(lists == block, axis=1), rows_each)[:, None]
-        preacts = jnp.einsum("rd,ld->rl", rows, words[step], preferred_element_type=jnp.float32)
-        preacts = preacts + bias
-        codes[step] = jnp.where(listed, jax.nn.softplus(preacts), 0.0).astype(jnp.bfloat16)
-        sigmas[step] = jnp.where(listed, jax.nn.sigmoid(preacts), 0.0)
+    for i, step in enumerate(steps):
+        mask = listed[:, i : i + 1] > 0
+        preacts = jnp.einsum("rd,ld->rl", rows_one, words[step], preferred_element_type=jnp.float32)
+        code = jnp.where(mask, jax.nn.softplus(preacts), 0.0).astype(jnp.bfloat16)
+        sigma = jnp.where(mask, jax.nn.sigmoid(preacts), 0.0)
+        codes[step], sigmas[step] = lax.optimization_barrier((code, sigma))
         pieces = jnp.einsum(
-            "rl,ld->rd", codes[step], words[step], preferred_element_type=jnp.float32
+            "rl,ld->rd", codes[step], words[step][:, :width], preferred_element_type=jnp.float32
         )
         rebuilt = pieces if rebuilt is None else rebuilt + pieces
     rebuilt = rebuilt.astype(jnp.bfloat16)
@@ -173,20 +200,27 @@
     errors = rebuilt.astype(jnp.float32) + swapped.astype(jnp.float32) - rows.astype(jnp.float32)
     errors = errors.astype(jnp.bfloat16)
 
-    def grads_of(step):
-        slopes = jnp.einsum("rd,ld->rl", errors, words[step], preferred_element_type=jnp.float32)
-        slopes = (slopes * sigmas[step]).astype(jnp.bfloat16)
-        total = jnp.einsum("rl,rd->ld", codes[step], errors, preferred_element_type=jnp.float32)
+    def grads_of(step, token):
+        code, sigma = codes[step], sigmas[step]
+        if token is not None:
+            code, sigma = after((code, sigma), token)
+        slopes = jnp.einsum(
+            "rd,ld->rl", errors, words[step][:, :width], preferred_element_type=jnp.float32
+        )
+        slopes = lax.optimization_barrier((slopes * sigma).astype(jnp.bfloat16))
+        total = jnp.einsum("rl,rd->ld", code, errors, preferred_element_type=jnp.float32)
         return total + jnp.einsum("rl,rd->ld", slopes, rows, preferred_element_type=jnp.float32)
 
     def send(x):
         return x.astype(jnp.bfloat16)
 
-    far = grads_of(half)
-    up = (to_right(send(far[:cut])), None)
-    down = (None, to_left(send(far[cut:])))
+    far = send(grads_of(half, None))
+    up = (to_right(far[:cut]), None)
+    down = (None, to_left(far[cut:]))
+    tokens = (far, far)
     for step in range(half - 1, 0, -1):
-        ahead, behind = grads_of(step), grads_of(-step)
+        ahead, behind = grads_of(step, tokens[0]), grads_of(-step, tokens[1])
+        tokens = (up[0], down[1])
         parts = []
         for total, came in ((ahead, up), (behind, down)):
             pieces = (total[:cut], total[cut:])
@@ -195,7 +229,7 @@
             )
         up = tuple(to_right(p) for p in parts[0])
         down = tuple(to_left(p) for p in parts[1])
-    own = grads_of(0)
+    own = grads_of(0, tokens[0])
     halves = []
     for i, part in enumerate((own[:cut], own[cut:])):
         for came in (up[i], down[i]):

time: 260 us -> 196 us (0.75)
  matrix products: 74.6 us -> 26 us
  waiting for transfers between devices: 85.4 us -> 126 us
  between operations: 22.2 us -> 0.77 us
  blocking collectives: 21.1 us -> 0 us
  other arithmetic: 20 us -> 7.2 us
  starting transfers between devices: 24.2 us -> 32.2 us
  local copies, waits for them, and re-layouts: 11.7 us -> 3.95 us
    ppermute x11 -> x14, waiting for transfers between devices: 63.1 us -> 113 us  [to_right(): return lax.ppermute(x, 'lat', right_pairs)]
    dot_general x8, matrix products: 41.9 us -> 3.95 us  [grads_of(): jnp.einsum('rl,rd->ld', slopes, rows, preferred_element_type=jnp.float32)]
    all_gather x1 -> x0, blocking collectives: 21.1 us -> none  [ring_body(): biases = lax.all_gather(enc_bias, 'lat', axis=0).astype(jnp.float32)]
    ppermute x11 -> x14, starting transfers between devices: 5.17 us -> 20.3 us  [to_right(): return lax.ppermute(x, 'lat', right_pairs)]
    dot_general x24 -> x32, matrix products: 32.7 us -> 22 us  [the longest x8 6.66 us: ring_body(): jnp.einsum('rd,ld->rl', rows_one, words[step], preferred_element_type=jnp...]
    ppermute x11 -> x14, waiting for transfers between devices: 18.2 us -> 8.84 us  [to_left(): return lax.ppermute(x, 'lat', left_pairs)]
    ppermute x11 -> x14, starting transfers between devices: 18.9 us -> 11.7 us  [to_left(): return lax.ppermute(x, 'lat', left_pairs)]
    convert_element_type x6, other arithmetic: 8.16 us -> 1.18 us  [send(): return x.astype(jnp.bfloat16)]
  transfers between devices with their start and end apart: 24 -> 30, of which waited for: 11 -> 18; matrix products, arithmetic and copies ran while one was open for 31% -> 12% of each run, Pallas kernels for 0% -> 0%
where the time goes in v2:
time: 196 us
  waiting for transfers between devices  126 us (64%)
  starting transfers between devices  32.2 us (16%)
  matrix products  26 us (13%)
  other arithmetic  7.2 us (4%)
  local copies, waits for them, and re-layouts  3.95 us (2%)
    ppermute x14, waiting for transfers between devices, to_right(): return lax.ppermute(x, 'lat', right_pairs)  113 us
    ppermute x14, starting transfers between devices, to_right(): return lax.ppermute(x, 'lat', right_pairs)  20.3 us
    ppermute x14, starting transfers between devices, to_left(): return lax.ppermute(x, 'lat', left_pairs)  11.7 us
    ppermute x14, waiting for transfers between devices, to_left(): return lax.ppermute(x, 'lat', left_pairs)  8.84 us
    dot_general x8, matrix products, ring_body(): jnp.einsum('rd,ld->rl', rows_one, words[step], preferred_element_type=jnp...  6.66 us
    dot_general x8, matrix products, grads_of(): jnp.einsum('rd,ld->rl', errors, words[step][:, :width], preferred_element...  5.77 us
    dot_general x8, matrix products, ring_body(): jnp.einsum('rl,ld->rd', codes[step], words[step][:, :width], preferred_el...  5.54 us
    ppermute x2, waiting for transfers between devices, to_core(): return lax.ppermute(x, 'row', [(0, 1), (1, 0)])  4.15 us
  transfers between devices with their start and end apart: 30, of which 18 were waited for; matrix products, arithmetic and copies ran while one was open for 12% of the time, Pallas kernels for 0%

profile of v2, /device:TPU:0, one launch (start us, length us, event | category | flops | bytes accessed | tf_op | source)
XLA Modules:
  0.0 195.6 jit_solution(11485693039959989094)
XLA Ops:
  0.9 2.3 %fusion.43 = (bf16[64,4224]{1,0:T(8,128)(2,1)}, bf16[64,4224]{1,0:T(8,128)(2,1)}) fusion(bf16[128,4096]{1,0:T(8,128)(2,1)} %param.7, bf16[128,128]{1,0:T(8,128)(2,1)S(1)} %broadcast_select_fusion), kind=kLoop, calls=%fused_computation.87 | loop fusion | flops 2162688 | bytes 2162688 | tf_op jit(solution)/shard_map/concatenate | solution.py:162
  3.1 3.0 %collective-permute-start.5 = (bf16[64,4224]{1,0:T(8,128)(2,1)}, bf16[64,4224]{1,0:T(8,128)(2,1)}, u32[]{:S(2)}, u32[]{:S(2)}) collective-permute-start(bf16[64,4224]{1,0:T(8,128)(2,1)} %get-tuple-element.86), channel_id=1, source_target_pairs={{0,4},{4,8},{8,12},{12,14},{14,10},{10,6},{6,2},{2,0},{1,5},{5,9},... | collective-permute-start | bytes 1622024 | tf_op jit(solution)/shard_map/ppermute | solution.py:148
  6.2 2.0 %collective-permute-start.11 = (bf16[64,4224]{1,0:T(8,128)(2,1)}, bf16[64,4224]{1,0:T(8,128)(2,1)}, u32[]{:S(2)}, u32[]{:S(2)}) collective-permute-start(bf16[64,4224]{1,0:T(8,128)(2,1)} %get-tuple-element.85), channel_id=1, source_target_pairs={{0,4},{4,8},{8,12},{12,14},{14,10},{10,6},{6,2},{2,0},{1,5},{5,9},... | collective-permute-start | bytes 1622024 | tf_op jit(solution)/shard_map/ppermute | solution.py:148
  9.3 10.2 %collective-permute-done.5 = bf16[64,4224]{1,0:T(8,128)(2,1)} collective-permute-done((bf16[64,4224]{1,0:T(8,128)(2,1)}, bf16[64,4224]{1,0:T(8,128)(2,1)}, u32[]{:S(2)}, u32[]{:S(2)}) %collective-permute-start.5) | collective-permute-done | bytes 540704 | tf_op jit(solution)/shard_map/ppermute | solution.py:148
  19.5 2.1 %collective-permute-start.6 = (bf16[64,4224]{1,0:T(8,128)(2,1)}, bf16[64,4224]{1,0:T(8,128)(2,1)S(1)}, u32[]{:S(2)}, u32[]{:S(2)}) collective-permute-start(bf16[64,4224]{1,0:T(8,128)(2,1)} %collective-permute-done.5), channel_id=1, source_target_pairs={{0,4},{4,8},{8,12},{12,14},{14,10},{10,6},{6,2},{2,0},{1,5},{5,9},... | collective-permute-start | bytes 1622024 | tf_op jit(solution)/shard_map/ppermute | solution.py:148
  21.6 9.4 %collective-permute-done.11 = bf16[64,4224]{1,0:T(8,128)(2,1)} collective-permute-done((bf16[64,4224]{1,0:T(8,128)(2,1)}, bf16[64,4224]{1,0:T(8,128)(2,1)}, u32[]{:S(2)}, u32[]{:S(2)}) %collective-permute-start.11) | collective-permute-done | bytes 540704 | tf_op jit(solution)/shard_map/ppermute | solution.py:148
  31.1 2.1 %collective-permute-start.12 = (bf16[64,4224]{1,0:T(8,128)(2,1)}, bf16[64,4224]{1,0:T(8,128)(2,1)S(1)}, u32[]{:S(2)}, u32[]{:S(2)}) collective-permute-start(bf16[64,4224]{1,0:T(8,128)(2,1)} %collective-permute-done.11), channel_id=1, source_target_pairs={{0,4},{4,8},{8,12},{12,14},{14,10},{10,6},{6,2},{2,0},{1,5},{5,9},... | collective-permute-start | bytes 1622024 | tf_op jit(solution)/shard_map/ppermute | solution.py:148
  34.5 2.0 %collective-permute-start.4 = (bf16[64,4224]{1,0:T(8,128)(2,1)S(1)}, bf16[64,4224]{1,0:T(8,128)(2,1)S(1)}, u32[]{:S(2)}, u32[]{:S(2)}) collective-permute-start(bf16[64,4224]{1,0:T(8,128)(2,1)S(1)} %collective-permute-done.3), channel_id=1, source_target_pairs={{4,0},{8,4},{12,8},{14,12},{10,14},{6,10},{2,6},{0,2},{5,1},{9,5},... | collective-permute-start | bytes 1622024 | tf_op jit(solution)/shard_map/ppermute | solution.py:151
  42.7 10.7 %collective-permute-done.12 = bf16[64,4224]{1,0:T(8,128)(2,1)S(1)} collective-permute-done((bf16[64,4224]{1,0:T(8,128)(2,1)}, bf16[64,4224]{1,0:T(8,128)(2,1)S(1)}, u32[]{:S(2)}, u32[]{:S(2)}) %collective-permute-start.12) | collective-permute-done | bytes 540704 | tf_op jit(solution)/shard_map/ppermute | solution.py:148
  54.3 3.4 %collective-permute-done.4 = bf16[64,4224]{1,0:T(8,128)(2,1)S(1)} collective-permute-done((bf16[64,4224]{1,0:T(8,128)(2,1)S(1)}, bf16[64,4224]{1,0:T(8,128)(2,1)S(1)}, u32[]{:S(2)}, u32[]{:S(2)}) %collective-permute-start.4) | collective-permute-done | bytes 540704 | tf_op jit(solution)/shard_map/ppermute | solution.py:151
  59.3 1.6 collective-permute-start.7
  60.9 1.6 collective-permute-start.13
  64.1 10.5 %collective-permute-done.7 = bf16[64,4224]{1,0:T(8,128)(2,1)S(1)} collective-permute-done((bf16[64,4224]{1,0:T(8,128)(2,1)S(1)}, bf16[64,4224]{1,0:T(8,128)(2,1)S(1)}, u32[]{:S(2)}, u32[]{:S(2)}) %collective-permute-start.7) | collective-permute-done | bytes 540704 | tf_op jit(solution)/shard_map/ppermute | solution.py:148
  74.6 7.1 %collective-permute-done.13 = bf16[64,4224]{1,0:T(8,128)(2,1)S(1)} collective-permute-done((bf16[64,4224]{1,0:T(8,128)(2,1)S(1)}, bf16[64,4224]{1,0:T(8,128)(2,1)S(1)}, u32[]{:S(2)}, u32[]{:S(2)}) %collective-permute-start.13) | collective-permute-done | bytes 540704 | tf_op jit(solution)/shard_map/ppermute | solution.py:148
  82.6 1.7 collective-permute-done.14
  85.9 1.5 collective-permute-start.8
  88.7 6.6 %collective-permute-done.8 = bf16[64,4224]{1,0:T(8,128)(2,1)S(1)} collective-permute-done((bf16[64,4224]{1,0:T(8,128)(2,1)S(1)}, bf16[64,4224]{1,0:T(8,128)(2,1)S(1)}, u32[]{:S(2)}, u32[]{:S(2)}) %collective-permute-start.8) | collective-permute-done | bytes 540704 | tf_op jit(solution)/shard_map/ppermute | solution.py:148
  95.4 1.5 collective-permute-done.10
  98.5 4.1 %collective-permute-done.15 = bf16[256,4096]{1,0:T(8,128)(2,1)S(1)} collective-permute-done((bf16[256,4096]{1,0:T(8,128)(2,1)S(1)}, bf16[256,4096]{1,0:T(8,128)(2,1)S(1)}, u32[]{:S(2)}, u32[]{:S(2)}) %collective-permute-start.15) | collective-permute-done | bytes 2097184 | tf_op jit(solution)/shard_map/ppermute | solution.py:154
  112.3 1.3 collective-permute-start.22
  113.6 8.2 %collective-permute-done.16.refs_2_ = bf16[64,4096]{1,0:T(8,128)(2,1)S(1)} collective-permute-done((bf16[64,4096]{1,0:T(8,128)(2,1)S(1)}, bf16[64,4096]{1,0:T(8,128)(2,1)S(1)}, u32[]{:S(2)}, u32[]{:S(2)}) %collective-permute-start.16) | collective-permute-done | bytes 524320 | tf_op jit(solution)/shard_map/ppermute | solution.py:148
  125.1 1.1 collective-permute-start.21
  128.2 15.2 %collective-permute-done.17.refs_2_ = bf16[64,4096]{1,0:T(8,128)(2,1)S(1)} collective-permute-done((bf16[64,4096]{1,0:T(8,128)(2,1)S(1)}, bf16[64,4096]{1,0:T(8,128)(2,1)S(1)}, u32[]{:S(2)}, u32[]{:S(2)}) %collective-permute-start.17) | collective-permute-done | bytes 524320 | tf_op jit(solution)/shard_map/ppermute | solution.py:148
  146.5 1.1 collective-permute-start.23
  147.6 1.3 collective-permute-start.28
  151.6 7.8 %collective-permute-done.18.refs_2_ = bf16[64,4096]{1,0:T(8,128)(2,1)S(1)} collective-permute-done((bf16[64,4096]{1,0:T(8,128)(2,1)S(1)}, bf16[64,4096]{1,0:T(8,128)(2,1)S(1)}, u32[]{:S(2)}, u32[]{:S(2)}) %collective-permute-start.18) | collective-permute-done | bytes 524320 | tf_op jit(solution)/shard_map/ppermute | solution.py:148
  159.4 9.5 %collective-permute-done.26 = bf16[64,4096]{1,0:T(8,128)(2,1)S(1)} collective-permute-done((bf16[64,4096]{1,0:T(8,128)(2,1)S(1)}, bf16[64,4096]{1,0:T(8,128)(2,1)S(1)}, u32[]{:S(2)}, u32[]{:S(2)}) %collective-permute-start.26) | collective-permute-done | bytes 524320 | tf_op jit(solution)/shard_map/ppermute | solution.py:148
  172.3 1.3 collective-permute-start.29
  175.3 8.7 %collective-permute-done.19 = bf16[64,4096]{1,0:T(8,128)(2,1)S(1)} collective-permute-done((bf16[64,4096]{1,0:T(8,128)(2,1)S(1)}, bf16[64,4096]{1,0:T(8,128)(2,1)S(1)}, u32[]{:S(2)}, u32[]{:S(2)}) %collective-permute-start.19) | collective-permute-done | bytes 524320 | tf_op jit(solution)/shard_map/ppermute | solution.py:148
  184.0 8.6 %collective-permute-done.27 = bf16[64,4096]{1,0:T(8,128)(2,1)S(1)} collective-permute-done((bf16[64,4096]{1,0:T(8,128)(2,1)S(1)}, bf16[64,4096]{1,0:T(8,128)(2,1)S(1)}, u32[]{:S(2)}, u32[]{:S(2)}) %collective-permute-start.27) | collective-permute-done | bytes 524320 | tf_op jit(solution)/shard_map/ppermute | solution.py:148
  192.6 1.5 collective-permute-done.29
  194.5 1.1 fusion.4
  (127 shorter events, 44.5 us)
Async XLA Ops:
  0.0 8.2 %copy-start.2 = (bf16[4096]{0:T(1024)(128)(2,1)S(1)}, bf16[4096]{0:T(1024)(128)(2,1)}, u32[]{:S(2)}) copy-start(bf16[4096]{0:T(1024)(128)(2,1)} %param.9) | copy-start | bytes 24580
  0.0 8.2 %copy-start.1 = (bf16[8,16,4096]{2,1,0:T(8,128)(2,1)S(1)}, bf16[8,16,4096]{2,1,0:T(8,128)(2,1)}, u32[]{:S(2)}) copy-start(bf16[8,16,4096]{2,1,0:T(8,128)(2,1)} %param.5) | copy-start | bytes 3145732
  3.1 16.4 %collective-permute-start.5 = (bf16[64,4224]{1,0:T(8,128)(2,1)}, bf16[64,4224]{1,0:T(8,128)(2,1)}, u32[]{:S(2)}, u32[]{:S(2)}) collective-permute-start(bf16[64,4224]{1,0:T(8,128)(2,1)} %get-tuple-element.86), channel_id=1, source_target_pairs={{0,4},{4,8},{8,12},{12,14},{14,10},{10,6},{6,2},{2,0},{1,5},{5,9},... | collective-permute-start | bytes 1622024 | tf_op jit(solution)/shard_map/ppermute | solution.py:148
  6.2 28.2 %collective-permute-start.1 = (bf16[64,4224]{1,0:T(8,128)(2,1)}, bf16[64,4224]{1,0:T(8,128)(2,1)S(1)}, u32[]{:S(2)}, u32[]{:S(2)}) collective-permute-start(bf16[64,4224]{1,0:T(8,128)(2,1)} %get-tuple-element.86), channel_id=1, source_target_pairs={{4,0},{8,4},{12,8},{14,12},{10,14},{6,10},{2,6},{0,2},{5,1},{9,5},... | collective-permute-start | bytes 1622024 | tf_op jit(solution)/shard_map/ppermute | solution.py:151
  6.2 24.9 %collective-permute-start.11 = (bf16[64,4224]{1,0:T(8,128)(2,1)}, bf16[64,4224]{1,0:T(8,128)(2,1)}, u32[]{:S(2)}, u32[]{:S(2)}) collective-permute-start(bf16[64,4224]{1,0:T(8,128)(2,1)} %get-tuple-element.85), channel_id=1, source_target_pairs={{0,4},{4,8},{8,12},{12,14},{14,10},{10,6},{6,2},{2,0},{1,5},{5,9},... | collective-permute-start | bytes 1622024 | tf_op jit(solution)/shard_map/ppermute | solution.py:148
  8.2 26.2 %collective-permute-start.3 = (bf16[64,4224]{1,0:T(8,128)(2,1)}, bf16[64,4224]{1,0:T(8,128)(2,1)S(1)}, u32[]{:S(2)}, u32[]{:S(2)}) collective-permute-start(bf16[64,4224]{1,0:T(8,128)(2,1)} %get-tuple-element.85), channel_id=1, source_target_pairs={{4,0},{8,4},{12,8},{14,12},{10,14},{6,10},{2,6},{0,2},{5,1},{9,5},... | collective-permute-start | bytes 1622024 | tf_op jit(solution)/shard_map/ppermute | solution.py:151
  8.4 29.2 %collective-permute-start = (bf16[128,4096]{1,0:T(8,128)(2,1)S(1)}, bf16[128,4096]{1,0:T(8,128)(2,1)S(1)}, u32[]{:S(2)}, u32[]{:S(2)}) collective-permute-start(bf16[128,4096]{1,0:T(8,128)(2,1)S(1)} %bitcast.67), channel_id=1, source_target_pairs={{0,1},{1,0},{2,3},{3,2},{4,5},{5,4},{6,7},{7,6},{8,9},{9,8},{10,11... | collective-permute-start | bytes 3145736 | tf_op jit(solution)/shard_map/ppermute | solution.py:154
  19.5 23.1 %collective-permute-start.6 = (bf16[64,4224]{1,0:T(8,128)(2,1)}, bf16[64,4224]{1,0:T(8,128)(2,1)S(1)}, u32[]{:S(2)}, u32[]{:S(2)}) collective-permute-start(bf16[64,4224]{1,0:T(8,128)(2,1)} %collective-permute-done.5), channel_id=1, source_target_pairs={{0,4},{4,8},{8,12},{12,14},{14,10},{10,6},{6,2},{2,0},{1,5},{5,9},... | collective-permute-start | bytes 1622024 | tf_op jit(solution)/shard_map/ppermute | solution.py:148
  31.1 22.2 %collective-permute-start.12 = (bf16[64,4224]{1,0:T(8,128)(2,1)}, bf16[64,4224]{1,0:T(8,128)(2,1)S(1)}, u32[]{:S(2)}, u32[]{:S(2)}) collective-permute-start(bf16[64,4224]{1,0:T(8,128)(2,1)} %collective-permute-done.11), channel_id=1, source_target_pairs={{0,4},{4,8},{8,12},{12,14},{14,10},{10,6},{6,2},{2,0},{1,5},{5,9},... | collective-permute-start | bytes 1622024 | tf_op jit(solution)/shard_map/ppermute | solution.py:148
  34.3 19.9 %collective-permute-start.2 = (bf16[64,4224]{1,0:T(8,128)(2,1)S(1)}, bf16[64,4224]{1,0:T(8,128)(2,1)S(1)}, u32[]{:S(2)}, u32[]{:S(2)}) collective-permute-start(bf16[64,4224]{1,0:T(8,128)(2,1)S(1)} %collective-permute-done.1), channel_id=1, source_target_pairs={{4,0},{8,4},{12,8},{14,12},{10,14},{6,10},{2,6},{0,2},{5,1},{9,5},... | collective-permute-start | bytes 1622024 | tf_op jit(solution)/shard_map/ppermute | solution.py:151
  34.5 23.2 %collective-permute-start.4 = (bf16[64,4224]{1,0:T(8,128)(2,1)S(1)}, bf16[64,4224]{1,0:T(8,128)(2,1)S(1)}, u32[]{:S(2)}, u32[]{:S(2)}) collective-permute-start(bf16[64,4224]{1,0:T(8,128)(2,1)S(1)} %collective-permute-done.3), channel_id=1, source_target_pairs={{4,0},{8,4},{12,8},{14,12},{10,14},{6,10},{2,6},{0,2},{5,1},{9,5},... | collective-permute-start | bytes 1622024 | tf_op jit(solution)/shard_map/ppermute | solution.py:151
  59.3 15.3 %collective-permute-start.7 = (bf16[64,4224]{1,0:T(8,128)(2,1)S(1)}, bf16[64,4224]{1,0:T(8,128)(2,1)S(1)}, u32[]{:S(2)}, u32[]{:S(2)}) collective-permute-start(bf16[64,4224]{1,0:T(8,128)(2,1)S(1)} %collective-permute-done.6), channel_id=1, source_target_pairs={{0,4},{4,8},{8,12},{12,14},{14,10},{10,6},{6,2},{2,0},{1,5},{5,9},... | collective-permute-start | bytes 1622024 | tf_op jit(solution)/shard_map/ppermute | solution.py:148
  60.9 20.8 %collective-permute-start.13 = (bf16[64,4224]{1,0:T(8,128)(2,1)S(1)}, bf16[64,4224]{1,0:T(8,128)(2,1)S(1)}, u32[]{:S(2)}, u32[]{:S(2)}) collective-permute-start(bf16[64,4224]{1,0:T(8,128)(2,1)S(1)} %collective-permute-done.12), channel_id=1, source_target_pairs={{0,4},{4,8},{8,12},{12,14},{14,10},{10,6},{6,2},{2,0},{1,5},{5,9},... | collective-permute-start | bytes 1622024 | tf_op jit(solution)/shard_map/ppermute | solution.py:148
  62.5 21.9 %collective-permute-start.9 = (bf16[64,4224]{1,0:T(8,128)(2,1)S(1)}, bf16[64,4224]{1,0:T(8,128)(2,1)S(1)}, u32[]{:S(2)}, u32[]{:S(2)}) collective-permute-start(bf16[64,4224]{1,0:T(8,128)(2,1)S(1)} %collective-permute-done.4), channel_id=1, source_target_pairs={{4,0},{8,4},{12,8},{14,12},{10,14},{6,10},{2,6},{0,2},{5,1},{9,5},... | collective-permute-start | bytes 1622024 | tf_op jit(solution)/shard_map/ppermute | solution.py:151
  62.9 21.4 %collective-permute-start.14 = (bf16[64,4224]{1,0:T(8,128)(2,1)S(1)}, bf16[64,4224]{1,0:T(8,128)(2,1)S(1)}, u32[]{:S(2)}, u32[]{:S(2)}) collective-permute-start(bf16[64,4224]{1,0:T(8,128)(2,1)S(1)} %collective-permute-done.2), channel_id=1, source_target_pairs={{4,0},{8,4},{12,8},{14,12},{10,14},{6,10},{2,6},{0,2},{5,1},{9,5},... | collective-permute-start | bytes 1622024 | tf_op jit(solution)/shard_map/ppermute | solution.py:151
  85.9 9.4 %collective-permute-start.8 = (bf16[64,4224]{1,0:T(8,128)(2,1)S(1)}, bf16[64,4224]{1,0:T(8,128)(2,1)S(1)}, u32[]{:S(2)}, u32[]{:S(2)}) collective-permute-start(bf16[64,4224]{1,0:T(8,128)(2,1)S(1)} %collective-permute-done.7), channel_id=1, source_target_pairs={{0,4},{4,8},{8,12},{12,14},{14,10},{10,6},{6,2},{2,0},{1,5},{5,9},... | collective-permute-start | bytes 1622024 | tf_op jit(solution)/shard_map/ppermute | solution.py:148
  87.5 9.4 %collective-permute-start.10 = (bf16[64,4224]{1,0:T(8,128)(2,1)S(1)}, bf16[64,4224]{1,0:T(8,128)(2,1)S(1)}, u32[]{:S(2)}, u32[]{:S(2)}) collective-permute-start(bf16[64,4224]{1,0:T(8,128)(2,1)S(1)} %collective-permute-done.9), channel_id=1, source_target_pairs={{4,0},{8,4},{12,8},{14,12},{10,14},{6,10},{2,6},{0,2},{5,1},{9,5},... | collective-permute-start | bytes 1622024 | tf_op jit(solution)/shard_map/ppermute | solution.py:151
  98.4 4.2 %collective-permute-start.15 = (bf16[256,4096]{1,0:T(8,128)(2,1)S(1)}, bf16[256,4096]{1,0:T(8,128)(2,1)S(1)}, u32[]{:S(2)}, u32[]{:S(2)}) collective-permute-start(bf16[256,4096]{1,0:T(8,128)(2,1)S(1)} %fusion.2), channel_id=1, source_target_pairs={{0,1},{1,0},{2,3},{3,2},{4,5},{5,4},{6,7},{7,6},{8,9},{9,8},{10,11... | collective-permute-start | bytes 6291464 | tf_op jit(solution)/shard_map/ppermute | solution.py:154
  107.0 14.8 %collective-permute-start.16 = (bf16[64,4096]{1,0:T(8,128)(2,1)S(1)}, bf16[64,4096]{1,0:T(8,128)(2,1)S(1)}, u32[]{:S(2)}, u32[]{:S(2)}) collective-permute-start(bf16[64,4096]{1,0:T(8,128)(2,1)S(1)} %get-tuple-element.88), channel_id=1, source_target_pairs={{0,4},{4,8},{8,12},{12,14},{14,10},{10,6},{6,2},{2,0},{1,5},{5,9},... | collective-permute-start | bytes 1572872 | tf_op jit(solution)/shard_map/ppermute | solution.py:148
  108.4 35.8 %collective-permute-start.25 = (bf16[64,4096]{1,0:T(8,128)(2,1)S(1)}, bf16[64,4096]{1,0:T(8,128)(2,1)S(1)}, u32[]{:S(2)}, u32[]{:S(2)}) collective-permute-start(bf16[64,4096]{1,0:T(8,128)(2,1)S(1)} %slice.272), channel_id=1, source_target_pairs={{0,4},{4,8},{8,12},{12,14},{14,10},{10,6},{6,2},{2,0},{1,5},{5,9},... | collective-permute-start | bytes 1572872 | tf_op jit(solution)/shard_map/ppermute | solution.py:148
  109.4 14.8 %collective-permute-start.20 = (bf16[64,4096]{1,0:T(8,128)(2,1)S(1)}, bf16[64,4096]{1,0:T(8,128)(2,1)S(1)}, u32[]{:S(2)}, u32[]{:S(2)}) collective-permute-start(bf16[64,4096]{1,0:T(8,128)(2,1)S(1)} %get-tuple-element.87), channel_id=1, source_target_pairs={{4,0},{8,4},{12,8},{14,12},{10,14},{6,10},{2,6},{0,2},{5,1},{9,5},... | collective-permute-start | bytes 1572872 | tf_op jit(solution)/shard_map/ppermute | solution.py:151
  112.3 33.9 %collective-permute-start.22 = (bf16[64,4096]{1,0:T(8,128)(2,1)S(1)}, bf16[64,4096]{1,0:T(8,128)(2,1)S(1)}, u32[]{:S(2)}, u32[]{:S(2)}) collective-permute-start(bf16[64,4096]{1,0:T(8,128)(2,1)S(1)} %slice.273), channel_id=1, source_target_pairs={{4,0},{8,4},{12,8},{14,12},{10,14},{6,10},{2,6},{0,2},{5,1},{9,5},... | collective-permute-start | bytes 1572872 | tf_op jit(solution)/shard_map/ppermute | solution.py:151
  121.9 21.5 %collective-permute-start.17 = (bf16[64,4096]{1,0:T(8,128)(2,1)S(1)}, bf16[64,4096]{1,0:T(8,128)(2,1)S(1)}, u32[]{:S(2)}, u32[]{:S(2)}) collective-permute-start(bf16[64,4096]{1,0:T(8,128)(2,1)S(1)} %fusion.23), channel_id=1, source_target_pairs={{0,4},{4,8},{8,12},{12,14},{14,10},{10,6},{6,2},{2,0},{1,5},{5,9},... | collective-permute-start | bytes 1572872 | tf_op jit(solution)/shard_map/ppermute | solution.py:148
  125.1 21.1 %collective-permute-start.21 = (bf16[64,4096]{1,0:T(8,128)(2,1)S(1)}, bf16[64,4096]{1,0:T(8,128)(2,1)S(1)}, u32[]{:S(2)}, u32[]{:S(2)}) collective-permute-start(bf16[64,4096]{1,0:T(8,128)(2,1)S(1)} %fusion.20), channel_id=1, source_target_pairs={{4,0},{8,4},{12,8},{14,12},{10,14},{6,10},{2,6},{0,2},{5,1},{9,5},... | collective-permute-start | bytes 1572872 | tf_op jit(solution)/shard_map/ppermute | solution.py:151
  144.4 14.9 %collective-permute-start.18 = (bf16[64,4096]{1,0:T(8,128)(2,1)S(1)}, bf16[64,4096]{1,0:T(8,128)(2,1)S(1)}, u32[]{:S(2)}, u32[]{:S(2)}) collective-permute-start(bf16[64,4096]{1,0:T(8,128)(2,1)S(1)} %get-tuple-element.82), channel_id=1, source_target_pairs={{0,4},{4,8},{8,12},{12,14},{14,10},{10,6},{6,2},{2,0},{1,5},{5,9},... | collective-permute-start | bytes 1572872 | tf_op jit(solution)/shard_map/ppermute | solution.py:148
  145.3 23.6 %collective-permute-start.26 = (bf16[64,4096]{1,0:T(8,128)(2,1)S(1)}, bf16[64,4096]{1,0:T(8,128)(2,1)S(1)}, u32[]{:S(2)}, u32[]{:S(2)}) collective-permute-start(bf16[64,4096]{1,0:T(8,128)(2,1)S(1)} %get-tuple-element.81), channel_id=1, source_target_pairs={{0,4},{4,8},{8,12},{12,14},{14,10},{10,6},{6,2},{2,0},{1,5},{5,9},... | collective-permute-start | bytes 1572872 | tf_op jit(solution)/shard_map/ppermute | solution.py:148
  146.5 24.4 %collective-permute-start.23 = (bf16[64,4096]{1,0:T(8,128)(2,1)S(1)}, bf16[64,4096]{1,0:T(8,128)(2,1)S(1)}, u32[]{:S(2)}, u32[]{:S(2)}) collective-permute-start(bf16[64,4096]{1,0:T(8,128)(2,1)S(1)} %get-tuple-element.79), channel_id=1, source_target_pairs={{4,0},{8,4},{12,8},{14,12},{10,14},{6,10},{2,6},{0,2},{5,1},{9,5},... | collective-permute-start | bytes 1572872 | tf_op jit(solution)/shard_map/ppermute | solution.py:151
  147.6 23.3 %collective-permute-start.28 = (bf16[64,4096]{1,0:T(8,128)(2,1)S(1)}, bf16[64,4096]{1,0:T(8,128)(2,1)S(1)}, u32[]{:S(2)}, u32[]{:S(2)}) collective-permute-start(bf16[64,4096]{1,0:T(8,128)(2,1)S(1)} %get-tuple-element.80), channel_id=1, source_target_pairs={{4,0},{8,4},{12,8},{14,12},{10,14},{6,10},{2,6},{0,2},{5,1},{9,5},... | collective-permute-start | bytes 1572872 | tf_op jit(solution)/shard_map/ppermute | solution.py:151
  169.1 14.9 %collective-permute-start.19 = (bf16[64,4096]{1,0:T(8,128)(2,1)S(1)}, bf16[64,4096]{1,0:T(8,128)(2,1)S(1)}, u32[]{:S(2)}, u32[]{:S(2)}) collective-permute-start(bf16[64,4096]{1,0:T(8,128)(2,1)S(1)} %get-tuple-element.75), channel_id=1, source_target_pairs={{0,4},{4,8},{8,12},{12,14},{14,10},{10,6},{6,2},{2,0},{1,5},{5,9},... | collective-permute-start | bytes 1572872 | tf_op jit(solution)/shard_map/ppermute | solution.py:148
  169.9 22.7 %collective-permute-start.27 = (bf16[64,4096]{1,0:T(8,128)(2,1)S(1)}, bf16[64,4096]{1,0:T(8,128)(2,1)S(1)}, u32[]{:S(2)}, u32[]{:S(2)}) collective-permute-start(bf16[64,4096]{1,0:T(8,128)(2,1)S(1)} %get-tuple-element.76), channel_id=1, source_target_pairs={{0,4},{4,8},{8,12},{12,14},{14,10},{10,6},{6,2},{2,0},{1,5},{5,9},... | collective-permute-start | bytes 1572872 | tf_op jit(solution)/shard_map/ppermute | solution.py:148
  171.1 21.5 %collective-permute-start.24 = (bf16[64,4096]{1,0:T(8,128)(2,1)S(1)}, bf16[64,4096]{1,0:T(8,128)(2,1)S(1)}, u32[]{:S(2)}, u32[]{:S(2)}) collective-permute-start(bf16[64,4096]{1,0:T(8,128)(2,1)S(1)} %get-tuple-element.77), channel_id=1, source_target_pairs={{4,0},{8,4},{12,8},{14,12},{10,14},{6,10},{2,6},{0,2},{5,1},{9,5},... | collective-permute-start | bytes 1572872 | tf_op jit(solution)/shard_map/ppermute | solution.py:151
  172.3 21.8 %collective-permute-start.29 = (bf16[64,4096]{1,0:T(8,128)(2,1)S(1)}, bf16[64,4096]{1,0:T(8,128)(2,1)S(1)}, u32[]{:S(2)}, u32[]{:S(2)}) collective-permute-start(bf16[64,4096]{1,0:T(8,128)(2,1)S(1)} %get-tuple-element.78), channel_id=1, source_target_pairs={{4,0},{8,4},{12,8},{14,12},{10,14},{6,10},{2,6},{0,2},{5,1},{9,5},... | collective-permute-start | bytes 1572872 | tf_op jit(solution)/shard_map/ppermute | solution.py:151
  (2 other events, 9.1 us)

commit v3 on v2

--- a/solution.py
+++ b/solution.py
@@ -8,7 +8,7 @@
 from jax.sharding import PartitionSpec as P
 
 GATHER_LIMIT = 32 * 2**20
-LANES = 128
+TILES = 4
 
 
 def slot_tables(lists, block_count, slot_count):
@@ -112,7 +112,7 @@
     return grads.astype(jnp.bfloat16)
 
 
-def after(values, token):
+def after(values, *tokens):
     anywhere = pl.BlockSpec(memory_space=pl.ANY)
 
     def nothing(*refs):
@@ -121,12 +121,144 @@
     return pl.pallas_call(
         nothing,
         out_shape=[jax.ShapeDtypeStruct(v.shape, v.dtype) for v in values],
-        in_specs=[anywhere] * (len(values) + 1),
+        in_specs=[anywhere] * (len(values) + len(tokens)),
         out_specs=[anywhere] * len(values),
         input_output_aliases={i: i for i in range(len(values))},
         compiler_params=pltpu.CompilerParams(vmem_limit_bytes=2**20),
         cost_estimate=pl.CostEstimate(flops=0, bytes_accessed=0, transcendentals=0),
-    )(*values, token)
+    )(*values, *tokens)
+
+
+def local_call(
+    kernel, grid, in_specs, out_specs, out_shape, args, aliases=None, scratch=(), cost=(0, 0)
+):
+    return pl.pallas_call(
+        kernel,
+        grid=grid,
+        in_specs=in_specs,
+        out_specs=out_specs,
+        out_shape=out_shape,
+        scratch_shapes=scratch,
+        input_output_aliases=aliases or {},
+        compiler_params=pltpu.CompilerParams(vmem_limit_bytes=24 * 2**20),
+        cost_estimate=pl.CostEstimate(flops=cost[0], bytes_accessed=cost[1], transcendentals=0),
+    )(*args)
+
+
+def whole(x):
+    return pl.BlockSpec(x.shape, lambda i: (0,) * x.ndim)
+
+
+def columns(x, tile):
+    return pl.BlockSpec((x.shape[0], tile), lambda i: (0, i))
+
+
+def centre(mine, theirs, dec_bias):
+    count, width = mine.shape
+
+    def kernel(x_ref, y_ref, b_ref, o_ref):
+        shift = b_ref[...].astype(jnp.float32)
+        o_ref[:count, :] = (x_ref[...].astype(jnp.float32) - shift).astype(o_ref.dtype)
+        o_ref[count:, :] = (y_ref[...].astype(jnp.float32) - shift).astype(o_ref.dtype)
+
+    tile = width // TILES
+    out = jax.ShapeDtypeStruct((2 * count, width), jnp.bfloat16)
+    args = (mine, theirs, dec_bias)
+    return local_call(kernel, (TILES,), [columns(x, tile) for x in args], columns(out, tile), out, args)
+
+
+def product(x, y, dims):
+    return lax.dot_general(x, y, (dims, ((), ())), preferred_element_type=jnp.float32)
+
+
+def encode(rows, words, bias, listed, which):
+    count, tile = words.shape[0], rows.shape[1] // TILES
+
+    def kernel(x_ref, w_ref, b_ref, m_ref, c_ref, s_ref, acc):
+        @pl.when(pl.program_id(0) == 0)
+        def _():
+            acc[...] = jnp.broadcast_to(b_ref[which : which + 1, :], acc.shape)
+
+        acc[...] += product(x_ref[...], w_ref[...], ((1,), (1,)))
+
+        @pl.when(pl.program_id(0) == TILES - 1)
+        def _():
+            p = acc[...]
+            mask = m_ref[:, which : which + 1] > 0
+            code = jnp.maximum(p, 0.0) + jnp.log1p(jnp.exp(-jnp.abs(p)))
+            c_ref[...] = jnp.where(mask, code, 0.0).astype(c_ref.dtype)
+            s_ref[...] = jnp.where(mask, jax.nn.sigmoid(p), 0.0)
+
+    shape = (rows.shape[0], count)
+    out = [jax.ShapeDtypeStruct(shape, jnp.bfloat16), jax.ShapeDtypeStruct(shape, jnp.float32)]
+    return local_call(
+        kernel,
+        (TILES,),
+        [columns(rows, tile), columns(words, tile), whole(bias), whole(listed)],
+        [whole(o) for o in out],
+        out,
+        (rows, words, bias, listed),
+        scratch=[pltpu.VMEM(shape, jnp.float32)],
+    )
+
+
+def decode(codes, words, total):
+    tile = words.shape[1] // TILES
+
+    def kernel(c_ref, w_ref, *rest):
+        part = product(c_ref[...], w_ref[...], ((1,), (0,)))
+        rest[-1][...] = part if len(rest) == 1 else part + rest[0][...]
+
+    out = jax.ShapeDtypeStruct((codes.shape[0], words.shape[1]), jnp.float32)
+    args = (codes, words) if total is None else (codes, words, total)
+    specs = [whole(codes), columns(words, tile)] + [columns(out, tile)] * (len(args) - 2)
+    aliases = {2: 0} if len(args) == 3 else None
+    return local_call(kernel, (TILES,), specs, columns(out, tile), out, args, aliases)
+
+
+def slope(errors, words, sigma):
+    tile = words.shape[1] // TILES
+
+    def kernel(e_ref, w_ref, s_ref, o_ref, acc):
+        @pl.when(pl.program_id(0) == 0)
+        def _():
+            acc[...] = jnp.zeros_like(acc)
+
+        acc[...] += product(e_ref[...], w_ref[...], ((1,), (1,)))
+
+        @pl.when(pl.program_id(0) == TILES - 1)
+        def _():
+            o_ref[...] = (acc[...] * s_ref[...]).astype(o_ref.dtype)
+
+    return local_call(
+        kernel,
+        (TILES,),
+        [columns(errors, tile), columns(words, tile), whole(sigma)],
+        whole(sigma),
+        jax.ShapeDtypeStruct(sigma.shape, jnp.bfloat16),
+        (errors, words, sigma),
+        scratch=[pltpu.VMEM(sigma.shape, jnp.float32)],
+        cost=(2 * sigma.size * words.shape[1], 2 * (errors.size + words.size)),
+    )
+
+
+def gradient(codes, slopes, errors, rows):
+    tile = rows.shape[1] // TILES
+
+    def kernel(c_ref, s_ref, e_ref, x_ref, o_ref):
+        part = product(c_ref[...], e_ref[...], ((0,), (0,)))
+        o_ref[...] = part + product(s_ref[...], x_ref[...], ((0,), (0,)))
+
+    out = jax.ShapeDtypeStruct((codes.shape[1], rows.shape[1]), jnp.float32)
+    return local_call(
+        kernel,
+        (TILES,),
+        [whole(codes), whole(slopes), columns(errors, tile), columns(rows, tile)],
+        columns(out, tile),
+        out,
+        (codes, slopes, errors, rows),
+        cost=(4 * codes.size * rows.shape[1], 4 * (rows.size + out.size)),
+    )
 
 
 def ring_body(activations, act_blocks, dictionary, enc_bias, dec_bias):
@@ -157,42 +289,46 @@
         at = (place + step + count) % count
         return jnp.where(at < half, 2 * at, 2 * (count - 1 - at) + 1)
 
-    first = jnp.arange(LANES) == 0
-    tail = jnp.where(first, enc_bias[:, None], jnp.zeros((), enc_bias.dtype))
-    own_words = jnp.concatenate([dictionary, tail], axis=1)
-    words = {0: own_words}
-    from_left = from_right = (own_words[:cut], own_words[cut:])
-    for step in range(1, half):
-        from_left = tuple(to_right(x) for x in from_left)
-        from_right = tuple(to_left(x) for x in from_right[::-1])[::-1]
-        words[-step], words[step] = jnp.concatenate(from_left), jnp.concatenate(from_right)
-    words[half] = jnp.concatenate([to_right(from_left[0]), to_left(from_right[1])])
-
-    centred = (activations.astype(jnp.float32) - dec_bias.astype(jnp.float32)).astype(jnp.bfloat16)
-    centred = centred.reshape(half_blocks * rows_each, width)
-    rows = jnp.concatenate([centred, to_core(centred)])
-    ones = jnp.broadcast_to(first.astype(rows.dtype), (rows.shape[0], LANES))
-    rows_one = jnp.concatenate([rows, ones], axis=1)
     lists = act_blocks.reshape(2, half_blocks, act_blocks.shape[1])
     lists = jnp.where(row_index == 0, lists, lists[::-1]).reshape(2 * half_blocks, -1)
-
     steps = [0] + [s for t in range(1, half) for s in (-t, t)] + [half]
     owners = jnp.stack([owner(s) for s in steps])
     listed = jnp.any(lists[:, :, None] == owners, axis=1).astype(jnp.float32)
-    listed = lax.optimization_barrier(jnp.repeat(listed, rows_each, axis=0))
-
-    codes, sigmas = {}, {}
-    rebuilt = None
-    for i, step in enumerate(steps):
-        mask = listed[:, i : i + 1] > 0
-        preacts = jnp.einsum("rd,ld->rl", rows_one, words[step], preferred_element_type=jnp.float32)
-        code = jnp.where(mask, jax.nn.softplus(preacts), 0.0).astype(jnp.bfloat16)
-        sigma = jnp.where(mask, jax.nn.sigmoid(preacts), 0.0)
-        codes[step], sigmas[step] = lax.optimization_barrier((code, sigma))
-        pieces = jnp.einsum(
-            "rl,ld->rd", codes[step], words[step][:, :width], preferred_element_type=jnp.float32
-        )
-        rebuilt = pieces if rebuilt is None else rebuilt + pieces
+    listed = jnp.repeat(listed, rows_each, axis=0)
+
+    biases = jnp.broadcast_to(enc_bias.reshape(1, latents), (count, latents))
+    biases = lax.all_to_all(biases, "lat", split_axis=0, concat_axis=0, tiled=True)
+    pick = (owners[:, None] == jnp.arange(count)).astype(biases.dtype)
+    biases = jnp.einsum("so,ol->sl", pick, biases, preferred_element_type=jnp.float32)
+
+    acts = activations.reshape(half_blocks * rows_each, width)
+    rows = None
+
+    words = {0: dictionary}
+    codes, sigmas, rebuilt = {}, {}, None
+    for t in range(1, half):
+        arrived = to_right(words[1 - t]), to_left(words[t - 1])
+        if t == 1:
+            words[-1], words[1] = after(arrived, biases)
+            (shift,) = after((dec_bias.reshape(1, width),), words[1])
+            rows = centre(acts, to_core(acts), shift)
+        else:
+            words[-t], words[t] = after(arrived, rebuilt)
+        for step in (-t, t) if t > 1 else (0, -t, t):
+            which = steps.index(step)
+            codes[step], sigmas[step] = encode(rows, words[step], biases, listed, which)
+            rebuilt = decode(codes[step], words[step], rebuilt)
+    last = to_right(words[1 - half][:cut]), to_left(words[half - 1][cut:])
+    words[half] = jnp.concatenate(after(last, rebuilt))
+    preacts = jnp.einsum("rd,ld->rl", rows, words[half], preferred_element_type=jnp.float32)
+    preacts = preacts + biases[-1:]
+    mask = listed[:, len(steps) - 1 :] > 0
+    code = jnp.where(mask, jax.nn.softplus(preacts), 0.0).astype(jnp.bfloat16)
+    sigma = jnp.where(mask, jax.nn.sigmoid(preacts), 0.0)
+    codes[half], sigmas[half] = lax.optimization_barrier((code, sigma))
+    rebuilt = rebuilt + jnp.einsum(
+        "rl,ld->rd", codes[half], words[half], preferred_element_type=jnp.float32
+    )
     rebuilt = rebuilt.astype(jnp.bfloat16)
     swapped = to_core(rebuilt)
     middle = half_blocks * rows_each
@@ -201,20 +337,17 @@
     errors = errors.astype(jnp.bfloat16)
 
     def grads_of(step, token):
-        code, sigma = codes[step], sigmas[step]
-        if token is not None:
-            code, sigma = after((code, sigma), token)
-        slopes = jnp.einsum(
-            "rd,ld->rl", errors, words[step][:, :width], preferred_element_type=jnp.float32
-        )
-        slopes = lax.optimization_barrier((slopes * sigma).astype(jnp.bfloat16))
-        total = jnp.einsum("rl,rd->ld", code, errors, preferred_element_type=jnp.float32)
-        return total + jnp.einsum("rl,rd->ld", slopes, rows, preferred_element_type=jnp.float32)
+        (sigma,) = after((sigmas[step],), token)
+        slopes = slope(errors, words[step], sigma)
+        return gradient(codes[step], slopes, errors, rows)
 
     def send(x):
         return x.astype(jnp.bfloat16)
 
-    far = send(grads_of(half, None))
+    slopes = jnp.einsum("rd,ld->rl", errors, words[half], preferred_element_type=jnp.float32)
+    slopes = lax.optimization_barrier((slopes * sigmas[half]).astype(jnp.bfloat16))
+    far = jnp.einsum("rl,rd->ld", codes[half], errors, preferred_element_type=jnp.float32)
+    far = send(far + jnp.einsum("rl,rd->ld", slopes, rows, preferred_element_type=jnp.float32))
     up = (to_right(far[:cut]), None)
     down = (None, to_left(far[cut:]))
     tokens = (far, far)

time: 196 us -> 186 us (0.949)
  Pallas kernels: 0.01 us -> 53.5 us
  waiting for transfers between devices: 126 us -> 90.1 us
  matrix products: 26 us -> 3.36 us
  other arithmetic: 7.2 us -> 3.99 us
    pallas_call x0 -> x29, Pallas kernels: none -> 53.4 us  [local_call(): pl.pallas_call(kernel, grid=grid, in_specs=in_specs, out_specs=out_specs,...]
    ppermute x14 -> x11, waiting for transfers between devices: 113 us -> 63.6 us  [to_right(): return lax.ppermute(x, 'lat', right_pairs)]
    dot_general x40 -> x6, matrix products: 26 us -> 3.36 us  [the longest x1 0.77 us: ring_body(): jnp.einsum('rd,ld->rl', rows, words[half], preferred_element_type=jnp.flo...]
    all_to_all x0 -> x1, waiting for transfers between devices: none -> 20 us  [ring_body(): lax.all_to_all(biases, 'lat', split_axis=0, concat_axis=0, tiled=True)]
    ppermute x14 -> x11, starting transfers between devices: 20.3 us -> 9.01 us  [to_right(): return lax.ppermute(x, 'lat', right_pairs)]
    ppermute x14 -> x11, waiting for transfers between devices: 8.84 us -> 2.32 us  [to_left(): return lax.ppermute(x, 'lat', left_pairs)]
    all_to_all x0 -> x1, starting transfers between devices: none -> 6.19 us  [ring_body(): lax.all_to_all(biases, 'lat', split_axis=0, concat_axis=0, tiled=True)]
    ppermute x14 -> x11, starting transfers between devices: 11.7 us -> 15.3 us  [to_left(): return lax.ppermute(x, 'lat', left_pairs)]
  transfers between devices with their start and end apart: 30 -> 25, of which waited for: 18 -> 15; matrix products, arithmetic and copies ran while one was open for 12% -> 2% of each run, Pallas kernels for 0% -> 29%
where the time goes in v3:
time: 186 us
  waiting for transfers between devices  90.1 us (48%)
  Pallas kernels  53.5 us (29%)
  starting transfers between devices  30.5 us (16%)
  other arithmetic  3.99 us (2%)
  local copies, waits for them, and re-layouts  3.4 us (2%)
  matrix products  3.36 us (2%)
    ppermute x11, waiting for transfers between devices, to_right(): return lax.ppermute(x, 'lat', right_pairs)  63.6 us
    pallas_call x29, Pallas kernels, local_call(): pl.pallas_call(kernel, grid=grid, in_specs=in_specs, out_specs=out_specs,...  53.4 us
    all_to_all x1, waiting for transfers between devices, ring_body(): lax.all_to_all(biases, 'lat', split_axis=0, concat_axis=0, tiled=True)  20 us
    ppermute x11, starting transfers between devices, to_left(): return lax.ppermute(x, 'lat', left_pairs)  15.3 us
    ppermute x11, starting transfers between devices, to_right(): return lax.ppermute(x, 'lat', right_pairs)  9.01 us
    all_to_all x1, starting transfers between devices, ring_body(): lax.all_to_all(biases, 'lat', split_axis=0, concat_axis=0, tiled=True)  6.19 us
    ppermute x2, waiting for transfers between devices, to_core(): return lax.ppermute(x, 'row', [(0, 1), (1, 0)])  4.15 us
  transfers between devices with their start and end apart: 25, of which 15 were waited for; matrix products, arithmetic and copies ran while one was open for 2% of the time, Pallas kernels for 29%

profile of v3, /device:TPU:0, one launch (start us, length us, event | category | flops | bytes accessed | tf_op | source)
XLA Modules:
  0.0 185.5 jit_solution(13614803434827968320)
XLA Ops:
  0.0 2.9 %collective-permute-start.2 = (bf16[128,4096]{1,0:T(8,128)(2,1)}, bf16[128,4096]{1,0:T(8,128)(2,1)S(1)}, u32[]{:S(2)}, u32[]{:S(2)}) collective-permute-start(bf16[128,4096]{1,0:T(8,128)(2,1)} %w_ref.5), channel_id=1, source_target_pairs={{4,0},{8,4},{12,8},{14,12},{10,14},{6,10},{2,6},{0,2},{5,1},{9,5},... | collective-permute-start | bytes 3145736 | tf_op jit(solution)/shard_map/ppermute | solution.py:283
  4.3 6.2 %all-to-all-start = ((bf16[8,1,128]{2,1,0:T(2,128)(2,1)}), bf16[8,1,128]{2,1,0:T(2,128)(2,1)S(1)}, u32[]{:S(2)}, u32[]{:S(2)}) async-start(bf16[8,1,128]{2,1,0:T(2,128)(2,1)} %broadcast_in_dim.27), calls=%async_computation | async-start | bytes 8192 | tf_op jit(solution)/shard_map/all_to_all | solution.py:300
  10.8 20.0 %all-to-all-done = bf16[8,1,128]{2,1,0:T(2,128)(2,1)S(1)} async-done(((bf16[8,1,128]{2,1,0:T(2,128)(2,1)}), bf16[8,1,128]{2,1,0:T(2,128)(2,1)S(1)}, u32[]{:S(2)}, u32[]{:S(2)}) %all-to-all-start) | async-done | bytes 2080 | tf_op jit(solution)/shard_map/all_to_all | solution.py:300
  34.7 2.4 %shard_map.57.x_ref = bf16[256,4096]{1,0:T(8,128)(2,1)S(1)} custom-call(bf16[128,4096]{1,0:T(8,128)(2,1)S(1)} %bitcast.41, bf16[128,4096]{1,0:T(8,128)(2,1)} %collective-permute-done.y_ref, bf16[1,4096]{1,0:T(2,128)(2,1)S(1)} %shard_map.56.b_ref), custom_call_target="tpu_custom_call" | custom-call | tf_op jit(solution)/shard_map/pallas_call | solution.py:135
  37.1 1.6 shard_map.60
  38.7 1.6 shard_map.59
  40.4 1.6 shard_map.58
  43.5 1.8 shard_map.62.rest_0_
  45.3 1.8 shard_map.63.refs_2_.rest_0_
  47.2 7.3 %collective-permute-done.3.refs_0_ = bf16[128,4096]{1,0:T(8,128)(2,1)S(1)} collective-permute-done((bf16[128,4096]{1,0:T(8,128)(2,1)S(1)}, bf16[128,4096]{1,0:T(8,128)(2,1)S(1)}, u32[]{:S(2)}, u32[]{:S(2)}) %collective-permute-start.3) | collective-permute-done | bytes 1048608 | tf_op jit(solution)/shard_map/ppermute | solution.py:280
  58.4 3.1 %shard_map.65 = (bf16[256,128]{1,0:T(8,128)(2,1)S(1)}, f32[256,128]{1,0:T(8,128)S(1)}) custom-call(bf16[256,4096]{1,0:T(8,128)(2,1)S(1)} %shard_map.57.x_ref, bf16[128,4096]{1,0:T(8,128)(2,1)} %get-tuple-element.35.w_ref, f32[8,128]{1,0:T(8,128)S(1)} %fusion.19.refs_2_.b_ref, f32[256,8]{1,0:T(8,128)S(1)} %bitcast.36), custom_call_target="tpu_custom_call" | custom-call | tf_op jit(solution)/shard_map/pallas_call | solution.py:135
  61.5 1.8 shard_map.67.rest_0_
  63.4 3.1 %shard_map.68.refs_2_.rest_0_ = f32[256,4096]{1,0:T(8,128)S(1)} custom-call(bf16[256,128]{1,0:T(8,128)(2,1)S(1)} %get-tuple-element.36.c_ref, bf16[128,4096]{1,0:T(8,128)(2,1)} %get-tuple-element.35.w_ref, f32[256,4096]{1,0:T(8,128)S(1)} %shard_map.67.rest_0_), custom_call_target="tpu_custom_call", output_to_operand_aliasing={{}: (2, {})} | custom-call | tf_op jit(solution)/shard_map/pallas_call | solution.py:135
  66.5 11.4 %collective-permute-done.5.refs_0_ = bf16[128,4096]{1,0:T(8,128)(2,1)S(1)} collective-permute-done((bf16[128,4096]{1,0:T(8,128)(2,1)S(1)}, bf16[128,4096]{1,0:T(8,128)(2,1)S(1)}, u32[]{:S(2)}, u32[]{:S(2)}) %collective-permute-start.5) | collective-permute-done | bytes 1048608 | tf_op jit(solution)/shard_map/ppermute | solution.py:280
  80.4 1.6 shard_map.70
  83.6 1.8 shard_map.72.rest_0_
  85.5 1.8 shard_map.73.refs_2_
  90.4 4.1 %collective-permute-done.9 = bf16[256,4096]{1,0:T(8,128)(2,1)S(1)} collective-permute-done((bf16[256,4096]{1,0:T(8,128)(2,1)S(1)}, bf16[256,4096]{1,0:T(8,128)(2,1)S(1)}, u32[]{:S(2)}, u32[]{:S(2)}) %collective-permute-start.9) | collective-permute-done | bytes 2097184 | tf_op jit(solution)/shard_map/ppermute | solution.py:286
  101.3 1.8 shard_map.80
  105.8 1.8 shard_map.89
  108.9 3.7 %collective-permute-done.10.refs_1_ = bf16[64,4096]{1,0:T(8,128)(2,1)S(1)} collective-permute-done((bf16[64,4096]{1,0:T(8,128)(2,1)S(1)}, bf16[64,4096]{1,0:T(8,128)(2,1)S(1)}, u32[]{:S(2)}, u32[]{:S(2)}) %collective-permute-start.10) | collective-permute-done | bytes 524320 | tf_op jit(solution)/shard_map/ppermute | solution.py:280
  116.4 3.0 %shard_map.76.s_ref = bf16[256,128]{1,0:T(8,128)(2,1)S(1)} custom-call(bf16[256,4096]{1,0:T(8,128)(2,1)S(1)} %subtract_convert_fusion.e_ref, bf16[128,4096]{1,0:T(8,128)(2,1)} %get-tuple-element.35.w_ref, f32[256,128]{1,0:T(8,128)S(1)} %shard_map.75.s_ref), custom_call_target="tpu_custom_call" | custom-call | flops 268435456 | bytes 3145728 | tf_op jit(solution)/shard_map/pallas_call | solution.py:135
  119.4 1.8 shard_map.77
  121.2 1.8 shard_map.95
  123.8 10.4 %collective-permute-done.11.refs_1_ = bf16[64,4096]{1,0:T(8,128)(2,1)S(1)} collective-permute-done((bf16[64,4096]{1,0:T(8,128)(2,1)S(1)}, bf16[64,4096]{1,0:T(8,128)(2,1)S(1)}, u32[]{:S(2)}, u32[]{:S(2)}) %collective-permute-start.11) | collective-permute-done | bytes 524320 | tf_op jit(solution)/shard_map/ppermute | solution.py:280
  141.9 1.8 shard_map.92
  143.7 1.8 shard_map.86
  145.5 3.9 %collective-permute-done.20 = bf16[64,4096]{1,0:T(8,128)(2,1)S(1)} collective-permute-done((bf16[64,4096]{1,0:T(8,128)(2,1)S(1)}, bf16[64,4096]{1,0:T(8,128)(2,1)S(1)}, u32[]{:S(2)}, u32[]{:S(2)}) %collective-permute-start.20) | collective-permute-done | bytes 524320 | tf_op jit(solution)/shard_map/ppermute | solution.py:280
  149.3 9.5 %collective-permute-done.12.refs_1_ = bf16[64,4096]{1,0:T(8,128)(2,1)S(1)} collective-permute-done((bf16[64,4096]{1,0:T(8,128)(2,1)S(1)}, bf16[64,4096]{1,0:T(8,128)(2,1)S(1)}, u32[]{:S(2)}, u32[]{:S(2)}) %collective-permute-start.12) | collective-permute-done | bytes 524320 | tf_op jit(solution)/shard_map/ppermute | solution.py:280
  165.0 1.8 shard_map.83
  166.8 7.2 %collective-permute-done.13 = bf16[64,4096]{1,0:T(8,128)(2,1)S(1)} collective-permute-done((bf16[64,4096]{1,0:T(8,128)(2,1)S(1)}, bf16[64,4096]{1,0:T(8,128)(2,1)S(1)}, u32[]{:S(2)}, u32[]{:S(2)}) %collective-permute-start.13) | collective-permute-done | bytes 524320 | tf_op jit(solution)/shard_map/ppermute | solution.py:280
  174.0 8.6 %collective-permute-done.21 = bf16[64,4096]{1,0:T(8,128)(2,1)S(1)} collective-permute-done((bf16[64,4096]{1,0:T(8,128)(2,1)S(1)}, bf16[64,4096]{1,0:T(8,128)(2,1)S(1)}, u32[]{:S(2)}, u32[]{:S(2)}) %collective-permute-start.21) | collective-permute-done | bytes 524320 | tf_op jit(solution)/shard_map/ppermute | solution.py:280
  (103 shorter events, 49.9 us)
Async XLA Ops:
  0.0 33.1 %copy-start.3 = (s32[16,4]{0,1:T(4,128)S(1)}, s32[16,4]{0,1:T(4,128)}, u32[]{:S(2)}) copy-start(s32[16,4]{0,1:T(4,128)} %param.6) | copy-start | bytes 772
  0.0 33.4 %copy-start.2 = (bf16[4096]{0:T(1024)(128)(2,1)S(1)}, bf16[4096]{0:T(1024)(128)(2,1)}, u32[]{:S(2)}) copy-start(bf16[4096]{0:T(1024)(128)(2,1)} %param.9) | copy-start | bytes 24580
  0.0 31.0 %collective-permute-start.2 = (bf16[128,4096]{1,0:T(8,128)(2,1)}, bf16[128,4096]{1,0:T(8,128)(2,1)S(1)}, u32[]{:S(2)}, u32[]{:S(2)}) collective-permute-start(bf16[128,4096]{1,0:T(8,128)(2,1)} %w_ref.5), channel_id=1, source_target_pairs={{4,0},{8,4},{12,8},{14,12},{10,14},{6,10},{2,6},{0,2},{5,1},{9,5},... | collective-permute-start | bytes 3145736 | tf_op jit(solution)/shard_map/ppermute | solution.py:283
  2.9 28.1 %collective-permute-start.1 = (bf16[128,4096]{1,0:T(8,128)(2,1)}, bf16[128,4096]{1,0:T(8,128)(2,1)S(1)}, u32[]{:S(2)}, u32[]{:S(2)}) collective-permute-start(bf16[128,4096]{1,0:T(8,128)(2,1)} %w_ref.5), channel_id=1, source_target_pairs={{0,4},{4,8},{8,12},{12,14},{14,10},{10,6},{6,2},{2,0},{1,5},{5,9},... | collective-permute-start | bytes 3145736 | tf_op jit(solution)/shard_map/ppermute | solution.py:280
  4.3 26.5 %all-to-all-start = ((bf16[8,1,128]{2,1,0:T(2,128)(2,1)}), bf16[8,1,128]{2,1,0:T(2,128)(2,1)S(1)}, u32[]{:S(2)}, u32[]{:S(2)}) async-start(bf16[8,1,128]{2,1,0:T(2,128)(2,1)} %broadcast_in_dim.27), calls=%async_computation | async-start | bytes 8192 | tf_op jit(solution)/shard_map/all_to_all | solution.py:300
  10.5 22.9 %collective-permute-start = (bf16[128,4096]{1,0:T(8,128)(2,1)}, bf16[128,4096]{1,0:T(8,128)(2,1)}, u32[]{:S(2)}, u32[]{:S(2)}) collective-permute-start(bf16[128,4096]{1,0:T(8,128)(2,1)} %bitcast.40), channel_id=1, source_target_pairs={{0,1},{1,0},{2,3},{3,2},{4,5},{5,4},{6,7},{7,6},{8,9},{9,8},{10,11... | collective-permute-start | bytes 3145736 | tf_op jit(solution)/shard_map/ppermute | solution.py:286
  31.0 23.4 %collective-permute-start.3 = (bf16[128,4096]{1,0:T(8,128)(2,1)S(1)}, bf16[128,4096]{1,0:T(8,128)(2,1)S(1)}, u32[]{:S(2)}, u32[]{:S(2)}) collective-permute-start(bf16[128,4096]{1,0:T(8,128)(2,1)S(1)} %get-tuple-element.31.w_ref), channel_id=1, source_target_pairs={{0,4},{4,8},{8,12},{12,14},{14,10},{10,6},{6,2},{2,0},{1,5},{5,9},... | collective-permute-start | bytes 3145736 | tf_op jit(solution)/shard_map/ppermute | solution.py:280
  31.6 23.2 %collective-permute-start.4 = (bf16[128,4096]{1,0:T(8,128)(2,1)S(1)}, bf16[128,4096]{1,0:T(8,128)(2,1)}, u32[]{:S(2)}, u32[]{:S(2)}) collective-permute-start(bf16[128,4096]{1,0:T(8,128)(2,1)S(1)} %get-tuple-element.29.refs_1_.w_ref), channel_id=1, source_target_pairs={{4,0},{8,4},{12,8},{14,12},{10,14},{6,10},{2,6},{0,2},{5,1},{9,5},... | collective-permute-start | bytes 3145736 | tf_op jit(solution)/shard_map/ppermute | solution.py:283
  33.5 1.2 copy-start.1
  38.7 1.6 copy-start
  54.8 23.0 %collective-permute-start.5 = (bf16[128,4096]{1,0:T(8,128)(2,1)S(1)}, bf16[128,4096]{1,0:T(8,128)(2,1)S(1)}, u32[]{:S(2)}, u32[]{:S(2)}) collective-permute-start(bf16[128,4096]{1,0:T(8,128)(2,1)S(1)} %get-tuple-element.34.w_ref), channel_id=1, source_target_pairs={{0,4},{4,8},{8,12},{12,14},{14,10},{10,6},{6,2},{2,0},{1,5},{5,9},... | collective-permute-start | bytes 3145736 | tf_op jit(solution)/shard_map/ppermute | solution.py:280
  55.4 22.4 %collective-permute-start.6 = (bf16[128,4096]{1,0:T(8,128)(2,1)}, bf16[128,4096]{1,0:T(8,128)(2,1)S(1)}, u32[]{:S(2)}, u32[]{:S(2)}) collective-permute-start(bf16[128,4096]{1,0:T(8,128)(2,1)} %get-tuple-element.35.w_ref), channel_id=1, source_target_pairs={{4,0},{8,4},{12,8},{14,12},{10,14},{6,10},{2,6},{0,2},{5,1},{9,5},... | collective-permute-start | bytes 3145736 | tf_op jit(solution)/shard_map/ppermute | solution.py:283
  77.9 10.4 %collective-permute-start.7 = (bf16[64,4096]{1,0:T(8,128)(2,1)S(1)}, bf16[64,4096]{1,0:T(8,128)(2,1)S(1)}, u32[]{:S(2)}, u32[]{:S(2)}) collective-permute-start(bf16[64,4096]{1,0:T(8,128)(2,1)S(1)} %slice.69), channel_id=1, source_target_pairs={{0,4},{4,8},{8,12},{12,14},{14,10},{10,6},{6,2},{2,0},{1,5},{5,9},... | collective-permute-start | bytes 1572872 | tf_op jit(solution)/shard_map/ppermute | solution.py:280
  79.0 9.8 %collective-permute-start.8 = (bf16[64,4096]{1,0:T(8,128)(2,1)S(1)}, bf16[64,4096]{1,0:T(8,128)(2,1)S(1)}, u32[]{:S(2)}, u32[]{:S(2)}) collective-permute-start(bf16[64,4096]{1,0:T(8,128)(2,1)S(1)} %slice.70), channel_id=1, source_target_pairs={{4,0},{8,4},{12,8},{14,12},{10,14},{6,10},{2,6},{0,2},{5,1},{9,5},... | collective-permute-start | bytes 1572872 | tf_op jit(solution)/shard_map/ppermute | solution.py:283
  90.3 4.2 %collective-permute-start.9 = (bf16[256,4096]{1,0:T(8,128)(2,1)S(1)}, bf16[256,4096]{1,0:T(8,128)(2,1)S(1)}, u32[]{:S(2)}, u32[]{:S(2)}) collective-permute-start(bf16[256,4096]{1,0:T(8,128)(2,1)S(1)} %fusion), channel_id=1, source_target_pairs={{0,1},{1,0},{2,3},{3,2},{4,5},{5,4},{6,7},{7,6},{8,9},{9,8},{10,11... | collective-permute-start | bytes 6291464 | tf_op jit(solution)/shard_map/ppermute | solution.py:286
  97.7 14.8 %collective-permute-start.10 = (bf16[64,4096]{1,0:T(8,128)(2,1)S(1)}, bf16[64,4096]{1,0:T(8,128)(2,1)S(1)}, u32[]{:S(2)}, u32[]{:S(2)}) collective-permute-start(bf16[64,4096]{1,0:T(8,128)(2,1)S(1)} %get-tuple-element.66), channel_id=1, source_target_pairs={{0,4},{4,8},{8,12},{12,14},{14,10},{10,6},{6,2},{2,0},{1,5},{5,9},... | collective-permute-start | bytes 1572872 | tf_op jit(solution)/shard_map/ppermute | solution.py:280
  98.7 14.9 %collective-permute-start.14 = (bf16[64,4096]{1,0:T(8,128)(2,1)S(1)}, bf16[64,4096]{1,0:T(8,128)(2,1)S(1)}, u32[]{:S(2)}, u32[]{:S(2)}) collective-permute-start(bf16[64,4096]{1,0:T(8,128)(2,1)S(1)} %get-tuple-element.65), channel_id=1, source_target_pairs={{4,0},{8,4},{12,8},{14,12},{10,14},{6,10},{2,6},{0,2},{5,1},{9,5},... | collective-permute-start | bytes 1572872 | tf_op jit(solution)/shard_map/ppermute | solution.py:283
  103.2 20.6 %collective-permute-start.19 = (bf16[64,4096]{1,0:T(8,128)(2,1)S(1)}, bf16[64,4096]{1,0:T(8,128)(2,1)S(1)}, u32[]{:S(2)}, u32[]{:S(2)}) collective-permute-start(bf16[64,4096]{1,0:T(8,128)(2,1)S(1)} %slice.151), channel_id=1, source_target_pairs={{0,4},{4,8},{8,12},{12,14},{14,10},{10,6},{6,2},{2,0},{1,5},{5,9},... | collective-permute-start | bytes 1572872 | tf_op jit(solution)/shard_map/ppermute | solution.py:280
  107.7 28.5 %collective-permute-start.16 = (bf16[64,4096]{1,0:T(8,128)(2,1)S(1)}, bf16[64,4096]{1,0:T(8,128)(2,1)S(1)}, u32[]{:S(2)}, u32[]{:S(2)}) collective-permute-start(bf16[64,4096]{1,0:T(8,128)(2,1)S(1)} %slice.152), channel_id=1, source_target_pairs={{4,0},{8,4},{12,8},{14,12},{10,14},{6,10},{2,6},{0,2},{5,1},{9,5},... | collective-permute-start | bytes 1572872 | tf_op jit(solution)/shard_map/ppermute | solution.py:283
  112.7 21.6 %collective-permute-start.11 = (bf16[64,4096]{1,0:T(8,128)(2,1)S(1)}, bf16[64,4096]{1,0:T(8,128)(2,1)S(1)}, u32[]{:S(2)}, u32[]{:S(2)}) collective-permute-start(bf16[64,4096]{1,0:T(8,128)(2,1)S(1)} %fusion.14), channel_id=1, source_target_pairs={{0,4},{4,8},{8,12},{12,14},{14,10},{10,6},{6,2},{2,0},{1,5},{5,9},... | collective-permute-start | bytes 1572872 | tf_op jit(solution)/shard_map/ppermute | solution.py:280
  113.7 22.5 %collective-permute-start.15 = (bf16[64,4096]{1,0:T(8,128)(2,1)S(1)}, bf16[64,4096]{1,0:T(8,128)(2,1)S(1)}, u32[]{:S(2)}, u32[]{:S(2)}) collective-permute-start(bf16[64,4096]{1,0:T(8,128)(2,1)S(1)} %fusion.11), channel_id=1, source_target_pairs={{4,0},{8,4},{12,8},{14,12},{10,14},{6,10},{2,6},{0,2},{5,1},{9,5},... | collective-permute-start | bytes 1572872 | tf_op jit(solution)/shard_map/ppermute | solution.py:283
  134.4 14.9 %collective-permute-start.20 = (bf16[64,4096]{1,0:T(8,128)(2,1)S(1)}, bf16[64,4096]{1,0:T(8,128)(2,1)S(1)}, u32[]{:S(2)}, u32[]{:S(2)}) collective-permute-start(bf16[64,4096]{1,0:T(8,128)(2,1)S(1)} %get-tuple-element.61), channel_id=1, source_target_pairs={{0,4},{4,8},{8,12},{12,14},{14,10},{10,6},{6,2},{2,0},{1,5},{5,9},... | collective-permute-start | bytes 1572872 | tf_op jit(solution)/shard_map/ppermute | solution.py:280
  135.4 23.5 %collective-permute-start.12 = (bf16[64,4096]{1,0:T(8,128)(2,1)S(1)}, bf16[64,4096]{1,0:T(8,128)(2,1)S(1)}, u32[]{:S(2)}, u32[]{:S(2)}) collective-permute-start(bf16[64,4096]{1,0:T(8,128)(2,1)S(1)} %get-tuple-element.62), channel_id=1, source_target_pairs={{0,4},{4,8},{8,12},{12,14},{14,10},{10,6},{6,2},{2,0},{1,5},{5,9},... | collective-permute-start | bytes 1572872 | tf_op jit(solution)/shard_map/ppermute | solution.py:280
  136.5 24.4 %collective-permute-start.17 = (bf16[64,4096]{1,0:T(8,128)(2,1)S(1)}, bf16[64,4096]{1,0:T(8,128)(2,1)S(1)}, u32[]{:S(2)}, u32[]{:S(2)}) collective-permute-start(bf16[64,4096]{1,0:T(8,128)(2,1)S(1)} %get-tuple-element.59), channel_id=1, source_target_pairs={{4,0},{8,4},{12,8},{14,12},{10,14},{6,10},{2,6},{0,2},{5,1},{9,5},... | collective-permute-start | bytes 1572872 | tf_op jit(solution)/shard_map/ppermute | solution.py:283
  137.7 23.2 %collective-permute-start.22 = (bf16[64,4096]{1,0:T(8,128)(2,1)S(1)}, bf16[64,4096]{1,0:T(8,128)(2,1)S(1)}, u32[]{:S(2)}, u32[]{:S(2)}) collective-permute-start(bf16[64,4096]{1,0:T(8,128)(2,1)S(1)} %get-tuple-element.60), channel_id=1, source_target_pairs={{4,0},{8,4},{12,8},{14,12},{10,14},{6,10},{2,6},{0,2},{5,1},{9,5},... | collective-permute-start | bytes 1572872 | tf_op jit(solution)/shard_map/ppermute | solution.py:283
  159.1 14.9 %collective-permute-start.13 = (bf16[64,4096]{1,0:T(8,128)(2,1)S(1)}, bf16[64,4096]{1,0:T(8,128)(2,1)S(1)}, u32[]{:S(2)}, u32[]{:S(2)}) collective-permute-start(bf16[64,4096]{1,0:T(8,128)(2,1)S(1)} %get-tuple-element.55), channel_id=1, source_target_pairs={{0,4},{4,8},{8,12},{12,14},{14,10},{10,6},{6,2},{2,0},{1,5},{5,9},... | collective-permute-start | bytes 1572872 | tf_op jit(solution)/shard_map/ppermute | solution.py:280
  160.0 22.6 %collective-permute-start.21 = (bf16[64,4096]{1,0:T(8,128)(2,1)S(1)}, bf16[64,4096]{1,0:T(8,128)(2,1)S(1)}, u32[]{:S(2)}, u32[]{:S(2)}) collective-permute-start(bf16[64,4096]{1,0:T(8,128)(2,1)S(1)} %get-tuple-element.56), channel_id=1, source_target_pairs={{0,4},{4,8},{8,12},{12,14},{14,10},{10,6},{6,2},{2,0},{1,5},{5,9},... | collective-permute-start | bytes 1572872 | tf_op jit(solution)/shard_map/ppermute | solution.py:280
  161.2 21.5 %collective-permute-start.18 = (bf16[64,4096]{1,0:T(8,128)(2,1)S(1)}, bf16[64,4096]{1,0:T(8,128)(2,1)S(1)}, u32[]{:S(2)}, u32[]{:S(2)}) collective-permute-start(bf16[64,4096]{1,0:T(8,128)(2,1)S(1)} %get-tuple-element.57), channel_id=1, source_target_pairs={{4,0},{8,4},{12,8},{14,12},{10,14},{6,10},{2,6},{0,2},{5,1},{9,5},... | collective-permute-start | bytes 1572872 | tf_op jit(solution)/shard_map/ppermute | solution.py:283
  162.4 21.7 %collective-permute-start.23 = (bf16[64,4096]{1,0:T(8,128)(2,1)S(1)}, bf16[64,4096]{1,0:T(8,128)(2,1)S(1)}, u32[]{:S(2)}, u32[]{:S(2)}) collective-permute-start(bf16[64,4096]{1,0:T(8,128)(2,1)S(1)} %get-tuple-element.58), channel_id=1, source_target_pairs={{4,0},{8,4},{12,8},{14,12},{10,14},{6,10},{2,6},{0,2},{5,1},{9,5},... | collective-permute-start | bytes 1572872 | tf_op jit(solution)/shard_map/ppermute | solution.py:283

commit v4 on v3

--- a/solution.py
+++ b/solution.py
@@ -259,6 +259,40 @@
         (codes, slopes, errors, rows),
         cost=(4 * codes.size * rows.shape[1], 4 * (rows.size + out.size)),
     )
+
+
+def join(total, came, which):
+    count, width = total.shape[0] // 2, total.shape[1]
+    tile = width // TILES
+
+    def kernel(*refs):
+        value = refs[0][...]
+        for ref in refs[1:-1]:
+            value = value + ref[...].astype(jnp.float32)
+        refs[-1][...] = value.astype(refs[-1].dtype)
+
+    out = jax.ShapeDtypeStruct((count, width), jnp.bfloat16)
+    args = (total,) if came is None else (total, came)
+    specs = [pl.BlockSpec((count, tile), lambda i: (which, i))]
+    specs += [columns(out, tile)] * (len(args) - 1)
+    cost = (out.size, 8 * out.size)
+    return local_call(kernel, (TILES,), specs, columns(out, tile), out, args, cost=cost)
+
+
+def finish(total, ups, downs, scale):
+    width, cut = total.shape[1], total.shape[0] // 2
+    tile = width // TILES
+
+    def kernel(t_ref, *refs):
+        for k in range(2):
+            half = slice(k * cut, (k + 1) * cut)
+            came = refs[k][...].astype(jnp.float32) + refs[2 + k][...].astype(jnp.float32)
+            refs[-1][half, :] = ((t_ref[half, :] + came) / scale).astype(refs[-1].dtype)
+
+    out = jax.ShapeDtypeStruct(total.shape, jnp.bfloat16)
+    args = (total, *ups, *downs)
+    specs = [columns(x, tile) for x in args]
+    return local_call(kernel, (TILES,), specs, columns(out, tile), out, args)
 
 
 def ring_body(activations, act_blocks, dictionary, enc_bias, dec_bias):
@@ -354,22 +388,9 @@
     for step in range(half - 1, 0, -1):
         ahead, behind = grads_of(step, tokens[0]), grads_of(-step, tokens[1])
         tokens = (up[0], down[1])
-        parts = []
-        for total, came in ((ahead, up), (behind, down)):
-            pieces = (total[:cut], total[cut:])
-            parts.append(
-                [send(p if c is None else p + c.astype(jnp.float32)) for p, c in zip(pieces, came)]
-            )
-        up = tuple(to_right(p) for p in parts[0])
-        down = tuple(to_left(p) for p in parts[1])
-    own = grads_of(0, tokens[0])
-    halves = []
-    for i, part in enumerate((own[:cut], own[cut:])):
-        for came in (up[i], down[i]):
-            if came is not None:
-                part = part + came.astype(jnp.float32)
-        halves.append(part)
-    return (jnp.concatenate(halves) / block_rows).astype(jnp.bfloat16)
+        up = tuple(to_right(join(ahead, came, k)) for k, came in enumerate(up))
+        down = tuple(to_left(join(behind, came, k)) for k, came in enumerate(down))
+    return finish(grads_of(0, tokens[0]), up, down, block_rows)
 
 
 def solution(mesh):

time: 186 us -> 182 us (0.978)
  waiting for transfers between devices: 90.1 us -> 83.1 us
  Pallas kernels: 53.5 us -> 59.1 us
  other arithmetic: 3.99 us -> 1.41 us
    ppermute x11, waiting for transfers between devices: 63.6 us -> 56.6 us  [to_right(): return lax.ppermute(x, 'lat', right_pairs)]
    pallas_call x29 -> x42, Pallas kernels: 53.4 us -> 59.1 us  [local_call(): pl.pallas_call(kernel, grid=grid, in_specs=in_specs, out_specs=out_specs,...]
    convert_element_type x7 -> x0, other arithmetic: 2.24 us -> none  [the longest x6 1.13 us: send(): return x.astype(jnp.bfloat16)]
  transfers between devices with their start and end apart: 25 -> 25, of which waited for: 15 -> 16; matrix products, arithmetic and copies ran while one was open for 2% -> 1% of each run, Pallas kernels for 29% -> 31%
where the time goes in v4:
time: 182 us
  waiting for transfers between devices  83.1 us (46%)
  Pallas kernels  59.1 us (32%)
  starting transfers between devices  30.7 us (17%)
  local copies, waits for them, and re-layouts  3.31 us (2%)
  matrix products  3.31 us (2%)
    pallas_call x42, Pallas kernels, local_call(): pl.pallas_call(kernel, grid=grid, in_specs=in_specs, out_specs=out_specs,...  59.1 us
    ppermute x11, waiting for transfers between devices, to_right(): return lax.ppermute(x, 'lat', right_pairs)  56.6 us
    all_to_all x1, waiting for transfers between devices, ring_body(): lax.all_to_all(biases, 'lat', split_axis=0, concat_axis=0, tiled=True)  20 us
    ppermute x11, starting transfers between devices, to_left(): return lax.ppermute(x, 'lat', left_pairs)  15.2 us
    ppermute x11, starting transfers between devices, to_right(): return lax.ppermute(x, 'lat', right_pairs)  9.25 us
    all_to_all x1, starting transfers between devices, ring_body(): lax.all_to_all(biases, 'lat', split_axis=0, concat_axis=0, tiled=True)  6.19 us
    ppermute x2, waiting for transfers between devices, to_core(): return lax.ppermute(x, 'row', [(0, 1), (1, 0)])  4.15 us
  transfers between devices with their start and end apart: 25, of which 16 were waited for; matrix products, arithmetic and copies ran while one was open for 1% of the time, Pallas kernels for 31%

profile of v4, /device:TPU:0, one launch (start us, length us, event | category | flops | bytes accessed | tf_op | source)
XLA Modules:
  0.0 181.7 jit_solution(11690038999924655357)
XLA Ops:
  0.0 2.9 %collective-permute-start.2 = (bf16[128,4096]{1,0:T(8,128)(2,1)}, bf16[128,4096]{1,0:T(8,128)(2,1)S(1)}, u32[]{:S(2)}, u32[]{:S(2)}) collective-permute-start(bf16[128,4096]{1,0:T(8,128)(2,1)} %w_ref.5), channel_id=1, source_target_pairs={{4,0},{8,4},{12,8},{14,12},{10,14},{6,10},{2,6},{0,2},{5,1},{9,5},... | collective-permute-start | bytes 3145736 | tf_op jit(solution)/shard_map/ppermute | solution.py:317
  4.3 6.2 %all-to-all-start = ((bf16[8,1,128]{2,1,0:T(2,128)(2,1)}), bf16[8,1,128]{2,1,0:T(2,128)(2,1)S(1)}, u32[]{:S(2)}, u32[]{:S(2)}) async-start(bf16[8,1,128]{2,1,0:T(2,128)(2,1)} %broadcast_in_dim.27), calls=%async_computation | async-start | bytes 8192 | tf_op jit(solution)/shard_map/all_to_all | solution.py:334
  10.8 20.0 %all-to-all-done = bf16[8,1,128]{2,1,0:T(2,128)(2,1)S(1)} async-done(((bf16[8,1,128]{2,1,0:T(2,128)(2,1)}), bf16[8,1,128]{2,1,0:T(2,128)(2,1)S(1)}, u32[]{:S(2)}, u32[]{:S(2)}) %all-to-all-start) | async-done | bytes 2080 | tf_op jit(solution)/shard_map/all_to_all | solution.py:334
  34.7 2.4 %shard_map.57.x_ref = bf16[256,4096]{1,0:T(8,128)(2,1)S(1)} custom-call(bf16[128,4096]{1,0:T(8,128)(2,1)S(1)} %bitcast.41, bf16[128,4096]{1,0:T(8,128)(2,1)} %collective-permute-done.y_ref, bf16[1,4096]{1,0:T(2,128)(2,1)S(1)} %shard_map.56.b_ref), custom_call_target="tpu_custom_call" | custom-call | tf_op jit(solution)/shard_map/pallas_call | solution.py:135
  37.1 1.6 shard_map.60
  38.7 1.6 shard_map.59
  43.5 1.8 %shard_map.62.rest_0_ = f32[256,4096]{1,0:T(8,128)S(1)} custom-call(bf16[256,128]{1,0:T(8,128)(2,1)S(1)} %get-tuple-element.33.c_ref, bf16[128,4096]{1,0:T(8,128)(2,1)S(1)} %get-tuple-element.31.w_ref, f32[256,4096]{1,0:T(8,128)S(1)} %shard_map.61.rest_0_), custom_call_target="tpu_custom_call", output_to_operand_aliasing={{}: (2, {})} | custom-call | tf_op jit(solution)/shard_map/pallas_call | solution.py:135
  45.3 1.8 %shard_map.63.refs_2_.rest_0_ = f32[256,4096]{1,0:T(8,128)S(1)} custom-call(bf16[256,128]{1,0:T(8,128)(2,1)S(1)} %get-tuple-element.32.c_ref, bf16[128,4096]{1,0:T(8,128)(2,1)S(1)} %get-tuple-element.29.refs_1_.w_ref, f32[256,4096]{1,0:T(8,128)S(1)} %shard_map.62.rest_0_), custom_call_target="tpu_custom_call", output_to_operand_aliasing={{}: (2, {})} | custom-call | tf_op jit(solution)/shard_map/pallas_call | solution.py:135
  47.2 7.3 %collective-permute-done.3.refs_0_ = bf16[128,4096]{1,0:T(8,128)(2,1)S(1)} collective-permute-done((bf16[128,4096]{1,0:T(8,128)(2,1)S(1)}, bf16[128,4096]{1,0:T(8,128)(2,1)S(1)}, u32[]{:S(2)}, u32[]{:S(2)}) %collective-permute-start.3) | collective-permute-done | bytes 1048608 | tf_op jit(solution)/shard_map/ppermute | solution.py:314
  58.4 3.1 %shard_map.65 = (bf16[256,128]{1,0:T(8,128)(2,1)S(1)}, f32[256,128]{1,0:T(8,128)S(1)}) custom-call(bf16[256,4096]{1,0:T(8,128)(2,1)S(1)} %shard_map.57.x_ref, bf16[128,4096]{1,0:T(8,128)(2,1)} %get-tuple-element.35.w_ref, f32[8,128]{1,0:T(8,128)S(1)} %fusion.6.refs_2_.b_ref, f32[256,8]{1,0:T(8,128)S(1)} %bitcast.36), custom_call_target="tpu_custom_call" | custom-call | tf_op jit(solution)/shard_map/pallas_call | solution.py:135
  61.5 1.8 %shard_map.67.rest_0_ = f32[256,4096]{1,0:T(8,128)S(1)} custom-call(bf16[256,128]{1,0:T(8,128)(2,1)S(1)} %get-tuple-element.37.c_ref, bf16[128,4096]{1,0:T(8,128)(2,1)S(1)} %get-tuple-element.34.w_ref, f32[256,4096]{1,0:T(8,128)S(1)} %shard_map.63.refs_2_.rest_0_), custom_call_target="tpu_custom_call", output_to_operand_aliasing={{}: (2, {})} | custom-call | tf_op jit(solution)/shard_map/pallas_call | solution.py:135
  63.4 3.1 %shard_map.68.refs_2_.rest_0_ = f32[256,4096]{1,0:T(8,128)S(1)} custom-call(bf16[256,128]{1,0:T(8,128)(2,1)S(1)} %get-tuple-element.36.c_ref, bf16[128,4096]{1,0:T(8,128)(2,1)} %get-tuple-element.35.w_ref, f32[256,4096]{1,0:T(8,128)S(1)} %shard_map.67.rest_0_), custom_call_target="tpu_custom_call", output_to_operand_aliasing={{}: (2, {})} | custom-call | tf_op jit(solution)/shard_map/pallas_call | solution.py:135
  66.5 11.4 %collective-permute-done.5.refs_0_ = bf16[128,4096]{1,0:T(8,128)(2,1)S(1)} collective-permute-done((bf16[128,4096]{1,0:T(8,128)(2,1)S(1)}, bf16[128,4096]{1,0:T(8,128)(2,1)S(1)}, u32[]{:S(2)}, u32[]{:S(2)}) %collective-permute-start.5) | collective-permute-done | bytes 1048608 | tf_op jit(solution)/shard_map/ppermute | solution.py:314
  83.6 1.8 %shard_map.72.rest_0_ = f32[256,4096]{1,0:T(8,128)S(1)} custom-call(bf16[256,128]{1,0:T(8,128)(2,1)S(1)} %get-tuple-element.41.c_ref, bf16[128,4096]{1,0:T(8,128)(2,1)S(1)} %get-tuple-element.40.w_ref, f32[256,4096]{1,0:T(8,128)S(1)} %shard_map.68.refs_2_.rest_0_), custom_call_target="tpu_custom_call", output_to_operand_aliasing={{}: (2, {})} | custom-call | tf_op jit(solution)/shard_map/pallas_call | solution.py:135
  85.5 1.8 %shard_map.73.refs_2_ = f32[256,4096]{1,0:T(8,128)S(1)} custom-call(bf16[256,128]{1,0:T(8,128)(2,1)S(1)} %get-tuple-element.39.c_ref, bf16[128,4096]{1,0:T(8,128)(2,1)S(1)} %get-tuple-element.38.w_ref, f32[256,4096]{1,0:T(8,128)S(1)} %shard_map.72.rest_0_), custom_call_target="tpu_custom_call", output_to_operand_aliasing={{}: (2, {})} | custom-call | tf_op jit(solution)/shard_map/pallas_call | solution.py:135
  90.4 4.1 %collective-permute-done.9 = bf16[256,4096]{1,0:T(8,128)(2,1)S(1)} collective-permute-done((bf16[256,4096]{1,0:T(8,128)(2,1)S(1)}, bf16[256,4096]{1,0:T(8,128)(2,1)S(1)}, u32[]{:S(2)}, u32[]{:S(2)}) %collective-permute-start.9) | collective-permute-done | bytes 2097184 | tf_op jit(solution)/shard_map/ppermute | solution.py:320
  101.3 1.8 shard_map.80.refs_0_
  106.0 1.8 shard_map.95.refs_0_
  109.2 3.3 %collective-permute-done.10.refs_1_ = bf16[64,4096]{1,0:T(8,128)(2,1)S(1)} collective-permute-done((bf16[64,4096]{1,0:T(8,128)(2,1)S(1)}, bf16[64,4096]{1,0:T(8,128)(2,1)S(1)}, u32[]{:S(2)}, u32[]{:S(2)}) %collective-permute-start.10) | collective-permute-done | bytes 524320 | tf_op jit(solution)/shard_map/ppermute | solution.py:314
  115.3 3.0 %shard_map.76.s_ref = bf16[256,128]{1,0:T(8,128)(2,1)S(1)} custom-call(bf16[256,4096]{1,0:T(8,128)(2,1)S(1)} %subtract_convert_fusion.e_ref, bf16[128,4096]{1,0:T(8,128)(2,1)} %get-tuple-element.35.w_ref, f32[256,128]{1,0:T(8,128)S(1)} %shard_map.75.s_ref), custom_call_target="tpu_custom_call" | custom-call | flops 268435456 | bytes 3145728 | tf_op jit(solution)/shard_map/pallas_call | solution.py:135
  118.3 1.8 shard_map.77.refs_0_
  120.1 3.7 %collective-permute-done.14.refs_1_ = bf16[64,4096]{1,0:T(8,128)(2,1)S(1)} collective-permute-done((bf16[64,4096]{1,0:T(8,128)(2,1)S(1)}, bf16[64,4096]{1,0:T(8,128)(2,1)S(1)}, u32[]{:S(2)}, u32[]{:S(2)}) %collective-permute-start.14) | collective-permute-done | bytes 524320 | tf_op jit(solution)/shard_map/ppermute | solution.py:314
  126.5 1.8 shard_map.102.refs_0_
  129.9 5.1 %collective-permute-done.11.refs_1_ = bf16[64,4096]{1,0:T(8,128)(2,1)S(1)} collective-permute-done((bf16[64,4096]{1,0:T(8,128)(2,1)S(1)}, bf16[64,4096]{1,0:T(8,128)(2,1)S(1)}, u32[]{:S(2)}, u32[]{:S(2)}) %collective-permute-start.11) | collective-permute-done | bytes 524320 | tf_op jit(solution)/shard_map/ppermute | solution.py:314
  139.3 1.8 shard_map.88.refs_0_
  141.1 5.2 %collective-permute-done.15.refs_1_ = bf16[64,4096]{1,0:T(8,128)(2,1)S(1)} collective-permute-done((bf16[64,4096]{1,0:T(8,128)(2,1)S(1)}, bf16[64,4096]{1,0:T(8,128)(2,1)S(1)}, u32[]{:S(2)}, u32[]{:S(2)}) %collective-permute-start.15) | collective-permute-done | bytes 524320 | tf_op jit(solution)/shard_map/ppermute | solution.py:314
  149.0 1.8 shard_map.99.refs_0_
  152.3 5.1 %collective-permute-done.12.refs_1_ = bf16[64,4096]{1,0:T(8,128)(2,1)S(1)} collective-permute-done((bf16[64,4096]{1,0:T(8,128)(2,1)S(1)}, bf16[64,4096]{1,0:T(8,128)(2,1)S(1)}, u32[]{:S(2)}, u32[]{:S(2)}) %collective-permute-start.12) | collective-permute-done | bytes 524320 | tf_op jit(solution)/shard_map/ppermute | solution.py:314
  161.7 1.8 shard_map.85.t_ref
  163.5 5.1 %collective-permute-done.16.refs_1_ = bf16[64,4096]{1,0:T(8,128)(2,1)S(1)} collective-permute-done((bf16[64,4096]{1,0:T(8,128)(2,1)S(1)}, bf16[64,4096]{1,0:T(8,128)(2,1)S(1)}, u32[]{:S(2)}, u32[]{:S(2)}) %collective-permute-start.16) | collective-permute-done | bytes 524320 | tf_op jit(solution)/shard_map/ppermute | solution.py:314
  169.6 9.5 %collective-permute-done.13.refs_0_ = bf16[64,4096]{1,0:T(8,128)(2,1)S(1)} collective-permute-done((bf16[64,4096]{1,0:T(8,128)(2,1)S(1)}, bf16[64,4096]{1,0:T(8,128)(2,1)S(1)}, u32[]{:S(2)}, u32[]{:S(2)}) %collective-permute-start.13) | collective-permute-done | bytes 524320 | tf_op jit(solution)/shard_map/ppermute | solution.py:314
  179.7 2.0 %shard_map.108 = bf16[128,4096]{1,0:T(8,128)(2,1)} custom-call(f32[128,4096]{1,0:T(8,128)S(1)} %shard_map.85.t_ref, bf16[64,4096]{1,0:T(8,128)(2,1)S(1)} %collective-permute-done.13.refs_0_, bf16[64,4096]{1,0:T(8,128)(2,1)S(1)} %collective-permute-done.16.refs_1_, bf16[64,4096]{1,0:T(8,128)(2,1)S(1)} %collective-permute-done.21.refs_2_, ...), custom_call_target="tpu_custom_call" | custom-call | tf_op jit(solution)/shard_map/pallas_call | solution.py:135
  (106 shorter events, 53.6 us)
Async XLA Ops:
  0.0 33.1 %copy-start.3 = (s32[16,4]{0,1:T(4,128)S(1)}, s32[16,4]{0,1:T(4,128)}, u32[]{:S(2)}) copy-start(s32[16,4]{0,1:T(4,128)} %param.6) | copy-start | bytes 772
  0.0 33.4 %copy-start.2 = (bf16[4096]{0:T(1024)(128)(2,1)S(1)}, bf16[4096]{0:T(1024)(128)(2,1)}, u32[]{:S(2)}) copy-start(bf16[4096]{0:T(1024)(128)(2,1)} %param.9) | copy-start | bytes 24580
  0.0 31.0 %collective-permute-start.2 = (bf16[128,4096]{1,0:T(8,128)(2,1)}, bf16[128,4096]{1,0:T(8,128)(2,1)S(1)}, u32[]{:S(2)}, u32[]{:S(2)}) collective-permute-start(bf16[128,4096]{1,0:T(8,128)(2,1)} %w_ref.5), channel_id=1, source_target_pairs={{4,0},{8,4},{12,8},{14,12},{10,14},{6,10},{2,6},{0,2},{5,1},{9,5},... | collective-permute-start | bytes 3145736 | tf_op jit(solution)/shard_map/ppermute | solution.py:317
  2.9 28.1 %collective-permute-start.1 = (bf16[128,4096]{1,0:T(8,128)(2,1)}, bf16[128,4096]{1,0:T(8,128)(2,1)S(1)}, u32[]{:S(2)}, u32[]{:S(2)}) collective-permute-start(bf16[128,4096]{1,0:T(8,128)(2,1)} %w_ref.5), channel_id=1, source_target_pairs={{0,4},{4,8},{8,12},{12,14},{14,10},{10,6},{6,2},{2,0},{1,5},{5,9},... | collective-permute-start | bytes 3145736 | tf_op jit(solution)/shard_map/ppermute | solution.py:314
  4.3 26.5 %all-to-all-start = ((bf16[8,1,128]{2,1,0:T(2,128)(2,1)}), bf16[8,1,128]{2,1,0:T(2,128)(2,1)S(1)}, u32[]{:S(2)}, u32[]{:S(2)}) async-start(bf16[8,1,128]{2,1,0:T(2,128)(2,1)} %broadcast_in_dim.27), calls=%async_computation | async-start | bytes 8192 | tf_op jit(solution)/shard_map/all_to_all | solution.py:334
  10.5 22.9 %collective-permute-start = (bf16[128,4096]{1,0:T(8,128)(2,1)}, bf16[128,4096]{1,0:T(8,128)(2,1)}, u32[]{:S(2)}, u32[]{:S(2)}) collective-permute-start(bf16[128,4096]{1,0:T(8,128)(2,1)} %bitcast.40), channel_id=1, source_target_pairs={{0,1},{1,0},{2,3},{3,2},{4,5},{5,4},{6,7},{7,6},{8,9},{9,8},{10,11... | collective-permute-start | bytes 3145736 | tf_op jit(solution)/shard_map/ppermute | solution.py:320
  31.0 23.4 %collective-permute-start.3 = (bf16[128,4096]{1,0:T(8,128)(2,1)S(1)}, bf16[128,4096]{1,0:T(8,128)(2,1)S(1)}, u32[]{:S(2)}, u32[]{:S(2)}) collective-permute-start(bf16[128,4096]{1,0:T(8,128)(2,1)S(1)} %get-tuple-element.31.w_ref), channel_id=1, source_target_pairs={{0,4},{4,8},{8,12},{12,14},{14,10},{10,6},{6,2},{2,0},{1,5},{5,9},... | collective-permute-start | bytes 3145736 | tf_op jit(solution)/shard_map/ppermute | solution.py:314
  31.6 23.2 %collective-permute-start.4 = (bf16[128,4096]{1,0:T(8,128)(2,1)S(1)}, bf16[128,4096]{1,0:T(8,128)(2,1)}, u32[]{:S(2)}, u32[]{:S(2)}) collective-permute-start(bf16[128,4096]{1,0:T(8,128)(2,1)S(1)} %get-tuple-element.29.refs_1_.w_ref), channel_id=1, source_target_pairs={{4,0},{8,4},{12,8},{14,12},{10,14},{6,10},{2,6},{0,2},{5,1},{9,5},... | collective-permute-start | bytes 3145736 | tf_op jit(solution)/shard_map/ppermute | solution.py:317
  33.5 1.2 copy-start.1
  38.7 1.6 copy-start
  54.8 23.0 %collective-permute-start.5 = (bf16[128,4096]{1,0:T(8,128)(2,1)S(1)}, bf16[128,4096]{1,0:T(8,128)(2,1)S(1)}, u32[]{:S(2)}, u32[]{:S(2)}) collective-permute-start(bf16[128,4096]{1,0:T(8,128)(2,1)S(1)} %get-tuple-element.34.w_ref), channel_id=1, source_target_pairs={{0,4},{4,8},{8,12},{12,14},{14,10},{10,6},{6,2},{2,0},{1,5},{5,9},... | collective-permute-start | bytes 3145736 | tf_op jit(solution)/shard_map/ppermute | solution.py:314
  55.4 22.4 %collective-permute-start.6 = (bf16[128,4096]{1,0:T(8,128)(2,1)}, bf16[128,4096]{1,0:T(8,128)(2,1)S(1)}, u32[]{:S(2)}, u32[]{:S(2)}) collective-permute-start(bf16[128,4096]{1,0:T(8,128)(2,1)} %get-tuple-element.35.w_ref), channel_id=1, source_target_pairs={{4,0},{8,4},{12,8},{14,12},{10,14},{6,10},{2,6},{0,2},{5,1},{9,5},... | collective-permute-start | bytes 3145736 | tf_op jit(solution)/shard_map/ppermute | solution.py:317
  77.9 10.4 %collective-permute-start.7 = (bf16[64,4096]{1,0:T(8,128)(2,1)S(1)}, bf16[64,4096]{1,0:T(8,128)(2,1)S(1)}, u32[]{:S(2)}, u32[]{:S(2)}) collective-permute-start(bf16[64,4096]{1,0:T(8,128)(2,1)S(1)} %slice.25), channel_id=1, source_target_pairs={{0,4},{4,8},{8,12},{12,14},{14,10},{10,6},{6,2},{2,0},{1,5},{5,9},... | collective-permute-start | bytes 1572872 | tf_op jit(solution)/shard_map/ppermute | solution.py:314
  79.0 9.8 %collective-permute-start.8 = (bf16[64,4096]{1,0:T(8,128)(2,1)S(1)}, bf16[64,4096]{1,0:T(8,128)(2,1)S(1)}, u32[]{:S(2)}, u32[]{:S(2)}) collective-permute-start(bf16[64,4096]{1,0:T(8,128)(2,1)S(1)} %slice.26), channel_id=1, source_target_pairs={{4,0},{8,4},{12,8},{14,12},{10,14},{6,10},{2,6},{0,2},{5,1},{9,5},... | collective-permute-start | bytes 1572872 | tf_op jit(solution)/shard_map/ppermute | solution.py:317
  90.3 4.2 %collective-permute-start.9 = (bf16[256,4096]{1,0:T(8,128)(2,1)S(1)}, bf16[256,4096]{1,0:T(8,128)(2,1)S(1)}, u32[]{:S(2)}, u32[]{:S(2)}) collective-permute-start(bf16[256,4096]{1,0:T(8,128)(2,1)S(1)} %fusion), channel_id=1, source_target_pairs={{0,1},{1,0},{2,3},{3,2},{4,5},{5,4},{6,7},{7,6},{8,9},{9,8},{10,11... | collective-permute-start | bytes 6291464 | tf_op jit(solution)/shard_map/ppermute | solution.py:320
  97.7 14.8 %collective-permute-start.10 = (bf16[64,4096]{1,0:T(8,128)(2,1)S(1)}, bf16[64,4096]{1,0:T(8,128)(2,1)S(1)}, u32[]{:S(2)}, u32[]{:S(2)}) collective-permute-start(bf16[64,4096]{1,0:T(8,128)(2,1)S(1)} %get-tuple-element.56), channel_id=1, source_target_pairs={{0,4},{4,8},{8,12},{12,14},{14,10},{10,6},{6,2},{2,0},{1,5},{5,9},... | collective-permute-start | bytes 1572872 | tf_op jit(solution)/shard_map/ppermute | solution.py:314
  98.6 15.1 %collective-permute-start.17 = (bf16[64,4096]{1,0:T(8,128)(2,1)S(1)}, bf16[64,4096]{1,0:T(8,128)(2,1)S(1)}, u32[]{:S(2)}, u32[]{:S(2)}) collective-permute-start(bf16[64,4096]{1,0:T(8,128)(2,1)S(1)} %get-tuple-element.55), channel_id=1, source_target_pairs={{4,0},{8,4},{12,8},{14,12},{10,14},{6,10},{2,6},{0,2},{5,1},{9,5},... | collective-permute-start | bytes 1572872 | tf_op jit(solution)/shard_map/ppermute | solution.py:317
  103.3 20.4 %collective-permute-start.14 = (bf16[64,4096]{1,0:T(8,128)(2,1)S(1)}, bf16[64,4096]{1,0:T(8,128)(2,1)S(1)}, u32[]{:S(2)}, u32[]{:S(2)}) collective-permute-start(bf16[64,4096]{1,0:T(8,128)(2,1)S(1)} %shard_map.90), channel_id=1, source_target_pairs={{0,4},{4,8},{8,12},{12,14},{14,10},{10,6},{6,2},{2,0},{1,5},{5,9},... | collective-permute-start | bytes 1572872 | tf_op jit(solution)/shard_map/ppermute | solution.py:314
  108.1 20.3 %collective-permute-start.19 = (bf16[64,4096]{1,0:T(8,128)(2,1)S(1)}, bf16[64,4096]{1,0:T(8,128)(2,1)S(1)}, u32[]{:S(2)}, u32[]{:S(2)}) collective-permute-start(bf16[64,4096]{1,0:T(8,128)(2,1)S(1)} %shard_map.103), channel_id=1, source_target_pairs={{4,0},{8,4},{12,8},{14,12},{10,14},{6,10},{2,6},{0,2},{5,1},{9,5},... | collective-permute-start | bytes 1572872 | tf_op jit(solution)/shard_map/ppermute | solution.py:317
  112.8 22.1 %collective-permute-start.11 = (bf16[64,4096]{1,0:T(8,128)(2,1)S(1)}, bf16[64,4096]{1,0:T(8,128)(2,1)S(1)}, u32[]{:S(2)}, u32[]{:S(2)}) collective-permute-start(bf16[64,4096]{1,0:T(8,128)(2,1)S(1)} %shard_map.81), channel_id=1, source_target_pairs={{0,4},{4,8},{8,12},{12,14},{14,10},{10,6},{6,2},{2,0},{1,5},{5,9},... | collective-permute-start | bytes 1572872 | tf_op jit(solution)/shard_map/ppermute | solution.py:314
  114.1 22.1 %collective-permute-start.18 = (bf16[64,4096]{1,0:T(8,128)(2,1)S(1)}, bf16[64,4096]{1,0:T(8,128)(2,1)S(1)}, u32[]{:S(2)}, u32[]{:S(2)}) collective-permute-start(bf16[64,4096]{1,0:T(8,128)(2,1)S(1)} %shard_map.96), channel_id=1, source_target_pairs={{4,0},{8,4},{12,8},{14,12},{10,14},{6,10},{2,6},{0,2},{5,1},{9,5},... | collective-permute-start | bytes 1572872 | tf_op jit(solution)/shard_map/ppermute | solution.py:317
  124.1 22.1 %collective-permute-start.15 = (bf16[64,4096]{1,0:T(8,128)(2,1)S(1)}, bf16[64,4096]{1,0:T(8,128)(2,1)S(1)}, u32[]{:S(2)}, u32[]{:S(2)}) collective-permute-start(bf16[64,4096]{1,0:T(8,128)(2,1)S(1)} %shard_map.91), channel_id=1, source_target_pairs={{0,4},{4,8},{8,12},{12,14},{14,10},{10,6},{6,2},{2,0},{1,5},{5,9},... | collective-permute-start | bytes 1572872 | tf_op jit(solution)/shard_map/ppermute | solution.py:314
  128.7 22.1 %collective-permute-start.20 = (bf16[64,4096]{1,0:T(8,128)(2,1)S(1)}, bf16[64,4096]{1,0:T(8,128)(2,1)S(1)}, u32[]{:S(2)}, u32[]{:S(2)}) collective-permute-start(bf16[64,4096]{1,0:T(8,128)(2,1)S(1)} %shard_map.104), channel_id=1, source_target_pairs={{4,0},{8,4},{12,8},{14,12},{10,14},{6,10},{2,6},{0,2},{5,1},{9,5},... | collective-permute-start | bytes 1572872 | tf_op jit(solution)/shard_map/ppermute | solution.py:317
  135.3 22.1 %collective-permute-start.12 = (bf16[64,4096]{1,0:T(8,128)(2,1)S(1)}, bf16[64,4096]{1,0:T(8,128)(2,1)S(1)}, u32[]{:S(2)}, u32[]{:S(2)}) collective-permute-start(bf16[64,4096]{1,0:T(8,128)(2,1)S(1)} %shard_map.82), channel_id=1, source_target_pairs={{0,4},{4,8},{8,12},{12,14},{14,10},{10,6},{6,2},{2,0},{1,5},{5,9},... | collective-permute-start | bytes 1572872 | tf_op jit(solution)/shard_map/ppermute | solution.py:314
  136.6 22.1 %collective-permute-start.22 = (bf16[64,4096]{1,0:T(8,128)(2,1)S(1)}, bf16[64,4096]{1,0:T(8,128)(2,1)S(1)}, u32[]{:S(2)}, u32[]{:S(2)}) collective-permute-start(bf16[64,4096]{1,0:T(8,128)(2,1)S(1)} %shard_map.106), channel_id=1, source_target_pairs={{4,0},{8,4},{12,8},{14,12},{10,14},{6,10},{2,6},{0,2},{5,1},{9,5},... | collective-permute-start | bytes 1572872 | tf_op jit(solution)/shard_map/ppermute | solution.py:317
  146.5 22.1 %collective-permute-start.16 = (bf16[64,4096]{1,0:T(8,128)(2,1)S(1)}, bf16[64,4096]{1,0:T(8,128)(2,1)S(1)}, u32[]{:S(2)}, u32[]{:S(2)}) collective-permute-start(bf16[64,4096]{1,0:T(8,128)(2,1)S(1)} %shard_map.92), channel_id=1, source_target_pairs={{0,4},{4,8},{8,12},{12,14},{14,10},{10,6},{6,2},{2,0},{1,5},{5,9},... | collective-permute-start | bytes 1572872 | tf_op jit(solution)/shard_map/ppermute | solution.py:314
  151.2 18.5 %collective-permute-start.21 = (bf16[64,4096]{1,0:T(8,128)(2,1)S(1)}, bf16[64,4096]{1,0:T(8,128)(2,1)S(1)}, u32[]{:S(2)}, u32[]{:S(2)}) collective-permute-start(bf16[64,4096]{1,0:T(8,128)(2,1)S(1)} %shard_map.105), channel_id=1, source_target_pairs={{4,0},{8,4},{12,8},{14,12},{10,14},{6,10},{2,6},{0,2},{5,1},{9,5},... | collective-permute-start | bytes 1572872 | tf_op jit(solution)/shard_map/ppermute | solution.py:317
  157.8 21.4 %collective-permute-start.13 = (bf16[64,4096]{1,0:T(8,128)(2,1)S(1)}, bf16[64,4096]{1,0:T(8,128)(2,1)S(1)}, u32[]{:S(2)}, u32[]{:S(2)}) collective-permute-start(bf16[64,4096]{1,0:T(8,128)(2,1)S(1)} %shard_map.89), channel_id=1, source_target_pairs={{0,4},{4,8},{8,12},{12,14},{14,10},{10,6},{6,2},{2,0},{1,5},{5,9},... | collective-permute-start | bytes 1572872 | tf_op jit(solution)/shard_map/ppermute | solution.py:314
  159.1 20.7 %collective-permute-start.23 = (bf16[64,4096]{1,0:T(8,128)(2,1)S(1)}, bf16[64,4096]{1,0:T(8,128)(2,1)S(1)}, u32[]{:S(2)}, u32[]{:S(2)}) collective-permute-start(bf16[64,4096]{1,0:T(8,128)(2,1)S(1)} %shard_map.107), channel_id=1, source_target_pairs={{4,0},{8,4},{12,8},{14,12},{10,14},{6,10},{2,6},{0,2},{5,1},{9,5},... | collective-permute-start | bytes 1572872 | tf_op jit(solution)/shard_map/ppermute | solution.py:317

commit v5 on v4

--- a/solution.py
+++ b/solution.py
@@ -172,47 +172,60 @@
 
 
 def encode(rows, words, bias, listed, which):
-    count, tile = words.shape[0], rows.shape[1] // TILES
-
-    def kernel(x_ref, w_ref, b_ref, m_ref, c_ref, s_ref, acc):
+    count, tile, n = words[0].shape[0], rows.shape[1] // TILES, len(words)
+
+    def kernel(x_ref, *refs):
+        w_refs, (b_ref, m_ref), outs, acc = refs[:n], refs[n : n + 2], refs[n + 2 : -1], refs[-1]
+
         @pl.when(pl.program_id(0) == 0)
         def _():
-            acc[...] = jnp.broadcast_to(b_ref[which : which + 1, :], acc.shape)
-
-        acc[...] += product(x_ref[...], w_ref[...], ((1,), (1,)))
+            for k, i in enumerate(which):
+                row = jnp.broadcast_to(b_ref[i : i + 1, :], (acc.shape[0], count))
+                acc[:, k * count : (k + 1) * count] = row
+
+        every = jnp.concatenate([w[...] for w in w_refs]) if n > 1 else w_refs[0][...]
+        acc[...] += product(x_ref[...], every, ((1,), (1,)))
 
         @pl.when(pl.program_id(0) == TILES - 1)
         def _():
-            p = acc[...]
-            mask = m_ref[:, which : which + 1] > 0
-            code = jnp.maximum(p, 0.0) + jnp.log1p(jnp.exp(-jnp.abs(p)))
-            c_ref[...] = jnp.where(mask, code, 0.0).astype(c_ref.dtype)
-            s_ref[...] = jnp.where(mask, jax.nn.sigmoid(p), 0.0)
+            for k, i in enumerate(which):
+                p = acc[:, k * count : (k + 1) * count]
+                mask = m_ref[:, i : i + 1] > 0
+                code = jnp.maximum(p, 0.0) + jnp.log1p(jnp.exp(-jnp.abs(p)))
+                outs[2 * k][...] = jnp.where(mask, code, 0.0).astype(jnp.bfloat16)
+                outs[2 * k + 1][...] = jnp.where(mask, jax.nn.sigmoid(p), 0.0)
 
     shape = (rows.shape[0], count)
-    out = [jax.ShapeDtypeStruct(shape, jnp.bfloat16), jax.ShapeDtypeStruct(shape, jnp.float32)]
+    out = [jax.ShapeDtypeStruct(shape, t) for _ in words for t in (jnp.bfloat16, jnp.float32)]
     return local_call(
         kernel,
         (TILES,),
-        [columns(rows, tile), columns(words, tile), whole(bias), whole(listed)],
+        [columns(x, tile) for x in (rows, *words)] + [whole(bias), whole(listed)],
         [whole(o) for o in out],
         out,
-        (rows, words, bias, listed),
-        scratch=[pltpu.VMEM(shape, jnp.float32)],
-    )
-
-
-def decode(codes, words, total):
-    tile = words.shape[1] // TILES
-
-    def kernel(c_ref, w_ref, *rest):
-        part = product(c_ref[...], w_ref[...], ((1,), (0,)))
-        rest[-1][...] = part if len(rest) == 1 else part + rest[0][...]
-
-    out = jax.ShapeDtypeStruct((codes.shape[0], words.shape[1]), jnp.float32)
-    args = (codes, words) if total is None else (codes, words, total)
-    specs = [whole(codes), columns(words, tile)] + [columns(out, tile)] * (len(args) - 2)
-    aliases = {2: 0} if len(args) == 3 else None
+        (rows, *words, bias, listed),
+        scratch=[pltpu.VMEM((shape[0], n * count), jnp.float32)],
+    )
+
+
+def decode(codes, words, total, dtype):
+    n, width = len(words), words[0].shape[1]
+    tile = width // TILES
+
+    def kernel(*refs):
+        part = None
+        for k in range(n):
+            one = product(refs[k][...], refs[n + k][...], ((1,), (0,)))
+            part = one if part is None else part + one
+        rest = refs[2 * n :]
+        part = part if len(rest) == 1 else part + rest[0][...]
+        rest[-1][...] = part.astype(dtype)
+
+    out = jax.ShapeDtypeStruct((codes[0].shape[0], width), dtype)
+    args = (*codes, *words) if total is None else (*codes, *words, total)
+    specs = [whole(c) for c in codes] + [columns(w, tile) for w in words]
+    specs += [columns(out, tile)] * (len(args) - 2 * n)
+    aliases = {2 * n: 0} if total is not None and total.dtype == dtype else None
     return local_call(kernel, (TILES,), specs, columns(out, tile), out, args, aliases)
 
 
@@ -277,22 +290,6 @@
     specs += [columns(out, tile)] * (len(args) - 1)
     cost = (out.size, 8 * out.size)
     return local_call(kernel, (TILES,), specs, columns(out, tile), out, args, cost=cost)
-
-
-def finish(total, ups, downs, scale):
-    width, cut = total.shape[1], total.shape[0] // 2
-    tile = width // TILES
-
-    def kernel(t_ref, *refs):
-        for k in range(2):
-            half = slice(k * cut, (k + 1) * cut)
-            came = refs[k][...].astype(jnp.float32) + refs[2 + k][...].astype(jnp.float32)
-            refs[-1][half, :] = ((t_ref[half, :] + came) / scale).astype(refs[-1].dtype)
-
-    out = jax.ShapeDtypeStruct(total.shape, jnp.bfloat16)
-    args = (total, *ups, *downs)
-    specs = [columns(x, tile) for x in args]
-    return local_call(kernel, (TILES,), specs, columns(out, tile), out, args)
 
 
 def ring_body(activations, act_blocks, dictionary, enc_bias, dec_bias):
@@ -348,26 +345,35 @@
             rows = centre(acts, to_core(acts), shift)
         else:
             words[-t], words[t] = after(arrived, rebuilt)
-        for step in (-t, t) if t > 1 else (0, -t, t):
-            which = steps.index(step)
-            codes[step], sigmas[step] = encode(rows, words[step], biases, listed, which)
-            rebuilt = decode(codes[step], words[step], rebuilt)
+        for group in ((-t, t),) if t > 1 else ((0,), (-t, t)):
+            blocks = [words[step] for step in group]
+            out = encode(rows, blocks, biases, listed, [steps.index(step) for step in group])
+            for k, step in enumerate(group):
+                codes[step], sigmas[step] = out[2 * k : 2 * k + 2]
+            dtype = jnp.bfloat16 if t == half - 1 and group[-1] == t else jnp.float32
+            rebuilt = decode([codes[step] for step in group], blocks, rebuilt, dtype)
+
+    middle = half_blocks * rows_each
+    swapped = to_core(rebuilt)
     last = to_right(words[1 - half][:cut]), to_left(words[half - 1][cut:])
-    words[half] = jnp.concatenate(after(last, rebuilt))
+    last = after(last, rebuilt)
+    words[half] = jnp.concatenate(last)
+    other_words = to_core(words[half])
     preacts = jnp.einsum("rd,ld->rl", rows, words[half], preferred_element_type=jnp.float32)
     preacts = preacts + biases[-1:]
     mask = listed[:, len(steps) - 1 :] > 0
     code = jnp.where(mask, jax.nn.softplus(preacts), 0.0).astype(jnp.bfloat16)
     sigma = jnp.where(mask, jax.nn.sigmoid(preacts), 0.0)
     codes[half], sigmas[half] = lax.optimization_barrier((code, sigma))
-    rebuilt = rebuilt + jnp.einsum(
-        "rl,ld->rd", codes[half], words[half], preferred_element_type=jnp.float32
-    )
-    rebuilt = rebuilt.astype(jnp.bfloat16)
-    swapped = to_core(rebuilt)
-    middle = half_blocks * rows_each
-    swapped = jnp.concatenate([swapped[middle:], swapped[:middle]])
-    errors = rebuilt.astype(jnp.float32) + swapped.astype(jnp.float32) - rows.astype(jnp.float32)
+    other_codes = to_core(codes[half])
+
+    def in_my_order(x):
+        return jnp.concatenate([x[middle:], x[:middle]])
+
+    errors = rebuilt.astype(jnp.float32) + in_my_order(swapped).astype(jnp.float32)
+    errors = errors - rows.astype(jnp.float32)
+    for code, word in ((codes[half], words[half]), (in_my_order(other_codes), other_words)):
+        errors = errors + jnp.einsum("rl,ld->rd", code, word, preferred_element_type=jnp.float32)
     errors = errors.astype(jnp.bfloat16)
 
     def grads_of(step, token):
@@ -390,7 +396,12 @@
         tokens = (up[0], down[1])
         up = tuple(to_right(join(ahead, came, k)) for k, came in enumerate(up))
         down = tuple(to_left(join(behind, came, k)) for k, came in enumerate(down))
-    return finish(grads_of(0, tokens[0]), up, down, block_rows)
+    mine = grads_of(0, tokens[0])
+    parts = []
+    for k in range(2):
+        part = mine[k * cut : (k + 1) * cut] + up[k].astype(jnp.float32) + down[k].astype(jnp.float32)
+        parts.append(part / block_rows)
+    return jnp.concatenate(parts).astype(jnp.bfloat16)
 
 
 def solution(mesh):

time: 182 us -> 179 us (0.984)
  Pallas kernels: 59.1 us -> 49.2 us
  waiting for transfers between devices: 83.1 us -> 88.1 us
    pallas_call x42 -> x35, Pallas kernels: 59.1 us -> 49.2 us  [local_call(): pl.pallas_call(kernel, grid=grid, in_specs=in_specs, out_specs=out_specs,...]
    ppermute x11, waiting for transfers between devices: 56.6 us -> 61.1 us  [to_right(): return lax.ppermute(x, 'lat', right_pairs)]
    ppermute x11, waiting for transfers between devices: 2.41 us -> 6.33 us  [to_left(): return lax.ppermute(x, 'lat', left_pairs)]
    ppermute x2 -> x4, waiting for transfers between devices: 4.15 us -> 0.7 us  [to_core(): return lax.ppermute(x, 'row', [(0, 1), (1, 0)])]
    ppermute x11, starting transfers between devices: 9.25 us -> 6.35 us  [to_right(): return lax.ppermute(x, 'lat', right_pairs)]
    ppermute x11, starting transfers between devices: 15.2 us -> 17.9 us  [to_left(): return lax.ppermute(x, 'lat', left_pairs)]
  transfers between devices with their start and end apart: 25 -> 27, of which waited for: 16 -> 17; matrix products, arithmetic and copies ran while one was open for 1% -> 2% of each run, Pallas kernels for 31% -> 28%
where the time goes in v5:
time: 179 us
  waiting for transfers between devices  88.1 us (49%)
  Pallas kernels  49.2 us (27%)
  starting transfers between devices  31.1 us (17%)
  matrix products  4.57 us (3%)
  local copies, waits for them, and re-layouts  3.4 us (2%)
    ppermute x11, waiting for transfers between devices, to_right(): return lax.ppermute(x, 'lat', right_pairs)  61.1 us
    pallas_call x35, Pallas kernels, local_call(): pl.pallas_call(kernel, grid=grid, in_specs=in_specs, out_specs=out_specs,...  49.2 us
    all_to_all x1, waiting for transfers between devices, ring_body(): lax.all_to_all(biases, 'lat', split_axis=0, concat_axis=0, tiled=True)  20 us
    ppermute x11, starting transfers between devices, to_left(): return lax.ppermute(x, 'lat', left_pairs)  17.9 us
    ppermute x11, starting transfers between devices, to_right(): return lax.ppermute(x, 'lat', right_pairs)  6.35 us
    ppermute x11, waiting for transfers between devices, to_left(): return lax.ppermute(x, 'lat', left_pairs)  6.33 us
    all_to_all x1, starting transfers between devices, ring_body(): lax.all_to_all(biases, 'lat', split_axis=0, concat_axis=0, tiled=True)  6.19 us
  transfers between devices with their start and end apart: 27, of which 17 were waited for; matrix products, arithmetic and copies ran while one was open for 2% of the time, Pallas kernels for 28%

profile of v5, /device:TPU:0, one launch (start us, length us, event | category | flops | bytes accessed | tf_op | source)
XLA Modules:
  0.0 178.9 jit_solution(13398827254686815253)
XLA Ops:
  0.0 2.9 %collective-permute-start.2 = (bf16[128,4096]{1,0:T(8,128)(2,1)}, bf16[128,4096]{1,0:T(8,128)(2,1)S(1)}, u32[]{:S(2)}, u32[]{:S(2)}) collective-permute-start(bf16[128,4096]{1,0:T(8,128)(2,1)} %w_ref.1), channel_id=1, source_target_pairs={{4,0},{8,4},{12,8},{14,12},{10,14},{6,10},{2,6},{0,2},{5,1},{9,5},... | collective-permute-start | bytes 3145736 | tf_op jit(solution)/shard_map/ppermute | solution.py:314
  4.3 6.2 %all-to-all-start = ((bf16[8,1,128]{2,1,0:T(2,128)(2,1)}), bf16[8,1,128]{2,1,0:T(2,128)(2,1)S(1)}, u32[]{:S(2)}, u32[]{:S(2)}) async-start(bf16[8,1,128]{2,1,0:T(2,128)(2,1)} %broadcast_in_dim.27), calls=%async_computation | async-start | bytes 8192 | tf_op jit(solution)/shard_map/all_to_all | solution.py:331
  10.8 20.0 %all-to-all-done = bf16[8,1,128]{2,1,0:T(2,128)(2,1)S(1)} async-done(((bf16[8,1,128]{2,1,0:T(2,128)(2,1)}), bf16[8,1,128]{2,1,0:T(2,128)(2,1)S(1)}, u32[]{:S(2)}, u32[]{:S(2)}) %all-to-all-start) | async-done | bytes 2080 | tf_op jit(solution)/shard_map/all_to_all | solution.py:331
  34.8 2.4 %shard_map.57.x_ref = bf16[256,4096]{1,0:T(8,128)(2,1)S(1)} custom-call(bf16[128,4096]{1,0:T(8,128)(2,1)S(1)} %bitcast.39, bf16[128,4096]{1,0:T(8,128)(2,1)} %collective-permute-done.y_ref, bf16[1,4096]{1,0:T(2,128)(2,1)S(1)} %shard_map.56.b_ref), custom_call_target="tpu_custom_call" | custom-call | tf_op jit(solution)/shard_map/pallas_call | solution.py:135
  37.2 1.6 shard_map.58
  38.8 2.0 %shard_map.59 = (bf16[256,128]{1,0:T(8,128)(2,1)S(1)}, f32[256,128]{1,0:T(8,128)S(1)}, bf16[256,128]{1,0:T(8,128)(2,1)S(1)}, f32[256,128]{1,0:T(8,128)S(1)}) custom-call(bf16[256,4096]{1,0:T(8,128)(2,1)S(1)} %shard_map.57.x_ref, bf16[128,4096]{1,0:T(8,128)(2,1)S(1)} %get-tuple-element.31.refs_0_.refs_2_.w_ref, ...), custom_call_target="tpu_custom_call" | custom-call | tf_op jit(solution)/shard_map/pallas_call | solution.py:135
  42.3 2.4 %shard_map.61.refs_2_.refs_4_ = f32[256,4096]{1,0:T(8,128)S(1)} custom-call(bf16[256,128]{1,0:T(8,128)(2,1)S(1)} %get-tuple-element.32.refs_0_.c_ref, bf16[256,128]{1,0:T(8,128)(2,1)S(1)} %get-tuple-element.33.refs_1_.c_ref, bf16[128,4096]{1,0:T(8,128)(2,1)S(1)} %get-tuple-element.31.refs_0_.refs_2_.w_ref, ...), custom_call_target="tpu_custom_call", output_to_operand_aliasing={{}: (4, {})} | custom-call | tf_op jit(solution)/shard_map/pallas_call | solution.py:135
  44.7 9.7 %collective-permute-done.3.refs_0_ = bf16[128,4096]{1,0:T(8,128)(2,1)S(1)} collective-permute-done((bf16[128,4096]{1,0:T(8,128)(2,1)S(1)}, bf16[128,4096]{1,0:T(8,128)(2,1)S(1)}, u32[]{:S(2)}, u32[]{:S(2)}) %collective-permute-start.3) | collective-permute-done | bytes 1048608 | tf_op jit(solution)/shard_map/ppermute | solution.py:311
  56.8 3.4 %shard_map.63 = (bf16[256,128]{1,0:T(8,128)(2,1)S(1)}, f32[256,128]{1,0:T(8,128)S(1)}, bf16[256,128]{1,0:T(8,128)(2,1)S(1)}, f32[256,128]{1,0:T(8,128)S(1)}) custom-call(bf16[256,4096]{1,0:T(8,128)(2,1)S(1)} %shard_map.57.x_ref, bf16[128,4096]{1,0:T(8,128)(2,1)S(1)} %get-tuple-element.34.refs_0_.refs_2_.w_ref, ...), custom_call_target="tpu_custom_call" | custom-call | tf_op jit(solution)/shard_map/pallas_call | solution.py:135
  60.2 3.5 %shard_map.64.refs_2_.refs_4_ = f32[256,4096]{1,0:T(8,128)S(1)} custom-call(bf16[256,128]{1,0:T(8,128)(2,1)S(1)} %get-tuple-element.36.refs_0_.c_ref, bf16[256,128]{1,0:T(8,128)(2,1)S(1)} %get-tuple-element.37.refs_1_.c_ref, bf16[128,4096]{1,0:T(8,128)(2,1)S(1)} %get-tuple-element.34.refs_0_.refs_2_.w_ref, ...), custom_call_target="tpu_custom_call", output_to_operand_aliasing={{}: (4, {})} | custom-call | tf_op jit(solution)/shard_map/pallas_call | solution.py:135
  63.8 13.3 %collective-permute-done.5.refs_0_ = bf16[128,4096]{1,0:T(8,128)(2,1)S(1)} collective-permute-done((bf16[128,4096]{1,0:T(8,128)(2,1)S(1)}, bf16[128,4096]{1,0:T(8,128)(2,1)S(1)}, u32[]{:S(2)}, u32[]{:S(2)}) %collective-permute-start.5) | collective-permute-done | bytes 1048608 | tf_op jit(solution)/shard_map/ppermute | solution.py:311
  77.0 1.7 collective-permute-done.6.refs_1_
  81.0 1.9 %shard_map.66 = (bf16[256,128]{1,0:T(8,128)(2,1)S(1)}, f32[256,128]{1,0:T(8,128)S(1)}, bf16[256,128]{1,0:T(8,128)(2,1)S(1)}, f32[256,128]{1,0:T(8,128)S(1)}) custom-call(bf16[256,4096]{1,0:T(8,128)(2,1)S(1)} %shard_map.57.x_ref, bf16[128,4096]{1,0:T(8,128)(2,1)S(1)} %get-tuple-element.38.refs_0_.refs_2_.w_ref, ...), custom_call_target="tpu_custom_call" | custom-call | tf_op jit(solution)/shard_map/pallas_call | solution.py:135
  82.9 2.3 %shard_map.67.refs_2_ = bf16[256,4096]{1,0:T(8,128)(2,1)S(1)} custom-call(bf16[256,128]{1,0:T(8,128)(2,1)S(1)} %get-tuple-element.40.refs_0_.c_ref, bf16[256,128]{1,0:T(8,128)(2,1)S(1)} %get-tuple-element.41.refs_1_.c_ref, bf16[128,4096]{1,0:T(8,128)(2,1)S(1)} %get-tuple-element.38.refs_0_.refs_2_.w_ref, ...), custom_call_target="tpu_custom_call" | custom-call | tf_op jit(solution)/shard_map/pallas_call | solution.py:135
  85.5 3.3 %collective-permute-done.9.refs_1_ = bf16[64,4096]{1,0:T(8,128)(2,1)S(1)} collective-permute-done((bf16[64,4096]{1,0:T(8,128)(2,1)S(1)}, bf16[64,4096]{1,0:T(8,128)(2,1)S(1)}, u32[]{:S(2)}, u32[]{:S(2)}) %collective-permute-start.9) | collective-permute-done | bytes 524320 | tf_op jit(solution)/shard_map/ppermute | solution.py:314
  99.3 1.8 %shard_map.74.refs_0_ = f32[128,4096]{1,0:T(8,128)S(1)} custom-call(bf16[256,128]{1,0:T(8,128)(2,1)S(1)} %get-tuple-element.41.refs_1_.c_ref, bf16[256,128]{1,0:T(8,128)(2,1)S(1)} %shard_map.73.s_ref, bf16[256,4096]{1,0:T(8,128)(2,1)S(1)} %add_convert_fusion.e_ref, bf16[256,4096]{1,0:T(8,128)(2,1)S(1)} %shard_map.57.x_ref), custom_call_target="tpu_custom_call" | custom-call | flops 536870912 | bytes 6291456 | tf_op jit(solution)/shard_map/pallas_call | solution.py:135
  103.5 1.8 %shard_map.86.refs_0_ = f32[128,4096]{1,0:T(8,128)S(1)} custom-call(bf16[256,128]{1,0:T(8,128)(2,1)S(1)} %get-tuple-element.40.refs_0_.c_ref, bf16[256,128]{1,0:T(8,128)(2,1)S(1)} %shard_map.85.s_ref, bf16[256,4096]{1,0:T(8,128)(2,1)S(1)} %add_convert_fusion.e_ref, bf16[256,4096]{1,0:T(8,128)(2,1)S(1)} %shard_map.57.x_ref), custom_call_target="tpu_custom_call" | custom-call | flops 536870912 | bytes 6291456 | tf_op jit(solution)/shard_map/pallas_call | solution.py:135
  107.1 3.5 %collective-permute-done.12.refs_1_ = bf16[64,4096]{1,0:T(8,128)(2,1)S(1)} collective-permute-done((bf16[64,4096]{1,0:T(8,128)(2,1)S(1)}, bf16[64,4096]{1,0:T(8,128)(2,1)S(1)}, u32[]{:S(2)}, u32[]{:S(2)}) %collective-permute-start.12) | collective-permute-done | bytes 524320 | tf_op jit(solution)/shard_map/ppermute | solution.py:311
  111.8 1.7 collective-permute-start.17
  113.5 3.0 %shard_map.70.s_ref = bf16[256,128]{1,0:T(8,128)(2,1)S(1)} custom-call(bf16[256,4096]{1,0:T(8,128)(2,1)S(1)} %add_convert_fusion.e_ref, bf16[128,4096]{1,0:T(8,128)(2,1)} %get-tuple-element.35.refs_1_.refs_3_.w_ref, f32[256,128]{1,0:T(8,128)S(1)} %shard_map.69.s_ref), custom_call_target="tpu_custom_call" | custom-call | flops 268435456 | bytes 3145728 | tf_op jit(solution)/shard_map/pallas_call | solution.py:135
  116.5 1.8 %shard_map.71.refs_0_ = f32[128,4096]{1,0:T(8,128)S(1)} custom-call(bf16[256,128]{1,0:T(8,128)(2,1)S(1)} %get-tuple-element.37.refs_1_.c_ref, bf16[256,128]{1,0:T(8,128)(2,1)S(1)} %shard_map.70.s_ref, bf16[256,4096]{1,0:T(8,128)(2,1)S(1)} %add_convert_fusion.e_ref, bf16[256,4096]{1,0:T(8,128)(2,1)S(1)} %shard_map.57.x_ref), custom_call_target="tpu_custom_call" | custom-call | flops 536870912 | bytes 6291456 | tf_op jit(solution)/shard_map/pallas_call | solution.py:135
  118.3 3.5 %collective-permute-done.21.refs_1_ = bf16[64,4096]{1,0:T(8,128)(2,1)S(1)} collective-permute-done((bf16[64,4096]{1,0:T(8,128)(2,1)S(1)}, bf16[64,4096]{1,0:T(8,128)(2,1)S(1)}, u32[]{:S(2)}, u32[]{:S(2)}) %collective-permute-start.21) | collective-permute-done | bytes 524320 | tf_op jit(solution)/shard_map/ppermute | solution.py:311
  124.2 1.8 %shard_map.93.refs_0_ = f32[128,4096]{1,0:T(8,128)S(1)} custom-call(bf16[256,128]{1,0:T(8,128)(2,1)S(1)} %get-tuple-element.36.refs_0_.c_ref, bf16[256,128]{1,0:T(8,128)(2,1)S(1)} %shard_map.92.s_ref, bf16[256,4096]{1,0:T(8,128)(2,1)S(1)} %add_convert_fusion.e_ref, bf16[256,4096]{1,0:T(8,128)(2,1)S(1)} %shard_map.57.x_ref), custom_call_target="tpu_custom_call" | custom-call | flops 536870912 | bytes 6291456 | tf_op jit(solution)/shard_map/pallas_call | solution.py:135
  127.9 5.1 %collective-permute-done.13.refs_1_ = bf16[64,4096]{1,0:T(8,128)(2,1)S(1)} collective-permute-done((bf16[64,4096]{1,0:T(8,128)(2,1)S(1)}, bf16[64,4096]{1,0:T(8,128)(2,1)S(1)}, u32[]{:S(2)}, u32[]{:S(2)}) %collective-permute-start.13) | collective-permute-done | bytes 524320 | tf_op jit(solution)/shard_map/ppermute | solution.py:311
  135.8 1.5 shard_map.81.s_ref
  137.3 1.8 %shard_map.82.refs_0_ = f32[128,4096]{1,0:T(8,128)S(1)} custom-call(bf16[256,128]{1,0:T(8,128)(2,1)S(1)} %get-tuple-element.33.refs_1_.c_ref, bf16[256,128]{1,0:T(8,128)(2,1)S(1)} %shard_map.81.s_ref, bf16[256,4096]{1,0:T(8,128)(2,1)S(1)} %add_convert_fusion.e_ref, bf16[256,4096]{1,0:T(8,128)(2,1)S(1)} %shard_map.57.x_ref), custom_call_target="tpu_custom_call" | custom-call | flops 536870912 | bytes 6291456 | tf_op jit(solution)/shard_map/pallas_call | solution.py:135
  139.1 5.1 %collective-permute-done.22.refs_1_ = bf16[64,4096]{1,0:T(8,128)(2,1)S(1)} collective-permute-done((bf16[64,4096]{1,0:T(8,128)(2,1)S(1)}, bf16[64,4096]{1,0:T(8,128)(2,1)S(1)}, u32[]{:S(2)}, u32[]{:S(2)}) %collective-permute-start.22) | collective-permute-done | bytes 524320 | tf_op jit(solution)/shard_map/ppermute | solution.py:311
  146.7 1.8 %shard_map.90.refs_0_ = f32[128,4096]{1,0:T(8,128)S(1)} custom-call(bf16[256,128]{1,0:T(8,128)(2,1)S(1)} %get-tuple-element.32.refs_0_.c_ref, bf16[256,128]{1,0:T(8,128)(2,1)S(1)} %shard_map.89.s_ref, bf16[256,4096]{1,0:T(8,128)(2,1)S(1)} %add_convert_fusion.e_ref, bf16[256,4096]{1,0:T(8,128)(2,1)S(1)} %shard_map.57.x_ref), custom_call_target="tpu_custom_call" | custom-call | flops 536870912 | bytes 6291456 | tf_op jit(solution)/shard_map/pallas_call | solution.py:135
  150.3 5.1 %collective-permute-done.14.refs_1_ = bf16[64,4096]{1,0:T(8,128)(2,1)S(1)} collective-permute-done((bf16[64,4096]{1,0:T(8,128)(2,1)S(1)}, bf16[64,4096]{1,0:T(8,128)(2,1)S(1)}, u32[]{:S(2)}, u32[]{:S(2)}) %collective-permute-start.14) | collective-permute-done | bytes 524320 | tf_op jit(solution)/shard_map/ppermute | solution.py:311
  159.8 1.8 %shard_map.79 = f32[128,4096]{1,0:T(8,128)S(1)} custom-call(bf16[256,128]{1,0:T(8,128)(2,1)S(1)} %get-tuple-element.30.refs_0_.c_ref, bf16[256,128]{1,0:T(8,128)(2,1)S(1)} %shard_map.78.s_ref, bf16[256,4096]{1,0:T(8,128)(2,1)S(1)} %add_convert_fusion.e_ref, bf16[256,4096]{1,0:T(8,128)(2,1)S(1)} %shard_map.57.x_ref), custom_call_target="tpu_custom_call" | custom-call | flops 536870912 | bytes 6291456 | tf_op jit(solution)/shard_map/pallas_call | solution.py:135
  161.6 5.2 %collective-permute-done.23 = bf16[64,4096]{1,0:T(8,128)(2,1)S(1)} collective-permute-done((bf16[64,4096]{1,0:T(8,128)(2,1)S(1)}, bf16[64,4096]{1,0:T(8,128)(2,1)S(1)}, u32[]{:S(2)}, u32[]{:S(2)}) %collective-permute-start.23) | collective-permute-done | bytes 524320 | tf_op jit(solution)/shard_map/ppermute | solution.py:311
  167.3 9.8 %collective-permute-done.15 = bf16[64,4096]{1,0:T(8,128)(2,1)S(1)} collective-permute-done((bf16[64,4096]{1,0:T(8,128)(2,1)S(1)}, bf16[64,4096]{1,0:T(8,128)(2,1)S(1)}, u32[]{:S(2)}, u32[]{:S(2)}) %collective-permute-start.15) | collective-permute-done | bytes 524320 | tf_op jit(solution)/shard_map/ppermute | solution.py:311
  (106 shorter events, 45.5 us)
Async XLA Ops:
  0.0 33.1 %copy-start.3 = (s32[16,4]{0,1:T(4,128)S(1)}, s32[16,4]{0,1:T(4,128)}, u32[]{:S(2)}) copy-start(s32[16,4]{0,1:T(4,128)} %param.6) | copy-start | bytes 772
  0.0 33.4 %copy-start.2 = (bf16[4096]{0:T(1024)(128)(2,1)S(1)}, bf16[4096]{0:T(1024)(128)(2,1)}, u32[]{:S(2)}) copy-start(bf16[4096]{0:T(1024)(128)(2,1)} %param.9) | copy-start | bytes 24580
  0.0 31.0 %collective-permute-start.2 = (bf16[128,4096]{1,0:T(8,128)(2,1)}, bf16[128,4096]{1,0:T(8,128)(2,1)S(1)}, u32[]{:S(2)}, u32[]{:S(2)}) collective-permute-start(bf16[128,4096]{1,0:T(8,128)(2,1)} %w_ref.1), channel_id=1, source_target_pairs={{4,0},{8,4},{12,8},{14,12},{10,14},{6,10},{2,6},{0,2},{5,1},{9,5},... | collective-permute-start | bytes 3145736 | tf_op jit(solution)/shard_map/ppermute | solution.py:314
  2.9 28.1 %collective-permute-start.1 = (bf16[128,4096]{1,0:T(8,128)(2,1)}, bf16[128,4096]{1,0:T(8,128)(2,1)S(1)}, u32[]{:S(2)}, u32[]{:S(2)}) collective-permute-start(bf16[128,4096]{1,0:T(8,128)(2,1)} %w_ref.1), channel_id=1, source_target_pairs={{0,4},{4,8},{8,12},{12,14},{14,10},{10,6},{6,2},{2,0},{1,5},{5,9},... | collective-permute-start | bytes 3145736 | tf_op jit(solution)/shard_map/ppermute | solution.py:311
  4.3 26.5 %all-to-all-start = ((bf16[8,1,128]{2,1,0:T(2,128)(2,1)}), bf16[8,1,128]{2,1,0:T(2,128)(2,1)S(1)}, u32[]{:S(2)}, u32[]{:S(2)}) async-start(bf16[8,1,128]{2,1,0:T(2,128)(2,1)} %broadcast_in_dim.27), calls=%async_computation | async-start | bytes 8192 | tf_op jit(solution)/shard_map/all_to_all | solution.py:331
  10.5 22.9 %collective-permute-start = (bf16[128,4096]{1,0:T(8,128)(2,1)}, bf16[128,4096]{1,0:T(8,128)(2,1)}, u32[]{:S(2)}, u32[]{:S(2)}) collective-permute-start(bf16[128,4096]{1,0:T(8,128)(2,1)} %bitcast.38), channel_id=1, source_target_pairs={{0,1},{1,0},{2,3},{3,2},{4,5},{5,4},{6,7},{7,6},{8,9},{9,8},{10,11... | collective-permute-start | bytes 3145736 | tf_op jit(solution)/shard_map/ppermute | solution.py:317
  31.0 23.4 %collective-permute-start.3 = (bf16[128,4096]{1,0:T(8,128)(2,1)S(1)}, bf16[128,4096]{1,0:T(8,128)(2,1)S(1)}, u32[]{:S(2)}, u32[]{:S(2)}) collective-permute-start(bf16[128,4096]{1,0:T(8,128)(2,1)S(1)} %get-tuple-element.31.refs_0_.refs_2_.w_ref), channel_id=1, source_target_pairs={{0,4},{4,8},{8,12},{12,14},{14,10},{10,6},{6,2},{2,0},{1,5},{5,9},... | collective-permute-start | bytes 3145736 | tf_op jit(solution)/shard_map/ppermute | solution.py:311
  31.6 23.2 %collective-permute-start.4 = (bf16[128,4096]{1,0:T(8,128)(2,1)S(1)}, bf16[128,4096]{1,0:T(8,128)(2,1)}, u32[]{:S(2)}, u32[]{:S(2)}) collective-permute-start(bf16[128,4096]{1,0:T(8,128)(2,1)S(1)} %get-tuple-element.29.refs_1_.refs_3_.w_ref), channel_id=1, source_target_pairs={{4,0},{8,4},{12,8},{14,12},{10,14},{6,10},{2,6},{0,2},{5,1},{9,5},... | collective-permute-start | bytes 3145736 | tf_op jit(solution)/shard_map/ppermute | solution.py:314
  33.5 3.7 %copy-start = (bf16[128,4096]{1,0:T(8,128)(2,1)S(1)}, bf16[128,4096]{1,0:T(8,128)(2,1)}, u32[]{:S(2)}) copy-start(bf16[128,4096]{1,0:T(8,128)(2,1)} %w_ref.1) | copy-start | bytes 3145732
  33.5 1.3 copy-start.1
  54.8 22.2 %collective-permute-start.5 = (bf16[128,4096]{1,0:T(8,128)(2,1)S(1)}, bf16[128,4096]{1,0:T(8,128)(2,1)S(1)}, u32[]{:S(2)}, u32[]{:S(2)}) collective-permute-start(bf16[128,4096]{1,0:T(8,128)(2,1)S(1)} %get-tuple-element.34.refs_0_.refs_2_.w_ref), channel_id=1, source_target_pairs={{0,4},{4,8},{8,12},{12,14},{14,10},{10,6},{6,2},{2,0},{1,5},{5,9},... | collective-permute-start | bytes 3145736 | tf_op jit(solution)/shard_map/ppermute | solution.py:311
  55.4 23.4 %collective-permute-start.6 = (bf16[128,4096]{1,0:T(8,128)(2,1)}, bf16[128,4096]{1,0:T(8,128)(2,1)S(1)}, u32[]{:S(2)}, u32[]{:S(2)}) collective-permute-start(bf16[128,4096]{1,0:T(8,128)(2,1)} %get-tuple-element.35.refs_1_.refs_3_.w_ref), channel_id=1, source_target_pairs={{4,0},{8,4},{12,8},{14,12},{10,14},{6,10},{2,6},{0,2},{5,1},{9,5},... | collective-permute-start | bytes 3145736 | tf_op jit(solution)/shard_map/ppermute | solution.py:314
  78.9 9.9 %collective-permute-start.9 = (bf16[64,4096]{1,0:T(8,128)(2,1)S(1)}, bf16[64,4096]{1,0:T(8,128)(2,1)S(1)}, u32[]{:S(2)}, u32[]{:S(2)}) collective-permute-start(bf16[64,4096]{1,0:T(8,128)(2,1)S(1)} %slice.40), channel_id=1, source_target_pairs={{4,0},{8,4},{12,8},{14,12},{10,14},{6,10},{2,6},{0,2},{5,1},{9,5},... | collective-permute-start | bytes 1572872 | tf_op jit(solution)/shard_map/ppermute | solution.py:314
  80.4 9.2 %collective-permute-start.8 = (bf16[64,4096]{1,0:T(8,128)(2,1)S(1)}, bf16[64,4096]{1,0:T(8,128)(2,1)S(1)}, u32[]{:S(2)}, u32[]{:S(2)}) collective-permute-start(bf16[64,4096]{1,0:T(8,128)(2,1)S(1)} %slice.39), channel_id=1, source_target_pairs={{0,4},{4,8},{8,12},{12,14},{14,10},{10,6},{6,2},{2,0},{1,5},{5,9},... | collective-permute-start | bytes 1572872 | tf_op jit(solution)/shard_map/ppermute | solution.py:311
  85.2 7.3 %collective-permute-start.7 = (bf16[256,4096]{1,0:T(8,128)(2,1)S(1)}, bf16[256,4096]{1,0:T(8,128)(2,1)S(1)}, u32[]{:S(2)}, u32[]{:S(2)}) collective-permute-start(bf16[256,4096]{1,0:T(8,128)(2,1)S(1)} %shard_map.67.refs_2_), channel_id=1, source_target_pairs={{0,1},{1,0},{2,3},{3,2},{4,5},{5,4},{6,7},{7,6},{8,9},{9,8},{10,11... | collective-permute-start | bytes 6291464 | tf_op jit(solution)/shard_map/ppermute | solution.py:317
  89.6 3.1 %collective-permute-start.11 = (bf16[128,4096]{1,0:T(8,128)(2,1)S(1)}, bf16[128,4096]{1,0:T(8,128)(2,1)S(1)}, u32[]{:S(2)}, u32[]{:S(2)}) collective-permute-start(bf16[128,4096]{1,0:T(8,128)(2,1)S(1)} %constant_dynamic-update-slice_fusion), channel_id=1, source_target_pairs={{0,1},{1,0},{2,3},{3,2},{4,5},{5,4},{6,7},{7,6},{8,9},{9,8},{10,11... | collective-permute-start | bytes 3145736 | tf_op jit(solution)/shard_map/ppermute | solution.py:317
  90.5 1.9 %collective-permute-start.10 = (bf16[256,128]{1,0:T(8,128)(2,1)S(1)}, bf16[256,128]{1,0:T(8,128)(2,1)S(1)}, u32[]{:S(2)}, u32[]{:S(2)}) collective-permute-start(bf16[256,128]{1,0:T(8,128)(2,1)S(1)} %get-tuple-element.44), channel_id=1, source_target_pairs={{0,1},{1,0},{2,3},{3,2},{4,5},{5,4},{6,7},{7,6},{8,9},{9,8},{10,11... | collective-permute-start | bytes 196616 | tf_op jit(solution)/shard_map/ppermute | solution.py:317
  95.7 14.8 %collective-permute-start.12 = (bf16[64,4096]{1,0:T(8,128)(2,1)S(1)}, bf16[64,4096]{1,0:T(8,128)(2,1)S(1)}, u32[]{:S(2)}, u32[]{:S(2)}) collective-permute-start(bf16[64,4096]{1,0:T(8,128)(2,1)S(1)} %get-tuple-element.58), channel_id=1, source_target_pairs={{0,4},{4,8},{8,12},{12,14},{14,10},{10,6},{6,2},{2,0},{1,5},{5,9},... | collective-permute-start | bytes 1572872 | tf_op jit(solution)/shard_map/ppermute | solution.py:311
  96.3 15.1 %collective-permute-start.16 = (bf16[64,4096]{1,0:T(8,128)(2,1)S(1)}, bf16[64,4096]{1,0:T(8,128)(2,1)S(1)}, u32[]{:S(2)}, u32[]{:S(2)}) collective-permute-start(bf16[64,4096]{1,0:T(8,128)(2,1)S(1)} %get-tuple-element.57), channel_id=1, source_target_pairs={{4,0},{8,4},{12,8},{14,12},{10,14},{6,10},{2,6},{0,2},{5,1},{9,5},... | collective-permute-start | bytes 1572872 | tf_op jit(solution)/shard_map/ppermute | solution.py:314
  101.4 20.4 %collective-permute-start.21 = (bf16[64,4096]{1,0:T(8,128)(2,1)S(1)}, bf16[64,4096]{1,0:T(8,128)(2,1)S(1)}, u32[]{:S(2)}, u32[]{:S(2)}) collective-permute-start(bf16[64,4096]{1,0:T(8,128)(2,1)S(1)} %shard_map.97), channel_id=1, source_target_pairs={{0,4},{4,8},{8,12},{12,14},{14,10},{10,6},{6,2},{2,0},{1,5},{5,9},... | collective-permute-start | bytes 1572872 | tf_op jit(solution)/shard_map/ppermute | solution.py:311
  105.6 20.4 %collective-permute-start.18 = (bf16[64,4096]{1,0:T(8,128)(2,1)S(1)}, bf16[64,4096]{1,0:T(8,128)(2,1)S(1)}, u32[]{:S(2)}, u32[]{:S(2)}) collective-permute-start(bf16[64,4096]{1,0:T(8,128)(2,1)S(1)} %shard_map.94), channel_id=1, source_target_pairs={{4,0},{8,4},{12,8},{14,12},{10,14},{6,10},{2,6},{0,2},{5,1},{9,5},... | collective-permute-start | bytes 1572872 | tf_op jit(solution)/shard_map/ppermute | solution.py:314
  110.9 22.1 %collective-permute-start.13 = (bf16[64,4096]{1,0:T(8,128)(2,1)S(1)}, bf16[64,4096]{1,0:T(8,128)(2,1)S(1)}, u32[]{:S(2)}, u32[]{:S(2)}) collective-permute-start(bf16[64,4096]{1,0:T(8,128)(2,1)S(1)} %shard_map.75), channel_id=1, source_target_pairs={{0,4},{4,8},{8,12},{12,14},{14,10},{10,6},{6,2},{2,0},{1,5},{5,9},... | collective-permute-start | bytes 1572872 | tf_op jit(solution)/shard_map/ppermute | solution.py:311
  111.8 22.1 %collective-permute-start.17 = (bf16[64,4096]{1,0:T(8,128)(2,1)S(1)}, bf16[64,4096]{1,0:T(8,128)(2,1)S(1)}, u32[]{:S(2)}, u32[]{:S(2)}) collective-permute-start(bf16[64,4096]{1,0:T(8,128)(2,1)S(1)} %shard_map.87), channel_id=1, source_target_pairs={{4,0},{8,4},{12,8},{14,12},{10,14},{6,10},{2,6},{0,2},{5,1},{9,5},... | collective-permute-start | bytes 1572872 | tf_op jit(solution)/shard_map/ppermute | solution.py:314
  122.1 22.1 %collective-permute-start.22 = (bf16[64,4096]{1,0:T(8,128)(2,1)S(1)}, bf16[64,4096]{1,0:T(8,128)(2,1)S(1)}, u32[]{:S(2)}, u32[]{:S(2)}) collective-permute-start(bf16[64,4096]{1,0:T(8,128)(2,1)S(1)} %shard_map.98), channel_id=1, source_target_pairs={{0,4},{4,8},{8,12},{12,14},{14,10},{10,6},{6,2},{2,0},{1,5},{5,9},... | collective-permute-start | bytes 1572872 | tf_op jit(solution)/shard_map/ppermute | solution.py:311
  126.4 22.1 %collective-permute-start.19 = (bf16[64,4096]{1,0:T(8,128)(2,1)S(1)}, bf16[64,4096]{1,0:T(8,128)(2,1)S(1)}, u32[]{:S(2)}, u32[]{:S(2)}) collective-permute-start(bf16[64,4096]{1,0:T(8,128)(2,1)S(1)} %shard_map.95), channel_id=1, source_target_pairs={{4,0},{8,4},{12,8},{14,12},{10,14},{6,10},{2,6},{0,2},{5,1},{9,5},... | collective-permute-start | bytes 1572872 | tf_op jit(solution)/shard_map/ppermute | solution.py:314
  133.3 22.1 %collective-permute-start.14 = (bf16[64,4096]{1,0:T(8,128)(2,1)S(1)}, bf16[64,4096]{1,0:T(8,128)(2,1)S(1)}, u32[]{:S(2)}, u32[]{:S(2)}) collective-permute-start(bf16[64,4096]{1,0:T(8,128)(2,1)S(1)} %shard_map.76), channel_id=1, source_target_pairs={{0,4},{4,8},{8,12},{12,14},{14,10},{10,6},{6,2},{2,0},{1,5},{5,9},... | collective-permute-start | bytes 1572872 | tf_op jit(solution)/shard_map/ppermute | solution.py:311
  134.3 22.1 %collective-permute-start.24 = (bf16[64,4096]{1,0:T(8,128)(2,1)S(1)}, bf16[64,4096]{1,0:T(8,128)(2,1)S(1)}, u32[]{:S(2)}, u32[]{:S(2)}) collective-permute-start(bf16[64,4096]{1,0:T(8,128)(2,1)S(1)} %shard_map.100), channel_id=1, source_target_pairs={{4,0},{8,4},{12,8},{14,12},{10,14},{6,10},{2,6},{0,2},{5,1},{9,5},... | collective-permute-start | bytes 1572872 | tf_op jit(solution)/shard_map/ppermute | solution.py:314
  144.6 22.1 %collective-permute-start.23 = (bf16[64,4096]{1,0:T(8,128)(2,1)S(1)}, bf16[64,4096]{1,0:T(8,128)(2,1)S(1)}, u32[]{:S(2)}, u32[]{:S(2)}) collective-permute-start(bf16[64,4096]{1,0:T(8,128)(2,1)S(1)} %shard_map.99), channel_id=1, source_target_pairs={{0,4},{4,8},{8,12},{12,14},{14,10},{10,6},{6,2},{2,0},{1,5},{5,9},... | collective-permute-start | bytes 1572872 | tf_op jit(solution)/shard_map/ppermute | solution.py:311
  148.8 18.5 %collective-permute-start.20 = (bf16[64,4096]{1,0:T(8,128)(2,1)S(1)}, bf16[64,4096]{1,0:T(8,128)(2,1)S(1)}, u32[]{:S(2)}, u32[]{:S(2)}) collective-permute-start(bf16[64,4096]{1,0:T(8,128)(2,1)S(1)} %shard_map.96), channel_id=1, source_target_pairs={{4,0},{8,4},{12,8},{14,12},{10,14},{6,10},{2,6},{0,2},{5,1},{9,5},... | collective-permute-start | bytes 1572872 | tf_op jit(solution)/shard_map/ppermute | solution.py:314
  155.8 21.3 %collective-permute-start.15 = (bf16[64,4096]{1,0:T(8,128)(2,1)S(1)}, bf16[64,4096]{1,0:T(8,128)(2,1)S(1)}, u32[]{:S(2)}, u32[]{:S(2)}) collective-permute-start(bf16[64,4096]{1,0:T(8,128)(2,1)S(1)} %shard_map.83), channel_id=1, source_target_pairs={{0,4},{4,8},{8,12},{12,14},{14,10},{10,6},{6,2},{2,0},{1,5},{5,9},... | collective-permute-start | bytes 1572872 | tf_op jit(solution)/shard_map/ppermute | solution.py:311
  156.8 20.7 %collective-permute-start.25 = (bf16[64,4096]{1,0:T(8,128)(2,1)S(1)}, bf16[64,4096]{1,0:T(8,128)(2,1)S(1)}, u32[]{:S(2)}, u32[]{:S(2)}) collective-permute-start(bf16[64,4096]{1,0:T(8,128)(2,1)S(1)} %shard_map.101), channel_id=1, source_target_pairs={{4,0},{8,4},{12,8},{14,12},{10,14},{6,10},{2,6},{0,2},{5,1},{9,5},... | collective-permute-start | bytes 1572872 | tf_op jit(solution)/shard_map/ppermute | solution.py:314

commit v6 on v5

--- a/solution.py
+++ b/solution.py
@@ -171,16 +171,17 @@
     return lax.dot_general(x, y, (dims, ((), ())), preferred_element_type=jnp.float32)
 
 
-def encode(rows, words, bias, listed, which):
+def encode(rows, words, biases, listed, which):
     count, tile, n = words[0].shape[0], rows.shape[1] // TILES, len(words)
 
     def kernel(x_ref, *refs):
-        w_refs, (b_ref, m_ref), outs, acc = refs[:n], refs[n : n + 2], refs[n + 2 : -1], refs[-1]
+        w_refs, b_refs, m_ref = refs[:n], refs[n : 2 * n], refs[2 * n]
+        outs, acc = refs[2 * n + 1 : -1], refs[-1]
 
         @pl.when(pl.program_id(0) == 0)
         def _():
-            for k, i in enumerate(which):
-                row = jnp.broadcast_to(b_ref[i : i + 1, :], (acc.shape[0], count))
+            for k in range(n):
+                row = jnp.broadcast_to(b_refs[k][...].astype(jnp.float32), (acc.shape[0], count))
                 acc[:, k * count : (k + 1) * count] = row
 
         every = jnp.concatenate([w[...] for w in w_refs]) if n > 1 else w_refs[0][...]
@@ -200,10 +201,10 @@
     return local_call(
         kernel,
         (TILES,),
-        [columns(x, tile) for x in (rows, *words)] + [whole(bias), whole(listed)],
+        [columns(x, tile) for x in (rows, *words)] + [whole(x) for x in (*biases, listed)],
         [whole(o) for o in out],
         out,
-        (rows, *words, bias, listed),
+        (rows, *words, *biases, listed),
         scratch=[pltpu.VMEM((shape[0], n * count), jnp.float32)],
     )
 
@@ -327,27 +328,23 @@
     listed = jnp.any(lists[:, :, None] == owners, axis=1).astype(jnp.float32)
     listed = jnp.repeat(listed, rows_each, axis=0)
 
-    biases = jnp.broadcast_to(enc_bias.reshape(1, latents), (count, latents))
-    biases = lax.all_to_all(biases, "lat", split_axis=0, concat_axis=0, tiled=True)
-    pick = (owners[:, None] == jnp.arange(count)).astype(biases.dtype)
-    biases = jnp.einsum("so,ol->sl", pick, biases, preferred_element_type=jnp.float32)
-
     acts = activations.reshape(half_blocks * rows_each, width)
     rows = None
 
-    words = {0: dictionary}
+    words, biases = {0: dictionary}, {0: enc_bias.reshape(1, latents)}
     codes, sigmas, rebuilt = {}, {}, None
     for t in range(1, half):
         arrived = to_right(words[1 - t]), to_left(words[t - 1])
+        small = to_right(biases[1 - t]), to_left(biases[t - 1])
+        tokens = () if rebuilt is None else (rebuilt,)
+        words[-t], words[t], biases[-t], biases[t] = after((*arrived, *small), *tokens)
         if t == 1:
-            words[-1], words[1] = after(arrived, biases)
             (shift,) = after((dec_bias.reshape(1, width),), words[1])
             rows = centre(acts, to_core(acts), shift)
-        else:
-            words[-t], words[t] = after(arrived, rebuilt)
         for group in ((-t, t),) if t > 1 else ((0,), (-t, t)):
             blocks = [words[step] for step in group]
-            out = encode(rows, blocks, biases, listed, [steps.index(step) for step in group])
+            shifts = [biases[step] for step in group]
+            out = encode(rows, blocks, shifts, listed, [steps.index(step) for step in group])
             for k, step in enumerate(group):
                 codes[step], sigmas[step] = out[2 * k : 2 * k + 2]
             dtype = jnp.bfloat16 if t == half - 1 and group[-1] == t else jnp.float32
@@ -356,11 +353,11 @@
     middle = half_blocks * rows_each
     swapped = to_core(rebuilt)
     last = to_right(words[1 - half][:cut]), to_left(words[half - 1][cut:])
-    last = after(last, rebuilt)
+    *last, biases[half] = after((*last, to_right(biases[1 - half])), rebuilt)
     words[half] = jnp.concatenate(last)
     other_words = to_core(words[half])
     preacts = jnp.einsum("rd,ld->rl", rows, words[half], preferred_element_type=jnp.float32)
-    preacts = preacts + biases[-1:]
+    preacts = preacts + biases[half].astype(jnp.float32)
     mask = listed[:, len(steps) - 1 :] > 0
     code = jnp.where(mask, jax.nn.softplus(preacts), 0.0).astype(jnp.bfloat16)
     sigma = jnp.where(mask, jax.nn.sigmoid(preacts), 0.0)

time: 179 us -> 178 us (level)
    ppermute x11 -> x14, waiting for transfers between devices: 6.33 us -> 26.7 us  [to_left(): return lax.ppermute(x, 'lat', left_pairs)]
    all_to_all x1 -> x0, waiting for transfers between devices: 20 us -> none  [ring_body(): lax.all_to_all(biases, 'lat', split_axis=0, concat_axis=0, tiled=True)]
    ppermute x11 -> x15, starting transfers between devices: 6.35 us -> 18.2 us  [to_right(): return lax.ppermute(x, 'lat', right_pairs)]
    all_to_all x1 -> x0, starting transfers between devices: 6.19 us -> none  [ring_body(): lax.all_to_all(biases, 'lat', split_axis=0, concat_axis=0, tiled=True)]
    ppermute x11 -> x14, starting transfers between devices: 17.9 us -> 13.8 us  [to_left(): return lax.ppermute(x, 'lat', left_pairs)]
    ppermute x11 -> x15, waiting for transfers between devices: 61.1 us -> 59.7 us  [to_right(): return lax.ppermute(x, 'lat', right_pairs)]
  transfers between devices with their start and end apart: 27 -> 33, of which waited for: 17 -> 18; matrix products, arithmetic and copies ran while one was open for 2% -> 1% of each run, Pallas kernels for 28% -> 28%
where the time goes in v6:
time: 178 us
  waiting for transfers between devices  87.6 us (49%)
  Pallas kernels  49.1 us (28%)
  starting transfers between devices  32.8 us (18%)
  matrix products  4.36 us (2%)
  local copies, waits for them, and re-layouts  1.99 us (1%)
    ppermute x15, waiting for transfers between devices, to_right(): return lax.ppermute(x, 'lat', right_pairs)  59.7 us
    pallas_call x35, Pallas kernels, local_call(): pl.pallas_call(kernel, grid=grid, in_specs=in_specs, out_specs=out_specs,...  49.1 us
    ppermute x14, waiting for transfers between devices, to_left(): return lax.ppermute(x, 'lat', left_pairs)  26.7 us
    ppermute x15, starting transfers between devices, to_right(): return lax.ppermute(x, 'lat', right_pairs)  18.2 us
    ppermute x14, starting transfers between devices, to_left(): return lax.ppermute(x, 'lat', left_pairs)  13.8 us
  transfers between devices with their start and end apart: 33, of which 18 were waited for; matrix products, arithmetic and copies ran while one was open for 1% of the time, Pallas kernels for 28%

profile of v6, /device:TPU:0, one launch (start us, length us, event | category | flops | bytes accessed | tf_op | source)
XLA Modules:
  0.0 178.1 jit_solution(4662825825083549764)
XLA Ops:
  0.0 2.9 %collective-permute-start.2 = (bf16[128,4096]{1,0:T(8,128)(2,1)}, bf16[128,4096]{1,0:T(8,128)(2,1)S(1)}, u32[]{:S(2)}, u32[]{:S(2)}) collective-permute-start(bf16[128,4096]{1,0:T(8,128)(2,1)} %w_ref.1), channel_id=1, source_target_pairs={{4,0},{8,4},{12,8},{14,12},{10,14},{6,10},{2,6},{0,2},{5,1},{9,5},... | collective-permute-start | bytes 3145736 | tf_op jit(solution)/shard_map/ppermute | solution.py:315
  3.1 1.9 %collective-permute-start.4 = (bf16[1,128]{1,0:T(2,128)(2,1)}, bf16[1,128]{1,0:T(2,128)(2,1)S(1)}, u32[]{:S(2)}, u32[]{:S(2)}) collective-permute-start(bf16[1,128]{1,0:T(2,128)(2,1)} %bitcast.39), channel_id=1, source_target_pairs={{4,0},{8,4},{12,8},{14,12},{10,14},{6,10},{2,6},{0,2},{5,1},{9,5},... | collective-permute-start | bytes 776 | tf_op jit(solution)/shard_map/ppermute | solution.py:315
  5.1 21.3 %collective-permute-done.4.refs_3_ = bf16[1,128]{1,0:T(2,128)(2,1)S(1)} collective-permute-done((bf16[1,128]{1,0:T(2,128)(2,1)}, bf16[1,128]{1,0:T(2,128)(2,1)S(1)}, u32[]{:S(2)}, u32[]{:S(2)}) %collective-permute-start.4) | collective-permute-done | bytes 288 | tf_op jit(solution)/shard_map/ppermute | solution.py:315
  28.4 1.6 collective-permute-start.6
  30.9 1.6 collective-permute-start.8
  33.8 2.4 %shard_map.57.x_ref = bf16[256,4096]{1,0:T(8,128)(2,1)S(1)} custom-call(bf16[128,4096]{1,0:T(8,128)(2,1)S(1)} %bitcast.38, bf16[128,4096]{1,0:T(8,128)(2,1)} %collective-permute-done.y_ref, bf16[1,4096]{1,0:T(2,128)(2,1)S(1)} %shard_map.56.b_ref), custom_call_target="tpu_custom_call" | custom-call | tf_op jit(solution)/shard_map/pallas_call | solution.py:135
  36.2 1.6 shard_map.58
  37.8 3.4 %shard_map.59 = (bf16[256,128]{1,0:T(8,128)(2,1)S(1)}, f32[256,128]{1,0:T(8,128)S(1)}, bf16[256,128]{1,0:T(8,128)(2,1)S(1)}, f32[256,128]{1,0:T(8,128)S(1)}) custom-call(bf16[256,4096]{1,0:T(8,128)(2,1)S(1)} %shard_map.57.x_ref, bf16[128,4096]{1,0:T(8,128)(2,1)} %get-tuple-element.38.refs_0_.refs_2_.w_ref, ...), custom_call_target="tpu_custom_call" | custom-call | tf_op jit(solution)/shard_map/pallas_call | solution.py:135
  42.7 3.5 %shard_map.61.refs_4_ = f32[256,4096]{1,0:T(8,128)S(1)} custom-call(bf16[256,128]{1,0:T(8,128)(2,1)S(1)} %get-tuple-element.41.refs_0_.c_ref, bf16[256,128]{1,0:T(8,128)(2,1)S(1)} %get-tuple-element.42.refs_1_.c_ref, bf16[128,4096]{1,0:T(8,128)(2,1)} %get-tuple-element.38.refs_0_.refs_2_.w_ref, ...), custom_call_target="tpu_custom_call", output_to_operand_aliasing={{}: (4, {})} | custom-call | tf_op jit(solution)/shard_map/pallas_call | solution.py:135
  46.2 5.7 %collective-permute-done.7.refs_2_ = bf16[1,128]{1,0:T(2,128)(2,1)S(1)} collective-permute-done((bf16[1,128]{1,0:T(2,128)(2,1)S(1)}, bf16[1,128]{1,0:T(2,128)(2,1)S(1)}, u32[]{:S(2)}, u32[]{:S(2)}) %collective-permute-start.7) | collective-permute-done | bytes 288 | tf_op jit(solution)/shard_map/ppermute | solution.py:312
  56.3 1.9 %shard_map.63 = (bf16[256,128]{1,0:T(8,128)(2,1)S(1)}, f32[256,128]{1,0:T(8,128)S(1)}, bf16[256,128]{1,0:T(8,128)(2,1)S(1)}, f32[256,128]{1,0:T(8,128)S(1)}) custom-call(bf16[256,4096]{1,0:T(8,128)(2,1)S(1)} %shard_map.57.x_ref, bf16[128,4096]{1,0:T(8,128)(2,1)S(1)} %get-tuple-element.43.refs_0_.refs_2_.w_ref, ...), custom_call_target="tpu_custom_call" | custom-call | tf_op jit(solution)/shard_map/pallas_call | solution.py:135
  58.2 2.4 %shard_map.64.refs_4_ = f32[256,4096]{1,0:T(8,128)S(1)} custom-call(bf16[256,128]{1,0:T(8,128)(2,1)S(1)} %get-tuple-element.47.refs_0_.c_ref, bf16[256,128]{1,0:T(8,128)(2,1)S(1)} %get-tuple-element.48.refs_1_.c_ref, bf16[128,4096]{1,0:T(8,128)(2,1)S(1)} %get-tuple-element.43.refs_0_.refs_2_.w_ref, ...), custom_call_target="tpu_custom_call", output_to_operand_aliasing={{}: (4, {})} | custom-call | tf_op jit(solution)/shard_map/pallas_call | solution.py:135
  60.7 14.4 %collective-permute-done.11.refs_2_ = bf16[1,128]{1,0:T(2,128)(2,1)S(1)} collective-permute-done((bf16[1,128]{1,0:T(2,128)(2,1)S(1)}, bf16[1,128]{1,0:T(2,128)(2,1)S(1)}, u32[]{:S(2)}, u32[]{:S(2)}) %collective-permute-start.11) | collective-permute-done | bytes 288 | tf_op jit(solution)/shard_map/ppermute | solution.py:312
  75.1 2.0 %collective-permute-done.12.refs_3_ = bf16[1,128]{1,0:T(2,128)(2,1)S(1)} collective-permute-done((bf16[1,128]{1,0:T(2,128)(2,1)S(1)}, bf16[1,128]{1,0:T(2,128)(2,1)S(1)}, u32[]{:S(2)}, u32[]{:S(2)}) %collective-permute-start.12) | collective-permute-done | bytes 288 | tf_op jit(solution)/shard_map/ppermute | solution.py:315
  80.8 1.9 %shard_map.66 = (bf16[256,128]{1,0:T(8,128)(2,1)S(1)}, f32[256,128]{1,0:T(8,128)S(1)}, bf16[256,128]{1,0:T(8,128)(2,1)S(1)}, f32[256,128]{1,0:T(8,128)S(1)}) custom-call(bf16[256,4096]{1,0:T(8,128)(2,1)S(1)} %shard_map.57.x_ref, bf16[128,4096]{1,0:T(8,128)(2,1)S(1)} %get-tuple-element.49.refs_0_.refs_2_.w_ref, ...), custom_call_target="tpu_custom_call" | custom-call | tf_op jit(solution)/shard_map/pallas_call | solution.py:135
  82.7 2.3 %shard_map.67.refs_3_ = bf16[256,4096]{1,0:T(8,128)(2,1)S(1)} custom-call(bf16[256,128]{1,0:T(8,128)(2,1)S(1)} %get-tuple-element.53.refs_0_.c_ref, bf16[256,128]{1,0:T(8,128)(2,1)S(1)} %get-tuple-element.54.refs_1_.c_ref, bf16[128,4096]{1,0:T(8,128)(2,1)S(1)} %get-tuple-element.49.refs_0_.refs_2_.w_ref, ...), custom_call_target="tpu_custom_call" | custom-call | tf_op jit(solution)/shard_map/pallas_call | solution.py:135
  85.3 1.7 collective-permute-done.16.refs_2_
  97.6 1.8 %shard_map.74.refs_0_ = f32[128,4096]{1,0:T(8,128)S(1)} custom-call(bf16[256,128]{1,0:T(8,128)(2,1)S(1)} %get-tuple-element.54.refs_1_.c_ref, bf16[256,128]{1,0:T(8,128)(2,1)S(1)} %shard_map.73.s_ref, bf16[256,4096]{1,0:T(8,128)(2,1)S(1)} %add_convert_fusion.e_ref, bf16[256,4096]{1,0:T(8,128)(2,1)S(1)} %shard_map.57.x_ref), custom_call_target="tpu_custom_call" | custom-call | flops 536870912 | bytes 6291456 | tf_op jit(solution)/shard_map/pallas_call | solution.py:135
  102.7 1.8 %shard_map.86.refs_0_ = f32[128,4096]{1,0:T(8,128)S(1)} custom-call(bf16[256,128]{1,0:T(8,128)(2,1)S(1)} %get-tuple-element.53.refs_0_.c_ref, bf16[256,128]{1,0:T(8,128)(2,1)S(1)} %shard_map.85.s_ref, bf16[256,4096]{1,0:T(8,128)(2,1)S(1)} %add_convert_fusion.e_ref, bf16[256,4096]{1,0:T(8,128)(2,1)S(1)} %shard_map.57.x_ref), custom_call_target="tpu_custom_call" | custom-call | flops 536870912 | bytes 6291456 | tf_op jit(solution)/shard_map/pallas_call | solution.py:135
  105.6 3.3 %collective-permute-done.19.refs_1_ = bf16[64,4096]{1,0:T(8,128)(2,1)S(1)} collective-permute-done((bf16[64,4096]{1,0:T(8,128)(2,1)S(1)}, bf16[64,4096]{1,0:T(8,128)(2,1)S(1)}, u32[]{:S(2)}, u32[]{:S(2)}) %collective-permute-start.19) | collective-permute-done | bytes 524320 | tf_op jit(solution)/shard_map/ppermute | solution.py:312
  113.1 1.8 %shard_map.71.refs_0_ = f32[128,4096]{1,0:T(8,128)S(1)} custom-call(bf16[256,128]{1,0:T(8,128)(2,1)S(1)} %get-tuple-element.48.refs_1_.c_ref, bf16[256,128]{1,0:T(8,128)(2,1)S(1)} %shard_map.70.s_ref, bf16[256,4096]{1,0:T(8,128)(2,1)S(1)} %add_convert_fusion.e_ref, bf16[256,4096]{1,0:T(8,128)(2,1)S(1)} %shard_map.57.x_ref), custom_call_target="tpu_custom_call" | custom-call | flops 536870912 | bytes 6291456 | tf_op jit(solution)/shard_map/pallas_call | solution.py:135
  114.9 5.2 %collective-permute-done.28.refs_1_ = bf16[64,4096]{1,0:T(8,128)(2,1)S(1)} collective-permute-done((bf16[64,4096]{1,0:T(8,128)(2,1)S(1)}, bf16[64,4096]{1,0:T(8,128)(2,1)S(1)}, u32[]{:S(2)}, u32[]{:S(2)}) %collective-permute-start.28) | collective-permute-done | bytes 524320 | tf_op jit(solution)/shard_map/ppermute | solution.py:312
  123.5 1.8 %shard_map.93.refs_0_ = f32[128,4096]{1,0:T(8,128)S(1)} custom-call(bf16[256,128]{1,0:T(8,128)(2,1)S(1)} %get-tuple-element.47.refs_0_.c_ref, bf16[256,128]{1,0:T(8,128)(2,1)S(1)} %shard_map.92.s_ref, bf16[256,4096]{1,0:T(8,128)(2,1)S(1)} %add_convert_fusion.e_ref, bf16[256,4096]{1,0:T(8,128)(2,1)S(1)} %shard_map.57.x_ref), custom_call_target="tpu_custom_call" | custom-call | flops 536870912 | bytes 6291456 | tf_op jit(solution)/shard_map/pallas_call | solution.py:135
  126.2 5.1 %collective-permute-done.20.refs_1_ = bf16[64,4096]{1,0:T(8,128)(2,1)S(1)} collective-permute-done((bf16[64,4096]{1,0:T(8,128)(2,1)S(1)}, bf16[64,4096]{1,0:T(8,128)(2,1)S(1)}, u32[]{:S(2)}, u32[]{:S(2)}) %collective-permute-start.20) | collective-permute-done | bytes 524320 | tf_op jit(solution)/shard_map/ppermute | solution.py:312
  135.6 1.8 %shard_map.82.refs_0_ = f32[128,4096]{1,0:T(8,128)S(1)} custom-call(bf16[256,128]{1,0:T(8,128)(2,1)S(1)} %get-tuple-element.42.refs_1_.c_ref, bf16[256,128]{1,0:T(8,128)(2,1)S(1)} %shard_map.81.s_ref, bf16[256,4096]{1,0:T(8,128)(2,1)S(1)} %add_convert_fusion.e_ref, bf16[256,4096]{1,0:T(8,128)(2,1)S(1)} %shard_map.57.x_ref), custom_call_target="tpu_custom_call" | custom-call | flops 536870912 | bytes 6291456 | tf_op jit(solution)/shard_map/pallas_call | solution.py:135
  137.4 5.2 %collective-permute-done.29.refs_1_ = bf16[64,4096]{1,0:T(8,128)(2,1)S(1)} collective-permute-done((bf16[64,4096]{1,0:T(8,128)(2,1)S(1)}, bf16[64,4096]{1,0:T(8,128)(2,1)S(1)}, u32[]{:S(2)}, u32[]{:S(2)}) %collective-permute-start.29) | collective-permute-done | bytes 524320 | tf_op jit(solution)/shard_map/ppermute | solution.py:312
  144.4 3.0 %shard_map.89.s_ref = bf16[256,128]{1,0:T(8,128)(2,1)S(1)} custom-call(bf16[256,4096]{1,0:T(8,128)(2,1)S(1)} %add_convert_fusion.e_ref, bf16[128,4096]{1,0:T(8,128)(2,1)} %get-tuple-element.38.refs_0_.refs_2_.w_ref, f32[256,128]{1,0:T(8,128)S(1)} %shard_map.88.s_ref), custom_call_target="tpu_custom_call" | custom-call | flops 268435456 | bytes 3145728 | tf_op jit(solution)/shard_map/pallas_call | solution.py:135
  147.4 1.8 %shard_map.90.refs_0_ = f32[128,4096]{1,0:T(8,128)S(1)} custom-call(bf16[256,128]{1,0:T(8,128)(2,1)S(1)} %get-tuple-element.41.refs_0_.c_ref, bf16[256,128]{1,0:T(8,128)(2,1)S(1)} %shard_map.89.s_ref, bf16[256,4096]{1,0:T(8,128)(2,1)S(1)} %add_convert_fusion.e_ref, bf16[256,4096]{1,0:T(8,128)(2,1)S(1)} %shard_map.57.x_ref), custom_call_target="tpu_custom_call" | custom-call | flops 536870912 | bytes 6291456 | tf_op jit(solution)/shard_map/pallas_call | solution.py:135
  150.1 3.6 %collective-permute-done.21.refs_1_ = bf16[64,4096]{1,0:T(8,128)(2,1)S(1)} collective-permute-done((bf16[64,4096]{1,0:T(8,128)(2,1)S(1)}, bf16[64,4096]{1,0:T(8,128)(2,1)S(1)}, u32[]{:S(2)}, u32[]{:S(2)}) %collective-permute-start.21) | collective-permute-done | bytes 524320 | tf_op jit(solution)/shard_map/ppermute | solution.py:312
  158.1 1.8 %shard_map.79 = f32[128,4096]{1,0:T(8,128)S(1)} custom-call(bf16[256,128]{1,0:T(8,128)(2,1)S(1)} %get-tuple-element.37.refs_0_.c_ref, bf16[256,128]{1,0:T(8,128)(2,1)S(1)} %shard_map.78.s_ref, bf16[256,4096]{1,0:T(8,128)(2,1)S(1)} %add_convert_fusion.e_ref, bf16[256,4096]{1,0:T(8,128)(2,1)S(1)} %shard_map.57.x_ref), custom_call_target="tpu_custom_call" | custom-call | flops 536870912 | bytes 6291456 | tf_op jit(solution)/shard_map/pallas_call | solution.py:135
  159.9 5.1 %collective-permute-done.30 = bf16[64,4096]{1,0:T(8,128)(2,1)S(1)} collective-permute-done((bf16[64,4096]{1,0:T(8,128)(2,1)S(1)}, bf16[64,4096]{1,0:T(8,128)(2,1)S(1)}, u32[]{:S(2)}, u32[]{:S(2)}) %collective-permute-start.30) | collective-permute-done | bytes 524320 | tf_op jit(solution)/shard_map/ppermute | solution.py:312
  166.5 8.9 %collective-permute-done.22 = bf16[64,4096]{1,0:T(8,128)(2,1)S(1)} collective-permute-done((bf16[64,4096]{1,0:T(8,128)(2,1)S(1)}, bf16[64,4096]{1,0:T(8,128)(2,1)S(1)}, u32[]{:S(2)}, u32[]{:S(2)}) %collective-permute-start.22) | collective-permute-done | bytes 524320 | tf_op jit(solution)/shard_map/ppermute | solution.py:312
  (118 shorter events, 53.1 us)
Async XLA Ops:
  0.0 27.9 %collective-permute-start.2 = (bf16[128,4096]{1,0:T(8,128)(2,1)}, bf16[128,4096]{1,0:T(8,128)(2,1)S(1)}, u32[]{:S(2)}, u32[]{:S(2)}) collective-permute-start(bf16[128,4096]{1,0:T(8,128)(2,1)} %w_ref.1), channel_id=1, source_target_pairs={{4,0},{8,4},{12,8},{14,12},{10,14},{6,10},{2,6},{0,2},{5,1},{9,5},... | collective-permute-start | bytes 3145736 | tf_op jit(solution)/shard_map/ppermute | solution.py:315
  2.9 24.9 %collective-permute-start.1 = (bf16[128,4096]{1,0:T(8,128)(2,1)}, bf16[128,4096]{1,0:T(8,128)(2,1)}, u32[]{:S(2)}, u32[]{:S(2)}) collective-permute-start(bf16[128,4096]{1,0:T(8,128)(2,1)} %w_ref.1), channel_id=1, source_target_pairs={{0,4},{4,8},{8,12},{12,14},{14,10},{10,6},{6,2},{2,0},{1,5},{5,9},... | collective-permute-start | bytes 3145736 | tf_op jit(solution)/shard_map/ppermute | solution.py:312
  3.1 29.5 %collective-permute-start = (bf16[128,4096]{1,0:T(8,128)(2,1)}, bf16[128,4096]{1,0:T(8,128)(2,1)}, u32[]{:S(2)}, u32[]{:S(2)}) collective-permute-start(bf16[128,4096]{1,0:T(8,128)(2,1)} %bitcast.37), channel_id=1, source_target_pairs={{0,1},{1,0},{2,3},{3,2},{4,5},{5,4},{6,7},{7,6},{8,9},{9,8},{10,11... | collective-permute-start | bytes 3145736 | tf_op jit(solution)/shard_map/ppermute | solution.py:318
  3.1 23.4 %collective-permute-start.4 = (bf16[1,128]{1,0:T(2,128)(2,1)}, bf16[1,128]{1,0:T(2,128)(2,1)S(1)}, u32[]{:S(2)}, u32[]{:S(2)}) collective-permute-start(bf16[1,128]{1,0:T(2,128)(2,1)} %bitcast.39), channel_id=1, source_target_pairs={{4,0},{8,4},{12,8},{14,12},{10,14},{6,10},{2,6},{0,2},{5,1},{9,5},... | collective-permute-start | bytes 776 | tf_op jit(solution)/shard_map/ppermute | solution.py:315
  5.0 22.9 %collective-permute-start.3 = (bf16[1,128]{1,0:T(2,128)(2,1)}, bf16[1,128]{1,0:T(2,128)(2,1)S(1)}, u32[]{:S(2)}, u32[]{:S(2)}) collective-permute-start(bf16[1,128]{1,0:T(2,128)(2,1)} %bitcast.40), channel_id=1, source_target_pairs={{0,4},{4,8},{8,12},{12,14},{14,10},{10,6},{6,2},{2,0},{1,5},{5,9},... | collective-permute-start | bytes 776 | tf_op jit(solution)/shard_map/ppermute | solution.py:312
  27.9 24.3 %collective-permute-start.5 = (bf16[128,4096]{1,0:T(8,128)(2,1)}, bf16[128,4096]{1,0:T(8,128)(2,1)S(1)}, u32[]{:S(2)}, u32[]{:S(2)}) collective-permute-start(bf16[128,4096]{1,0:T(8,128)(2,1)} %get-tuple-element.38.refs_0_.refs_2_.w_ref), channel_id=1, source_target_pairs={{0,4},{4,8},{8,12},{12,14},{14,10},{10,6},{6,2},{2,0},{1,5},{5,9},... | collective-permute-start | bytes 3145736 | tf_op jit(solution)/shard_map/ppermute | solution.py:312
  28.4 23.8 %collective-permute-start.6 = (bf16[128,4096]{1,0:T(8,128)(2,1)S(1)}, bf16[128,4096]{1,0:T(8,128)(2,1)S(1)}, u32[]{:S(2)}, u32[]{:S(2)}) collective-permute-start(bf16[128,4096]{1,0:T(8,128)(2,1)S(1)} %get-tuple-element.36.refs_1_.refs_3_.w_ref), channel_id=1, source_target_pairs={{4,0},{8,4},{12,8},{14,12},{10,14},{6,10},{2,6},{0,2},{5,1},{9,5},... | collective-permute-start | bytes 3145736 | tf_op jit(solution)/shard_map/ppermute | solution.py:315
  30.5 21.5 %collective-permute-start.7 = (bf16[1,128]{1,0:T(2,128)(2,1)S(1)}, bf16[1,128]{1,0:T(2,128)(2,1)S(1)}, u32[]{:S(2)}, u32[]{:S(2)}) collective-permute-start(bf16[1,128]{1,0:T(2,128)(2,1)S(1)} %get-tuple-element.39.refs_2_), channel_id=1, source_target_pairs={{0,4},{4,8},{8,12},{12,14},{14,10},{10,6},{6,2},{2,0},{1,5},{5,9},... | collective-permute-start | bytes 776 | tf_op jit(solution)/shard_map/ppermute | solution.py:312
  30.9 21.2 %collective-permute-start.8 = (bf16[1,128]{1,0:T(2,128)(2,1)S(1)}, bf16[1,128]{1,0:T(2,128)(2,1)S(1)}, u32[]{:S(2)}, u32[]{:S(2)}) collective-permute-start(bf16[1,128]{1,0:T(2,128)(2,1)S(1)} %get-tuple-element.40.refs_3_), channel_id=1, source_target_pairs={{4,0},{8,4},{12,8},{14,12},{10,14},{6,10},{2,6},{0,2},{5,1},{9,5},... | collective-permute-start | bytes 776 | tf_op jit(solution)/shard_map/ppermute | solution.py:315
  52.2 24.8 %collective-permute-start.9 = (bf16[128,4096]{1,0:T(8,128)(2,1)S(1)}, bf16[128,4096]{1,0:T(8,128)(2,1)S(1)}, u32[]{:S(2)}, u32[]{:S(2)}) collective-permute-start(bf16[128,4096]{1,0:T(8,128)(2,1)S(1)} %get-tuple-element.43.refs_0_.refs_2_.w_ref), channel_id=1, source_target_pairs={{0,4},{4,8},{8,12},{12,14},{14,10},{10,6},{6,2},{2,0},{1,5},{5,9},... | collective-permute-start | bytes 3145736 | tf_op jit(solution)/shard_map/ppermute | solution.py:312
  53.8 23.3 %collective-permute-start.10 = (bf16[128,4096]{1,0:T(8,128)(2,1)S(1)}, bf16[128,4096]{1,0:T(8,128)(2,1)S(1)}, u32[]{:S(2)}, u32[]{:S(2)}) collective-permute-start(bf16[128,4096]{1,0:T(8,128)(2,1)S(1)} %get-tuple-element.44.refs_1_.refs_3_.w_ref), channel_id=1, source_target_pairs={{4,0},{8,4},{12,8},{14,12},{10,14},{6,10},{2,6},{0,2},{5,1},{9,5},... | collective-permute-start | bytes 3145736 | tf_op jit(solution)/shard_map/ppermute | solution.py:315
  54.3 20.8 %collective-permute-start.11 = (bf16[1,128]{1,0:T(2,128)(2,1)S(1)}, bf16[1,128]{1,0:T(2,128)(2,1)S(1)}, u32[]{:S(2)}, u32[]{:S(2)}) collective-permute-start(bf16[1,128]{1,0:T(2,128)(2,1)S(1)} %get-tuple-element.45.refs_2_), channel_id=1, source_target_pairs={{0,4},{4,8},{8,12},{12,14},{14,10},{10,6},{6,2},{2,0},{1,5},{5,9},... | collective-permute-start | bytes 776 | tf_op jit(solution)/shard_map/ppermute | solution.py:312
  55.8 21.2 %collective-permute-start.12 = (bf16[1,128]{1,0:T(2,128)(2,1)S(1)}, bf16[1,128]{1,0:T(2,128)(2,1)S(1)}, u32[]{:S(2)}, u32[]{:S(2)}) collective-permute-start(bf16[1,128]{1,0:T(2,128)(2,1)S(1)} %get-tuple-element.46.refs_3_), channel_id=1, source_target_pairs={{4,0},{8,4},{12,8},{14,12},{10,14},{6,10},{2,6},{0,2},{5,1},{9,5},... | collective-permute-start | bytes 776 | tf_op jit(solution)/shard_map/ppermute | solution.py:315
  77.1 10.2 %collective-permute-start.15 = (bf16[64,4096]{1,0:T(8,128)(2,1)S(1)}, bf16[64,4096]{1,0:T(8,128)(2,1)S(1)}, u32[]{:S(2)}, u32[]{:S(2)}) collective-permute-start(bf16[64,4096]{1,0:T(8,128)(2,1)S(1)} %slice.37), channel_id=1, source_target_pairs={{4,0},{8,4},{12,8},{14,12},{10,14},{6,10},{2,6},{0,2},{5,1},{9,5},... | collective-permute-start | bytes 1572872 | tf_op jit(solution)/shard_map/ppermute | solution.py:315
  77.7 9.7 %collective-permute-start.14 = (bf16[64,4096]{1,0:T(8,128)(2,1)S(1)}, bf16[64,4096]{1,0:T(8,128)(2,1)S(1)}, u32[]{:S(2)}, u32[]{:S(2)}) collective-permute-start(bf16[64,4096]{1,0:T(8,128)(2,1)S(1)} %slice.36), channel_id=1, source_target_pairs={{0,4},{4,8},{8,12},{12,14},{14,10},{10,6},{6,2},{2,0},{1,5},{5,9},... | collective-permute-start | bytes 1572872 | tf_op jit(solution)/shard_map/ppermute | solution.py:312
  79.2 7.8 %collective-permute-start.16 = (bf16[1,128]{1,0:T(2,128)(2,1)S(1)}, bf16[1,128]{1,0:T(2,128)(2,1)S(1)}, u32[]{:S(2)}, u32[]{:S(2)}) collective-permute-start(bf16[1,128]{1,0:T(2,128)(2,1)S(1)} %get-tuple-element.51.refs_2_), channel_id=1, source_target_pairs={{0,4},{4,8},{8,12},{12,14},{14,10},{10,6},{6,2},{2,0},{1,5},{5,9},... | collective-permute-start | bytes 776 | tf_op jit(solution)/shard_map/ppermute | solution.py:312
  85.0 5.8 %collective-permute-start.13 = (bf16[256,4096]{1,0:T(8,128)(2,1)S(1)}, bf16[256,4096]{1,0:T(8,128)(2,1)S(1)}, u32[]{:S(2)}, u32[]{:S(2)}) collective-permute-start(bf16[256,4096]{1,0:T(8,128)(2,1)S(1)} %shard_map.67.refs_3_), channel_id=1, source_target_pairs={{0,1},{1,0},{2,3},{3,2},{4,5},{5,4},{6,7},{7,6},{8,9},{9,8},{10,11... | collective-permute-start | bytes 6291464 | tf_op jit(solution)/shard_map/ppermute | solution.py:318
  87.4 3.6 %collective-permute-start.18 = (bf16[128,4096]{1,0:T(8,128)(2,1)S(1)}, bf16[128,4096]{1,0:T(8,128)(2,1)S(1)}, u32[]{:S(2)}, u32[]{:S(2)}) collective-permute-start(bf16[128,4096]{1,0:T(8,128)(2,1)S(1)} %constant_dynamic-update-slice_fusion), channel_id=1, source_target_pairs={{0,1},{1,0},{2,3},{3,2},{4,5},{5,4},{6,7},{7,6},{8,9},{9,8},{10,11... | collective-permute-start | bytes 3145736 | tf_op jit(solution)/shard_map/ppermute | solution.py:318
  94.0 14.8 %collective-permute-start.19 = (bf16[64,4096]{1,0:T(8,128)(2,1)S(1)}, bf16[64,4096]{1,0:T(8,128)(2,1)S(1)}, u32[]{:S(2)}, u32[]{:S(2)}) collective-permute-start(bf16[64,4096]{1,0:T(8,128)(2,1)S(1)} %get-tuple-element.72), channel_id=1, source_target_pairs={{0,4},{4,8},{8,12},{12,14},{14,10},{10,6},{6,2},{2,0},{1,5},{5,9},... | collective-permute-start | bytes 1572872 | tf_op jit(solution)/shard_map/ppermute | solution.py:312
  95.6 15.1 %collective-permute-start.23 = (bf16[64,4096]{1,0:T(8,128)(2,1)S(1)}, bf16[64,4096]{1,0:T(8,128)(2,1)S(1)}, u32[]{:S(2)}, u32[]{:S(2)}) collective-permute-start(bf16[64,4096]{1,0:T(8,128)(2,1)S(1)} %get-tuple-element.71), channel_id=1, source_target_pairs={{4,0},{8,4},{12,8},{14,12},{10,14},{6,10},{2,6},{0,2},{5,1},{9,5},... | collective-permute-start | bytes 1572872 | tf_op jit(solution)/shard_map/ppermute | solution.py:315
  99.7 20.4 %collective-permute-start.28 = (bf16[64,4096]{1,0:T(8,128)(2,1)S(1)}, bf16[64,4096]{1,0:T(8,128)(2,1)S(1)}, u32[]{:S(2)}, u32[]{:S(2)}) collective-permute-start(bf16[64,4096]{1,0:T(8,128)(2,1)S(1)} %shard_map.97), channel_id=1, source_target_pairs={{0,4},{4,8},{8,12},{12,14},{14,10},{10,6},{6,2},{2,0},{1,5},{5,9},... | collective-permute-start | bytes 1572872 | tf_op jit(solution)/shard_map/ppermute | solution.py:312
  104.8 20.5 %collective-permute-start.25 = (bf16[64,4096]{1,0:T(8,128)(2,1)S(1)}, bf16[64,4096]{1,0:T(8,128)(2,1)S(1)}, u32[]{:S(2)}, u32[]{:S(2)}) collective-permute-start(bf16[64,4096]{1,0:T(8,128)(2,1)S(1)} %shard_map.94), channel_id=1, source_target_pairs={{4,0},{8,4},{12,8},{14,12},{10,14},{6,10},{2,6},{0,2},{5,1},{9,5},... | collective-permute-start | bytes 1572872 | tf_op jit(solution)/shard_map/ppermute | solution.py:315
  109.2 22.1 %collective-permute-start.20 = (bf16[64,4096]{1,0:T(8,128)(2,1)S(1)}, bf16[64,4096]{1,0:T(8,128)(2,1)S(1)}, u32[]{:S(2)}, u32[]{:S(2)}) collective-permute-start(bf16[64,4096]{1,0:T(8,128)(2,1)S(1)} %shard_map.75), channel_id=1, source_target_pairs={{0,4},{4,8},{8,12},{12,14},{14,10},{10,6},{6,2},{2,0},{1,5},{5,9},... | collective-permute-start | bytes 1572872 | tf_op jit(solution)/shard_map/ppermute | solution.py:312
  111.0 22.1 %collective-permute-start.24 = (bf16[64,4096]{1,0:T(8,128)(2,1)S(1)}, bf16[64,4096]{1,0:T(8,128)(2,1)S(1)}, u32[]{:S(2)}, u32[]{:S(2)}) collective-permute-start(bf16[64,4096]{1,0:T(8,128)(2,1)S(1)} %shard_map.87), channel_id=1, source_target_pairs={{4,0},{8,4},{12,8},{14,12},{10,14},{6,10},{2,6},{0,2},{5,1},{9,5},... | collective-permute-start | bytes 1572872 | tf_op jit(solution)/shard_map/ppermute | solution.py:315
  120.4 22.1 %collective-permute-start.29 = (bf16[64,4096]{1,0:T(8,128)(2,1)S(1)}, bf16[64,4096]{1,0:T(8,128)(2,1)S(1)}, u32[]{:S(2)}, u32[]{:S(2)}) collective-permute-start(bf16[64,4096]{1,0:T(8,128)(2,1)S(1)} %shard_map.98), channel_id=1, source_target_pairs={{0,4},{4,8},{8,12},{12,14},{14,10},{10,6},{6,2},{2,0},{1,5},{5,9},... | collective-permute-start | bytes 1572872 | tf_op jit(solution)/shard_map/ppermute | solution.py:312
  125.6 23.6 %collective-permute-start.26 = (bf16[64,4096]{1,0:T(8,128)(2,1)S(1)}, bf16[64,4096]{1,0:T(8,128)(2,1)S(1)}, u32[]{:S(2)}, u32[]{:S(2)}) collective-permute-start(bf16[64,4096]{1,0:T(8,128)(2,1)S(1)} %shard_map.95), channel_id=1, source_target_pairs={{4,0},{8,4},{12,8},{14,12},{10,14},{6,10},{2,6},{0,2},{5,1},{9,5},... | collective-permute-start | bytes 1572872 | tf_op jit(solution)/shard_map/ppermute | solution.py:315
  131.6 22.1 %collective-permute-start.21 = (bf16[64,4096]{1,0:T(8,128)(2,1)S(1)}, bf16[64,4096]{1,0:T(8,128)(2,1)S(1)}, u32[]{:S(2)}, u32[]{:S(2)}) collective-permute-start(bf16[64,4096]{1,0:T(8,128)(2,1)S(1)} %shard_map.76), channel_id=1, source_target_pairs={{0,4},{4,8},{8,12},{12,14},{14,10},{10,6},{6,2},{2,0},{1,5},{5,9},... | collective-permute-start | bytes 1572872 | tf_op jit(solution)/shard_map/ppermute | solution.py:312
  133.5 22.1 %collective-permute-start.31 = (bf16[64,4096]{1,0:T(8,128)(2,1)S(1)}, bf16[64,4096]{1,0:T(8,128)(2,1)S(1)}, u32[]{:S(2)}, u32[]{:S(2)}) collective-permute-start(bf16[64,4096]{1,0:T(8,128)(2,1)S(1)} %shard_map.100), channel_id=1, source_target_pairs={{4,0},{8,4},{12,8},{14,12},{10,14},{6,10},{2,6},{0,2},{5,1},{9,5},... | collective-permute-start | bytes 1572872 | tf_op jit(solution)/shard_map/ppermute | solution.py:315
  142.9 22.1 %collective-permute-start.30 = (bf16[64,4096]{1,0:T(8,128)(2,1)S(1)}, bf16[64,4096]{1,0:T(8,128)(2,1)S(1)}, u32[]{:S(2)}, u32[]{:S(2)}) collective-permute-start(bf16[64,4096]{1,0:T(8,128)(2,1)S(1)} %shard_map.99), channel_id=1, source_target_pairs={{0,4},{4,8},{8,12},{12,14},{14,10},{10,6},{6,2},{2,0},{1,5},{5,9},... | collective-permute-start | bytes 1572872 | tf_op jit(solution)/shard_map/ppermute | solution.py:312
  149.5 17.0 %collective-permute-start.27 = (bf16[64,4096]{1,0:T(8,128)(2,1)S(1)}, bf16[64,4096]{1,0:T(8,128)(2,1)S(1)}, u32[]{:S(2)}, u32[]{:S(2)}) collective-permute-start(bf16[64,4096]{1,0:T(8,128)(2,1)S(1)} %shard_map.96), channel_id=1, source_target_pairs={{4,0},{8,4},{12,8},{14,12},{10,14},{6,10},{2,6},{0,2},{5,1},{9,5},... | collective-permute-start | bytes 1572872 | tf_op jit(solution)/shard_map/ppermute | solution.py:315
  154.1 21.4 %collective-permute-start.22 = (bf16[64,4096]{1,0:T(8,128)(2,1)S(1)}, bf16[64,4096]{1,0:T(8,128)(2,1)S(1)}, u32[]{:S(2)}, u32[]{:S(2)}) collective-permute-start(bf16[64,4096]{1,0:T(8,128)(2,1)S(1)} %shard_map.83), channel_id=1, source_target_pairs={{0,4},{4,8},{8,12},{12,14},{14,10},{10,6},{6,2},{2,0},{1,5},{5,9},... | collective-permute-start | bytes 1572872 | tf_op jit(solution)/shard_map/ppermute | solution.py:312
  156.0 20.7 %collective-permute-start.32 = (bf16[64,4096]{1,0:T(8,128)(2,1)S(1)}, bf16[64,4096]{1,0:T(8,128)(2,1)S(1)}, u32[]{:S(2)}, u32[]{:S(2)}) collective-permute-start(bf16[64,4096]{1,0:T(8,128)(2,1)S(1)} %shard_map.101), channel_id=1, source_target_pairs={{4,0},{8,4},{12,8},{14,12},{10,14},{6,10},{2,6},{0,2},{5,1},{9,5},... | collective-permute-start | bytes 1572872 | tf_op jit(solution)/shard_map/ppermute | solution.py:315
  (6 other events, 74.7 us)

commit v7 on v6

--- a/solution.py
+++ b/solution.py
@@ -337,7 +337,8 @@
         arrived = to_right(words[1 - t]), to_left(words[t - 1])
         small = to_right(biases[1 - t]), to_left(biases[t - 1])
         tokens = () if rebuilt is None else (rebuilt,)
-        words[-t], words[t], biases[-t], biases[t] = after((*arrived, *small), *tokens)
+        words[-t], biases[-t] = after((arrived[0], small[0]), *tokens)
+        words[t], biases[t] = after((arrived[1], small[1]), *tokens)
         if t == 1:
             (shift,) = after((dec_bias.reshape(1, width),), words[1])
             rows = centre(acts, to_core(acts), shift)

time: 178 us -> 177 us (level)
    ppermute x14, waiting for transfers between devices: 26.7 us -> 3.57 us  [to_left(): return lax.ppermute(x, 'lat', left_pairs)]
    ppermute x15, waiting for transfers between devices: 59.7 us -> 82 us  [to_right(): return lax.ppermute(x, 'lat', right_pairs)]
    ppermute x14, starting transfers between devices: 13.8 us -> 5.76 us  [to_left(): return lax.ppermute(x, 'lat', left_pairs)]
    ppermute x15, starting transfers between devices: 18.2 us -> 26 us  [to_right(): return lax.ppermute(x, 'lat', right_pairs)]
  transfers between devices with their start and end apart: 33 -> 33, of which waited for: 18 -> 15; matrix products, arithmetic and copies ran while one was open for 1% -> 1% of each run, Pallas kernels for 28% -> 28%
where the time goes in v7:
time: 177 us
  waiting for transfers between devices  86.3 us (49%)
  Pallas kernels  49.1 us (28%)
  starting transfers between devices  32.5 us (18%)
  matrix products  4.37 us (2%)
  local copies, waits for them, and re-layouts  2.1 us (1%)
    ppermute x15, waiting for transfers between devices, to_right(): return lax.ppermute(x, 'lat', right_pairs)  82 us
    pallas_call x35, Pallas kernels, local_call(): pl.pallas_call(kernel, grid=grid, in_specs=in_specs, out_specs=out_specs,...  49.1 us
    ppermute x15, starting transfers between devices, to_right(): return lax.ppermute(x, 'lat', right_pairs)  26 us
    ppermute x14, starting transfers between devices, to_left(): return lax.ppermute(x, 'lat', left_pairs)  5.76 us
    ppermute x14, waiting for transfers between devices, to_left(): return lax.ppermute(x, 'lat', left_pairs)  3.57 us
  transfers between devices with their start and end apart: 33, of which 15 were waited for; matrix products, arithmetic and copies ran while one was open for 1% of the time, Pallas kernels for 28%

profile of v7, /device:TPU:0, one launch (start us, length us, event | category | flops | bytes accessed | tf_op | source)
XLA Modules:
  0.0 176.6 jit_solution(7215687918619896223)
XLA Ops:
  0.0 3.0 %collective-permute-start.3 = (bf16[128,4096]{1,0:T(8,128)(2,1)}, bf16[128,4096]{1,0:T(8,128)(2,1)S(1)}, u32[]{:S(2)}, u32[]{:S(2)}) collective-permute-start(bf16[128,4096]{1,0:T(8,128)(2,1)} %w_ref.1), channel_id=1, source_target_pairs={{0,4},{4,8},{8,12},{12,14},{14,10},{10,6},{6,2},{2,0},{1,5},{5,9},... | collective-permute-start | bytes 3145736 | tf_op jit(solution)/shard_map/ppermute | solution.py:312
  3.0 2.0 %collective-permute-start.4 = (bf16[1,128]{1,0:T(2,128)(2,1)}, bf16[1,128]{1,0:T(2,128)(2,1)S(1)}, u32[]{:S(2)}, u32[]{:S(2)}) collective-permute-start(bf16[1,128]{1,0:T(2,128)(2,1)} %bitcast.39), channel_id=1, source_target_pairs={{0,4},{4,8},{8,12},{12,14},{14,10},{10,6},{6,2},{2,0},{1,5},{5,9},... | collective-permute-start | bytes 776 | tf_op jit(solution)/shard_map/ppermute | solution.py:312
  5.1 21.3 %collective-permute-done.4.refs_1_ = bf16[1,128]{1,0:T(2,128)(2,1)S(1)} collective-permute-done((bf16[1,128]{1,0:T(2,128)(2,1)}, bf16[1,128]{1,0:T(2,128)(2,1)S(1)}, u32[]{:S(2)}, u32[]{:S(2)}) %collective-permute-start.4) | collective-permute-done | bytes 288 | tf_op jit(solution)/shard_map/ppermute | solution.py:312
  26.4 1.8 %collective-permute-start.5 = (bf16[128,4096]{1,0:T(8,128)(2,1)S(1)}, bf16[128,4096]{1,0:T(8,128)(2,1)}, u32[]{:S(2)}, u32[]{:S(2)}) collective-permute-start(bf16[128,4096]{1,0:T(8,128)(2,1)S(1)} %get-tuple-element.38.refs_0_.refs_2_.w_ref), channel_id=1, source_target_pairs={{0,4},{4,8},{8,12},{12,14},{14,10},{10,6},{6,2},{2,0},{1,5},{5,9},... | collective-permute-start | bytes 3145736 | tf_op jit(solution)/shard_map/ppermute | solution.py:312
  28.9 1.9 %collective-permute-start.6 = (bf16[1,128]{1,0:T(2,128)(2,1)S(1)}, bf16[1,128]{1,0:T(2,128)(2,1)S(1)}, u32[]{:S(2)}, u32[]{:S(2)}) collective-permute-start(bf16[1,128]{1,0:T(2,128)(2,1)S(1)} %get-tuple-element.39.refs_2_), channel_id=1, source_target_pairs={{0,4},{4,8},{8,12},{12,14},{14,10},{10,6},{6,2},{2,0},{1,5},{5,9},... | collective-permute-start | bytes 776 | tf_op jit(solution)/shard_map/ppermute | solution.py:312
  32.3 2.4 %shard_map.57.x_ref = bf16[256,4096]{1,0:T(8,128)(2,1)S(1)} custom-call(bf16[128,4096]{1,0:T(8,128)(2,1)S(1)} %bitcast.38, bf16[128,4096]{1,0:T(8,128)(2,1)} %collective-permute-done.y_ref, bf16[1,4096]{1,0:T(2,128)(2,1)S(1)} %shard_map.56.b_ref), custom_call_target="tpu_custom_call" | custom-call | tf_op jit(solution)/shard_map/pallas_call | solution.py:135
  36.4 1.9 %shard_map.60 = (bf16[256,128]{1,0:T(8,128)(2,1)S(1)}, f32[256,128]{1,0:T(8,128)S(1)}, bf16[256,128]{1,0:T(8,128)(2,1)S(1)}, f32[256,128]{1,0:T(8,128)S(1)}) custom-call(bf16[256,4096]{1,0:T(8,128)(2,1)S(1)} %shard_map.57.x_ref, bf16[128,4096]{1,0:T(8,128)(2,1)S(1)} %get-tuple-element.38.refs_0_.refs_2_.w_ref, ...), custom_call_target="tpu_custom_call" | custom-call | tf_op jit(solution)/shard_map/pallas_call | solution.py:135
  39.8 2.4 %shard_map.62.refs_2_.refs_4_ = f32[256,4096]{1,0:T(8,128)S(1)} custom-call(bf16[256,128]{1,0:T(8,128)(2,1)S(1)} %get-tuple-element.41.refs_0_.c_ref, bf16[256,128]{1,0:T(8,128)(2,1)S(1)} %get-tuple-element.42.refs_1_.c_ref, bf16[128,4096]{1,0:T(8,128)(2,1)S(1)} %get-tuple-element.38.refs_0_.refs_2_.w_ref, ...), custom_call_target="tpu_custom_call", output_to_operand_aliasing={{}: (4, {})} | custom-call | tf_op jit(solution)/shard_map/pallas_call | solution.py:135
  42.3 8.5 %collective-permute-done.6.refs_1_ = bf16[1,128]{1,0:T(2,128)(2,1)S(1)} collective-permute-done((bf16[1,128]{1,0:T(2,128)(2,1)S(1)}, bf16[1,128]{1,0:T(2,128)(2,1)S(1)}, u32[]{:S(2)}, u32[]{:S(2)}) %collective-permute-start.6) | collective-permute-done | bytes 288 | tf_op jit(solution)/shard_map/ppermute | solution.py:312
  54.8 3.3 %shard_map.65 = (bf16[256,128]{1,0:T(8,128)(2,1)S(1)}, f32[256,128]{1,0:T(8,128)S(1)}, bf16[256,128]{1,0:T(8,128)(2,1)S(1)}, f32[256,128]{1,0:T(8,128)S(1)}) custom-call(bf16[256,4096]{1,0:T(8,128)(2,1)S(1)} %shard_map.57.x_ref, bf16[128,4096]{1,0:T(8,128)(2,1)} %get-tuple-element.43.refs_0_.refs_2_.w_ref, ...), custom_call_target="tpu_custom_call" | custom-call | tf_op jit(solution)/shard_map/pallas_call | solution.py:135
  58.2 3.5 %shard_map.66.refs_2_.refs_4_ = f32[256,4096]{1,0:T(8,128)S(1)} custom-call(bf16[256,128]{1,0:T(8,128)(2,1)S(1)} %get-tuple-element.47.refs_0_.c_ref, bf16[256,128]{1,0:T(8,128)(2,1)S(1)} %get-tuple-element.48.refs_1_.c_ref, bf16[128,4096]{1,0:T(8,128)(2,1)} %get-tuple-element.43.refs_0_.refs_2_.w_ref, ...), custom_call_target="tpu_custom_call", output_to_operand_aliasing={{}: (4, {})} | custom-call | tf_op jit(solution)/shard_map/pallas_call | solution.py:135
  61.7 12.7 %collective-permute-done.8.refs_1_ = bf16[1,128]{1,0:T(2,128)(2,1)S(1)} collective-permute-done((bf16[1,128]{1,0:T(2,128)(2,1)S(1)}, bf16[1,128]{1,0:T(2,128)(2,1)S(1)}, u32[]{:S(2)}, u32[]{:S(2)}) %collective-permute-start.8) | collective-permute-done | bytes 288 | tf_op jit(solution)/shard_map/ppermute | solution.py:312
  78.0 1.9 %shard_map.69 = (bf16[256,128]{1,0:T(8,128)(2,1)S(1)}, f32[256,128]{1,0:T(8,128)S(1)}, bf16[256,128]{1,0:T(8,128)(2,1)S(1)}, f32[256,128]{1,0:T(8,128)S(1)}) custom-call(bf16[256,4096]{1,0:T(8,128)(2,1)S(1)} %shard_map.57.x_ref, bf16[128,4096]{1,0:T(8,128)(2,1)S(1)} %get-tuple-element.49.refs_0_.refs_2_.w_ref, ...), custom_call_target="tpu_custom_call" | custom-call | tf_op jit(solution)/shard_map/pallas_call | solution.py:135
  80.0 2.3 %shard_map.70.refs_3_ = bf16[256,4096]{1,0:T(8,128)(2,1)S(1)} custom-call(bf16[256,128]{1,0:T(8,128)(2,1)S(1)} %get-tuple-element.53.refs_0_.c_ref, bf16[256,128]{1,0:T(8,128)(2,1)S(1)} %get-tuple-element.54.refs_1_.c_ref, bf16[128,4096]{1,0:T(8,128)(2,1)S(1)} %get-tuple-element.49.refs_0_.refs_2_.w_ref, ...), custom_call_target="tpu_custom_call" | custom-call | tf_op jit(solution)/shard_map/pallas_call | solution.py:135
  82.5 3.2 %collective-permute-done.16.refs_2_ = bf16[1,128]{1,0:T(2,128)(2,1)S(1)} collective-permute-done((bf16[1,128]{1,0:T(2,128)(2,1)S(1)}, bf16[1,128]{1,0:T(2,128)(2,1)S(1)}, u32[]{:S(2)}, u32[]{:S(2)}) %collective-permute-start.16) | collective-permute-done | bytes 288 | tf_op jit(solution)/shard_map/ppermute | solution.py:312
  92.4 1.6 collective-permute-start.19
  96.0 1.8 %shard_map.77.refs_0_ = f32[128,4096]{1,0:T(8,128)S(1)} custom-call(bf16[256,128]{1,0:T(8,128)(2,1)S(1)} %get-tuple-element.54.refs_1_.c_ref, bf16[256,128]{1,0:T(8,128)(2,1)S(1)} %shard_map.76.s_ref, bf16[256,4096]{1,0:T(8,128)(2,1)S(1)} %add_convert_fusion.e_ref, bf16[256,4096]{1,0:T(8,128)(2,1)S(1)} %shard_map.57.x_ref), custom_call_target="tpu_custom_call" | custom-call | flops 536870912 | bytes 6291456 | tf_op jit(solution)/shard_map/pallas_call | solution.py:135
  98.1 1.6 collective-permute-start.28
  101.2 1.8 %shard_map.89.refs_0_ = f32[128,4096]{1,0:T(8,128)S(1)} custom-call(bf16[256,128]{1,0:T(8,128)(2,1)S(1)} %get-tuple-element.53.refs_0_.c_ref, bf16[256,128]{1,0:T(8,128)(2,1)S(1)} %shard_map.88.s_ref, bf16[256,4096]{1,0:T(8,128)(2,1)S(1)} %add_convert_fusion.e_ref, bf16[256,4096]{1,0:T(8,128)(2,1)S(1)} %shard_map.57.x_ref), custom_call_target="tpu_custom_call" | custom-call | flops 536870912 | bytes 6291456 | tf_op jit(solution)/shard_map/pallas_call | solution.py:135
  104.0 3.3 %collective-permute-done.19.refs_1_ = bf16[64,4096]{1,0:T(8,128)(2,1)S(1)} collective-permute-done((bf16[64,4096]{1,0:T(8,128)(2,1)S(1)}, bf16[64,4096]{1,0:T(8,128)(2,1)S(1)}, u32[]{:S(2)}, u32[]{:S(2)}) %collective-permute-start.19) | collective-permute-done | bytes 524320 | tf_op jit(solution)/shard_map/ppermute | solution.py:312
  111.5 1.8 %shard_map.74.refs_0_ = f32[128,4096]{1,0:T(8,128)S(1)} custom-call(bf16[256,128]{1,0:T(8,128)(2,1)S(1)} %get-tuple-element.48.refs_1_.c_ref, bf16[256,128]{1,0:T(8,128)(2,1)S(1)} %shard_map.73.s_ref, bf16[256,4096]{1,0:T(8,128)(2,1)S(1)} %add_convert_fusion.e_ref, bf16[256,4096]{1,0:T(8,128)(2,1)S(1)} %shard_map.57.x_ref), custom_call_target="tpu_custom_call" | custom-call | flops 536870912 | bytes 6291456 | tf_op jit(solution)/shard_map/pallas_call | solution.py:135
  113.3 5.1 %collective-permute-done.28.refs_1_ = bf16[64,4096]{1,0:T(8,128)(2,1)S(1)} collective-permute-done((bf16[64,4096]{1,0:T(8,128)(2,1)S(1)}, bf16[64,4096]{1,0:T(8,128)(2,1)S(1)}, u32[]{:S(2)}, u32[]{:S(2)}) %collective-permute-start.28) | collective-permute-done | bytes 524320 | tf_op jit(solution)/shard_map/ppermute | solution.py:312
  120.4 3.0 %shard_map.95.s_ref = bf16[256,128]{1,0:T(8,128)(2,1)S(1)} custom-call(bf16[256,4096]{1,0:T(8,128)(2,1)S(1)} %add_convert_fusion.e_ref, bf16[128,4096]{1,0:T(8,128)(2,1)} %get-tuple-element.43.refs_0_.refs_2_.w_ref, f32[256,128]{1,0:T(8,128)S(1)} %shard_map.94.s_ref), custom_call_target="tpu_custom_call" | custom-call | flops 268435456 | bytes 3145728 | tf_op jit(solution)/shard_map/pallas_call | solution.py:135
  123.4 1.8 %shard_map.96.refs_0_ = f32[128,4096]{1,0:T(8,128)S(1)} custom-call(bf16[256,128]{1,0:T(8,128)(2,1)S(1)} %get-tuple-element.47.refs_0_.c_ref, bf16[256,128]{1,0:T(8,128)(2,1)S(1)} %shard_map.95.s_ref, bf16[256,4096]{1,0:T(8,128)(2,1)S(1)} %add_convert_fusion.e_ref, bf16[256,4096]{1,0:T(8,128)(2,1)S(1)} %shard_map.57.x_ref), custom_call_target="tpu_custom_call" | custom-call | flops 536870912 | bytes 6291456 | tf_op jit(solution)/shard_map/pallas_call | solution.py:135
  126.1 3.6 %collective-permute-done.20.refs_1_ = bf16[64,4096]{1,0:T(8,128)(2,1)S(1)} collective-permute-done((bf16[64,4096]{1,0:T(8,128)(2,1)S(1)}, bf16[64,4096]{1,0:T(8,128)(2,1)S(1)}, u32[]{:S(2)}, u32[]{:S(2)}) %collective-permute-start.20) | collective-permute-done | bytes 524320 | tf_op jit(solution)/shard_map/ppermute | solution.py:312
  134.0 1.8 %shard_map.85.refs_0_ = f32[128,4096]{1,0:T(8,128)S(1)} custom-call(bf16[256,128]{1,0:T(8,128)(2,1)S(1)} %get-tuple-element.42.refs_1_.c_ref, bf16[256,128]{1,0:T(8,128)(2,1)S(1)} %shard_map.84.s_ref, bf16[256,4096]{1,0:T(8,128)(2,1)S(1)} %add_convert_fusion.e_ref, bf16[256,4096]{1,0:T(8,128)(2,1)S(1)} %shard_map.57.x_ref), custom_call_target="tpu_custom_call" | custom-call | flops 536870912 | bytes 6291456 | tf_op jit(solution)/shard_map/pallas_call | solution.py:135
  135.8 5.2 %collective-permute-done.29.refs_1_ = bf16[64,4096]{1,0:T(8,128)(2,1)S(1)} collective-permute-done((bf16[64,4096]{1,0:T(8,128)(2,1)S(1)}, bf16[64,4096]{1,0:T(8,128)(2,1)S(1)}, u32[]{:S(2)}, u32[]{:S(2)}) %collective-permute-start.29) | collective-permute-done | bytes 524320 | tf_op jit(solution)/shard_map/ppermute | solution.py:312
  144.4 1.8 %shard_map.93.refs_0_ = f32[128,4096]{1,0:T(8,128)S(1)} custom-call(bf16[256,128]{1,0:T(8,128)(2,1)S(1)} %get-tuple-element.41.refs_0_.c_ref, bf16[256,128]{1,0:T(8,128)(2,1)S(1)} %shard_map.92.s_ref, bf16[256,4096]{1,0:T(8,128)(2,1)S(1)} %add_convert_fusion.e_ref, bf16[256,4096]{1,0:T(8,128)(2,1)S(1)} %shard_map.57.x_ref), custom_call_target="tpu_custom_call" | custom-call | flops 536870912 | bytes 6291456 | tf_op jit(solution)/shard_map/pallas_call | solution.py:135
  147.1 5.1 %collective-permute-done.21.refs_1_ = bf16[64,4096]{1,0:T(8,128)(2,1)S(1)} collective-permute-done((bf16[64,4096]{1,0:T(8,128)(2,1)S(1)}, bf16[64,4096]{1,0:T(8,128)(2,1)S(1)}, u32[]{:S(2)}, u32[]{:S(2)}) %collective-permute-start.21) | collective-permute-done | bytes 524320 | tf_op jit(solution)/shard_map/ppermute | solution.py:312
  156.5 1.8 %shard_map.82 = f32[128,4096]{1,0:T(8,128)S(1)} custom-call(bf16[256,128]{1,0:T(8,128)(2,1)S(1)} %get-tuple-element.37.refs_0_.c_ref, bf16[256,128]{1,0:T(8,128)(2,1)S(1)} %shard_map.81.s_ref, bf16[256,4096]{1,0:T(8,128)(2,1)S(1)} %add_convert_fusion.e_ref, bf16[256,4096]{1,0:T(8,128)(2,1)S(1)} %shard_map.57.x_ref), custom_call_target="tpu_custom_call" | custom-call | flops 536870912 | bytes 6291456 | tf_op jit(solution)/shard_map/pallas_call | solution.py:135
  158.3 5.2 %collective-permute-done.30 = bf16[64,4096]{1,0:T(8,128)(2,1)S(1)} collective-permute-done((bf16[64,4096]{1,0:T(8,128)(2,1)S(1)}, bf16[64,4096]{1,0:T(8,128)(2,1)S(1)}, u32[]{:S(2)}, u32[]{:S(2)}) %collective-permute-start.30) | collective-permute-done | bytes 524320 | tf_op jit(solution)/shard_map/ppermute | solution.py:312
  165.0 8.8 %collective-permute-done.22 = bf16[64,4096]{1,0:T(8,128)(2,1)S(1)} collective-permute-done((bf16[64,4096]{1,0:T(8,128)(2,1)S(1)}, bf16[64,4096]{1,0:T(8,128)(2,1)S(1)}, u32[]{:S(2)}, u32[]{:S(2)}) %collective-permute-start.22) | collective-permute-done | bytes 524320 | tf_op jit(solution)/shard_map/ppermute | solution.py:312
  (121 shorter events, 48.7 us)
Async XLA Ops:
  0.0 26.4 %collective-permute-start.3 = (bf16[128,4096]{1,0:T(8,128)(2,1)}, bf16[128,4096]{1,0:T(8,128)(2,1)S(1)}, u32[]{:S(2)}, u32[]{:S(2)}) collective-permute-start(bf16[128,4096]{1,0:T(8,128)(2,1)} %w_ref.1), channel_id=1, source_target_pairs={{0,4},{4,8},{8,12},{12,14},{14,10},{10,6},{6,2},{2,0},{1,5},{5,9},... | collective-permute-start | bytes 3145736 | tf_op jit(solution)/shard_map/ppermute | solution.py:312
  3.0 25.2 %collective-permute-start.1 = (bf16[128,4096]{1,0:T(8,128)(2,1)}, bf16[128,4096]{1,0:T(8,128)(2,1)S(1)}, u32[]{:S(2)}, u32[]{:S(2)}) collective-permute-start(bf16[128,4096]{1,0:T(8,128)(2,1)} %w_ref.1), channel_id=1, source_target_pairs={{4,0},{8,4},{12,8},{14,12},{10,14},{6,10},{2,6},{0,2},{5,1},{9,5},... | collective-permute-start | bytes 3145736 | tf_op jit(solution)/shard_map/ppermute | solution.py:315
  3.0 28.0 %collective-permute-start = (bf16[128,4096]{1,0:T(8,128)(2,1)}, bf16[128,4096]{1,0:T(8,128)(2,1)}, u32[]{:S(2)}, u32[]{:S(2)}) collective-permute-start(bf16[128,4096]{1,0:T(8,128)(2,1)} %bitcast.37), channel_id=1, source_target_pairs={{0,1},{1,0},{2,3},{3,2},{4,5},{5,4},{6,7},{7,6},{8,9},{9,8},{10,11... | collective-permute-start | bytes 3145736 | tf_op jit(solution)/shard_map/ppermute | solution.py:318
  3.0 23.3 %collective-permute-start.4 = (bf16[1,128]{1,0:T(2,128)(2,1)}, bf16[1,128]{1,0:T(2,128)(2,1)S(1)}, u32[]{:S(2)}, u32[]{:S(2)}) collective-permute-start(bf16[1,128]{1,0:T(2,128)(2,1)} %bitcast.39), channel_id=1, source_target_pairs={{0,4},{4,8},{8,12},{12,14},{14,10},{10,6},{6,2},{2,0},{1,5},{5,9},... | collective-permute-start | bytes 776 | tf_op jit(solution)/shard_map/ppermute | solution.py:312
  5.1 23.2 %collective-permute-start.2 = (bf16[1,128]{1,0:T(2,128)(2,1)}, bf16[1,128]{1,0:T(2,128)(2,1)S(1)}, u32[]{:S(2)}, u32[]{:S(2)}) collective-permute-start(bf16[1,128]{1,0:T(2,128)(2,1)} %bitcast.40), channel_id=1, source_target_pairs={{4,0},{8,4},{12,8},{14,12},{10,14},{6,10},{2,6},{0,2},{5,1},{9,5},... | collective-permute-start | bytes 776 | tf_op jit(solution)/shard_map/ppermute | solution.py:315
  26.4 24.4 %collective-permute-start.5 = (bf16[128,4096]{1,0:T(8,128)(2,1)S(1)}, bf16[128,4096]{1,0:T(8,128)(2,1)}, u32[]{:S(2)}, u32[]{:S(2)}) collective-permute-start(bf16[128,4096]{1,0:T(8,128)(2,1)S(1)} %get-tuple-element.38.refs_0_.refs_2_.w_ref), channel_id=1, source_target_pairs={{0,4},{4,8},{8,12},{12,14},{14,10},{10,6},{6,2},{2,0},{1,5},{5,9},... | collective-permute-start | bytes 3145736 | tf_op jit(solution)/shard_map/ppermute | solution.py:312
  28.2 24.1 %collective-permute-start.9 = (bf16[128,4096]{1,0:T(8,128)(2,1)S(1)}, bf16[128,4096]{1,0:T(8,128)(2,1)S(1)}, u32[]{:S(2)}, u32[]{:S(2)}) collective-permute-start(bf16[128,4096]{1,0:T(8,128)(2,1)S(1)} %get-tuple-element.36.refs_1_.refs_3_.w_ref), channel_id=1, source_target_pairs={{4,0},{8,4},{12,8},{14,12},{10,14},{6,10},{2,6},{0,2},{5,1},{9,5},... | collective-permute-start | bytes 3145736 | tf_op jit(solution)/shard_map/ppermute | solution.py:315
  28.9 21.9 %collective-permute-start.6 = (bf16[1,128]{1,0:T(2,128)(2,1)S(1)}, bf16[1,128]{1,0:T(2,128)(2,1)S(1)}, u32[]{:S(2)}, u32[]{:S(2)}) collective-permute-start(bf16[1,128]{1,0:T(2,128)(2,1)S(1)} %get-tuple-element.39.refs_2_), channel_id=1, source_target_pairs={{0,4},{4,8},{8,12},{12,14},{14,10},{10,6},{6,2},{2,0},{1,5},{5,9},... | collective-permute-start | bytes 776 | tf_op jit(solution)/shard_map/ppermute | solution.py:312
  30.8 21.5 %collective-permute-start.10 = (bf16[1,128]{1,0:T(2,128)(2,1)S(1)}, bf16[1,128]{1,0:T(2,128)(2,1)S(1)}, u32[]{:S(2)}, u32[]{:S(2)}) collective-permute-start(bf16[1,128]{1,0:T(2,128)(2,1)S(1)} %get-tuple-element.40.refs_3_), channel_id=1, source_target_pairs={{4,0},{8,4},{12,8},{14,12},{10,14},{6,10},{2,6},{0,2},{5,1},{9,5},... | collective-permute-start | bytes 776 | tf_op jit(solution)/shard_map/ppermute | solution.py:315
  50.8 23.6 %collective-permute-start.7 = (bf16[128,4096]{1,0:T(8,128)(2,1)}, bf16[128,4096]{1,0:T(8,128)(2,1)S(1)}, u32[]{:S(2)}, u32[]{:S(2)}) collective-permute-start(bf16[128,4096]{1,0:T(8,128)(2,1)} %get-tuple-element.43.refs_0_.refs_2_.w_ref), channel_id=1, source_target_pairs={{0,4},{4,8},{8,12},{12,14},{14,10},{10,6},{6,2},{2,0},{1,5},{5,9},... | collective-permute-start | bytes 3145736 | tf_op jit(solution)/shard_map/ppermute | solution.py:312
  52.3 23.6 %collective-permute-start.11 = (bf16[128,4096]{1,0:T(8,128)(2,1)S(1)}, bf16[128,4096]{1,0:T(8,128)(2,1)S(1)}, u32[]{:S(2)}, u32[]{:S(2)}) collective-permute-start(bf16[128,4096]{1,0:T(8,128)(2,1)S(1)} %get-tuple-element.45.refs_1_.refs_3_.w_ref), channel_id=1, source_target_pairs={{4,0},{8,4},{12,8},{14,12},{10,14},{6,10},{2,6},{0,2},{5,1},{9,5},... | collective-permute-start | bytes 3145736 | tf_op jit(solution)/shard_map/ppermute | solution.py:315
  52.8 21.6 %collective-permute-start.8 = (bf16[1,128]{1,0:T(2,128)(2,1)S(1)}, bf16[1,128]{1,0:T(2,128)(2,1)S(1)}, u32[]{:S(2)}, u32[]{:S(2)}) collective-permute-start(bf16[1,128]{1,0:T(2,128)(2,1)S(1)} %get-tuple-element.44.refs_2_), channel_id=1, source_target_pairs={{0,4},{4,8},{8,12},{12,14},{14,10},{10,6},{6,2},{2,0},{1,5},{5,9},... | collective-permute-start | bytes 776 | tf_op jit(solution)/shard_map/ppermute | solution.py:312
  54.3 21.6 %collective-permute-start.12 = (bf16[1,128]{1,0:T(2,128)(2,1)S(1)}, bf16[1,128]{1,0:T(2,128)(2,1)S(1)}, u32[]{:S(2)}, u32[]{:S(2)}) collective-permute-start(bf16[1,128]{1,0:T(2,128)(2,1)S(1)} %get-tuple-element.46.refs_3_), channel_id=1, source_target_pairs={{4,0},{8,4},{12,8},{14,12},{10,14},{6,10},{2,6},{0,2},{5,1},{9,5},... | collective-permute-start | bytes 776 | tf_op jit(solution)/shard_map/ppermute | solution.py:315
  74.5 11.3 %collective-permute-start.14 = (bf16[64,4096]{1,0:T(8,128)(2,1)S(1)}, bf16[64,4096]{1,0:T(8,128)(2,1)S(1)}, u32[]{:S(2)}, u32[]{:S(2)}) collective-permute-start(bf16[64,4096]{1,0:T(8,128)(2,1)S(1)} %slice.36), channel_id=1, source_target_pairs={{0,4},{4,8},{8,12},{12,14},{14,10},{10,6},{6,2},{2,0},{1,5},{5,9},... | collective-permute-start | bytes 1572872 | tf_op jit(solution)/shard_map/ppermute | solution.py:312
  75.9 10.4 %collective-permute-start.15 = (bf16[64,4096]{1,0:T(8,128)(2,1)S(1)}, bf16[64,4096]{1,0:T(8,128)(2,1)S(1)}, u32[]{:S(2)}, u32[]{:S(2)}) collective-permute-start(bf16[64,4096]{1,0:T(8,128)(2,1)S(1)} %slice.37), channel_id=1, source_target_pairs={{4,0},{8,4},{12,8},{14,12},{10,14},{6,10},{2,6},{0,2},{5,1},{9,5},... | collective-permute-start | bytes 1572872 | tf_op jit(solution)/shard_map/ppermute | solution.py:315
  76.6 9.1 %collective-permute-start.16 = (bf16[1,128]{1,0:T(2,128)(2,1)S(1)}, bf16[1,128]{1,0:T(2,128)(2,1)S(1)}, u32[]{:S(2)}, u32[]{:S(2)}) collective-permute-start(bf16[1,128]{1,0:T(2,128)(2,1)S(1)} %get-tuple-element.51.refs_2_), channel_id=1, source_target_pairs={{0,4},{4,8},{8,12},{12,14},{14,10},{10,6},{6,2},{2,0},{1,5},{5,9},... | collective-permute-start | bytes 776 | tf_op jit(solution)/shard_map/ppermute | solution.py:312
  82.3 7.0 %collective-permute-start.13 = (bf16[256,4096]{1,0:T(8,128)(2,1)S(1)}, bf16[256,4096]{1,0:T(8,128)(2,1)S(1)}, u32[]{:S(2)}, u32[]{:S(2)}) collective-permute-start(bf16[256,4096]{1,0:T(8,128)(2,1)S(1)} %shard_map.70.refs_3_), channel_id=1, source_target_pairs={{0,1},{1,0},{2,3},{3,2},{4,5},{5,4},{6,7},{7,6},{8,9},{9,8},{10,11... | collective-permute-start | bytes 6291464 | tf_op jit(solution)/shard_map/ppermute | solution.py:318
  86.4 3.0 %collective-permute-start.18 = (bf16[128,4096]{1,0:T(8,128)(2,1)S(1)}, bf16[128,4096]{1,0:T(8,128)(2,1)S(1)}, u32[]{:S(2)}, u32[]{:S(2)}) collective-permute-start(bf16[128,4096]{1,0:T(8,128)(2,1)S(1)} %constant_dynamic-update-slice_fusion), channel_id=1, source_target_pairs={{0,1},{1,0},{2,3},{3,2},{4,5},{5,4},{6,7},{7,6},{8,9},{9,8},{10,11... | collective-permute-start | bytes 3145736 | tf_op jit(solution)/shard_map/ppermute | solution.py:318
  92.4 14.8 %collective-permute-start.19 = (bf16[64,4096]{1,0:T(8,128)(2,1)S(1)}, bf16[64,4096]{1,0:T(8,128)(2,1)S(1)}, u32[]{:S(2)}, u32[]{:S(2)}) collective-permute-start(bf16[64,4096]{1,0:T(8,128)(2,1)S(1)} %get-tuple-element.72), channel_id=1, source_target_pairs={{0,4},{4,8},{8,12},{12,14},{14,10},{10,6},{6,2},{2,0},{1,5},{5,9},... | collective-permute-start | bytes 1572872 | tf_op jit(solution)/shard_map/ppermute | solution.py:312
  94.1 15.1 %collective-permute-start.23 = (bf16[64,4096]{1,0:T(8,128)(2,1)S(1)}, bf16[64,4096]{1,0:T(8,128)(2,1)S(1)}, u32[]{:S(2)}, u32[]{:S(2)}) collective-permute-start(bf16[64,4096]{1,0:T(8,128)(2,1)S(1)} %get-tuple-element.71), channel_id=1, source_target_pairs={{4,0},{8,4},{12,8},{14,12},{10,14},{6,10},{2,6},{0,2},{5,1},{9,5},... | collective-permute-start | bytes 1572872 | tf_op jit(solution)/shard_map/ppermute | solution.py:315
  98.1 20.4 %collective-permute-start.28 = (bf16[64,4096]{1,0:T(8,128)(2,1)S(1)}, bf16[64,4096]{1,0:T(8,128)(2,1)S(1)}, u32[]{:S(2)}, u32[]{:S(2)}) collective-permute-start(bf16[64,4096]{1,0:T(8,128)(2,1)S(1)} %shard_map.100), channel_id=1, source_target_pairs={{0,4},{4,8},{8,12},{12,14},{14,10},{10,6},{6,2},{2,0},{1,5},{5,9},... | collective-permute-start | bytes 1572872 | tf_op jit(solution)/shard_map/ppermute | solution.py:312
  103.3 21.9 %collective-permute-start.25 = (bf16[64,4096]{1,0:T(8,128)(2,1)S(1)}, bf16[64,4096]{1,0:T(8,128)(2,1)S(1)}, u32[]{:S(2)}, u32[]{:S(2)}) collective-permute-start(bf16[64,4096]{1,0:T(8,128)(2,1)S(1)} %shard_map.97), channel_id=1, source_target_pairs={{4,0},{8,4},{12,8},{14,12},{10,14},{6,10},{2,6},{0,2},{5,1},{9,5},... | collective-permute-start | bytes 1572872 | tf_op jit(solution)/shard_map/ppermute | solution.py:315
  107.6 22.1 %collective-permute-start.20 = (bf16[64,4096]{1,0:T(8,128)(2,1)S(1)}, bf16[64,4096]{1,0:T(8,128)(2,1)S(1)}, u32[]{:S(2)}, u32[]{:S(2)}) collective-permute-start(bf16[64,4096]{1,0:T(8,128)(2,1)S(1)} %shard_map.78), channel_id=1, source_target_pairs={{0,4},{4,8},{8,12},{12,14},{14,10},{10,6},{6,2},{2,0},{1,5},{5,9},... | collective-permute-start | bytes 1572872 | tf_op jit(solution)/shard_map/ppermute | solution.py:312
  109.5 22.1 %collective-permute-start.24 = (bf16[64,4096]{1,0:T(8,128)(2,1)S(1)}, bf16[64,4096]{1,0:T(8,128)(2,1)S(1)}, u32[]{:S(2)}, u32[]{:S(2)}) collective-permute-start(bf16[64,4096]{1,0:T(8,128)(2,1)S(1)} %shard_map.90), channel_id=1, source_target_pairs={{4,0},{8,4},{12,8},{14,12},{10,14},{6,10},{2,6},{0,2},{5,1},{9,5},... | collective-permute-start | bytes 1572872 | tf_op jit(solution)/shard_map/ppermute | solution.py:315
  118.8 22.1 %collective-permute-start.29 = (bf16[64,4096]{1,0:T(8,128)(2,1)S(1)}, bf16[64,4096]{1,0:T(8,128)(2,1)S(1)}, u32[]{:S(2)}, u32[]{:S(2)}) collective-permute-start(bf16[64,4096]{1,0:T(8,128)(2,1)S(1)} %shard_map.101), channel_id=1, source_target_pairs={{0,4},{4,8},{8,12},{12,14},{14,10},{10,6},{6,2},{2,0},{1,5},{5,9},... | collective-permute-start | bytes 1572872 | tf_op jit(solution)/shard_map/ppermute | solution.py:312
  125.6 20.6 %collective-permute-start.26 = (bf16[64,4096]{1,0:T(8,128)(2,1)S(1)}, bf16[64,4096]{1,0:T(8,128)(2,1)S(1)}, u32[]{:S(2)}, u32[]{:S(2)}) collective-permute-start(bf16[64,4096]{1,0:T(8,128)(2,1)S(1)} %shard_map.98), channel_id=1, source_target_pairs={{4,0},{8,4},{12,8},{14,12},{10,14},{6,10},{2,6},{0,2},{5,1},{9,5},... | collective-permute-start | bytes 1572872 | tf_op jit(solution)/shard_map/ppermute | solution.py:315
  130.0 22.1 %collective-permute-start.21 = (bf16[64,4096]{1,0:T(8,128)(2,1)S(1)}, bf16[64,4096]{1,0:T(8,128)(2,1)S(1)}, u32[]{:S(2)}, u32[]{:S(2)}) collective-permute-start(bf16[64,4096]{1,0:T(8,128)(2,1)S(1)} %shard_map.79), channel_id=1, source_target_pairs={{0,4},{4,8},{8,12},{12,14},{14,10},{10,6},{6,2},{2,0},{1,5},{5,9},... | collective-permute-start | bytes 1572872 | tf_op jit(solution)/shard_map/ppermute | solution.py:312
  132.0 22.1 %collective-permute-start.31 = (bf16[64,4096]{1,0:T(8,128)(2,1)S(1)}, bf16[64,4096]{1,0:T(8,128)(2,1)S(1)}, u32[]{:S(2)}, u32[]{:S(2)}) collective-permute-start(bf16[64,4096]{1,0:T(8,128)(2,1)S(1)} %shard_map.103), channel_id=1, source_target_pairs={{4,0},{8,4},{12,8},{14,12},{10,14},{6,10},{2,6},{0,2},{5,1},{9,5},... | collective-permute-start | bytes 1572872 | tf_op jit(solution)/shard_map/ppermute | solution.py:315
  141.3 22.1 %collective-permute-start.30 = (bf16[64,4096]{1,0:T(8,128)(2,1)S(1)}, bf16[64,4096]{1,0:T(8,128)(2,1)S(1)}, u32[]{:S(2)}, u32[]{:S(2)}) collective-permute-start(bf16[64,4096]{1,0:T(8,128)(2,1)S(1)} %shard_map.102), channel_id=1, source_target_pairs={{0,4},{4,8},{8,12},{12,14},{14,10},{10,6},{6,2},{2,0},{1,5},{5,9},... | collective-permute-start | bytes 1572872 | tf_op jit(solution)/shard_map/ppermute | solution.py:312
  146.6 18.5 %collective-permute-start.27 = (bf16[64,4096]{1,0:T(8,128)(2,1)S(1)}, bf16[64,4096]{1,0:T(8,128)(2,1)S(1)}, u32[]{:S(2)}, u32[]{:S(2)}) collective-permute-start(bf16[64,4096]{1,0:T(8,128)(2,1)S(1)} %shard_map.99), channel_id=1, source_target_pairs={{4,0},{8,4},{12,8},{14,12},{10,14},{6,10},{2,6},{0,2},{5,1},{9,5},... | collective-permute-start | bytes 1572872 | tf_op jit(solution)/shard_map/ppermute | solution.py:315
  152.5 21.3 %collective-permute-start.22 = (bf16[64,4096]{1,0:T(8,128)(2,1)S(1)}, bf16[64,4096]{1,0:T(8,128)(2,1)S(1)}, u32[]{:S(2)}, u32[]{:S(2)}) collective-permute-start(bf16[64,4096]{1,0:T(8,128)(2,1)S(1)} %shard_map.86), channel_id=1, source_target_pairs={{0,4},{4,8},{8,12},{12,14},{14,10},{10,6},{6,2},{2,0},{1,5},{5,9},... | collective-permute-start | bytes 1572872 | tf_op jit(solution)/shard_map/ppermute | solution.py:312
  154.5 20.7 %collective-permute-start.32 = (bf16[64,4096]{1,0:T(8,128)(2,1)S(1)}, bf16[64,4096]{1,0:T(8,128)(2,1)S(1)}, u32[]{:S(2)}, u32[]{:S(2)}) collective-permute-start(bf16[64,4096]{1,0:T(8,128)(2,1)S(1)} %shard_map.104), channel_id=1, source_target_pairs={{4,0},{8,4},{12,8},{14,12},{10,14},{6,10},{2,6},{0,2},{5,1},{9,5},... | collective-permute-start | bytes 1572872 | tf_op jit(solution)/shard_map/ppermute | solution.py:315
  (6 other events, 68.5 us)

commit v8 on v7

--- a/solution.py
+++ b/solution.py
@@ -8,7 +8,7 @@
 from jax.sharding import PartitionSpec as P
 
 GATHER_LIMIT = 32 * 2**20
-TILES = 4
+TILES = 2
 
 
 def slot_tables(lists, block_count, slot_count):
@@ -153,18 +153,21 @@
     return pl.BlockSpec((x.shape[0], tile), lambda i: (0, i))
 
 
-def centre(mine, theirs, dec_bias):
+def centre(mine, theirs, dec_bias, first):
     count, width = mine.shape
 
-    def kernel(x_ref, y_ref, b_ref, o_ref):
+    def kernel(x_ref, y_ref, b_ref, f_ref, o_ref):
         shift = b_ref[...].astype(jnp.float32)
-        o_ref[:count, :] = (x_ref[...].astype(jnp.float32) - shift).astype(o_ref.dtype)
-        o_ref[count:, :] = (y_ref[...].astype(jnp.float32) - shift).astype(o_ref.dtype)
+        x, y = (r[...].astype(jnp.float32) - shift for r in (x_ref, y_ref))
+        mask = f_ref[:, :1] > 0
+        o_ref[:count, :] = jnp.where(mask, x, y).astype(o_ref.dtype)
+        o_ref[count:, :] = jnp.where(mask, y, x).astype(o_ref.dtype)
 
     tile = width // TILES
     out = jax.ShapeDtypeStruct((2 * count, width), jnp.bfloat16)
-    args = (mine, theirs, dec_bias)
-    return local_call(kernel, (TILES,), [columns(x, tile) for x in args], columns(out, tile), out, args)
+    args = (mine, theirs, dec_bias, first)
+    specs = [columns(x, tile) for x in args[:3]] + [whole(first)]
+    return local_call(kernel, (TILES,), specs, columns(out, tile), out, args)
 
 
 def product(x, y, dims):
@@ -321,8 +324,8 @@
         at = (place + step + count) % count
         return jnp.where(at < half, 2 * at, 2 * (count - 1 - at) + 1)
 
-    lists = act_blocks.reshape(2, half_blocks, act_blocks.shape[1])
-    lists = jnp.where(row_index == 0, lists, lists[::-1]).reshape(2 * half_blocks, -1)
+    lists = act_blocks
+    core_0 = jnp.broadcast_to((row_index == 0).astype(jnp.float32), (1, 128))
     steps = [0] + [s for t in range(1, half) for s in (-t, t)] + [half]
     owners = jnp.stack([owner(s) for s in steps])
     listed = jnp.any(lists[:, :, None] == owners, axis=1).astype(jnp.float32)
@@ -338,10 +341,15 @@
         small = to_right(biases[1 - t]), to_left(biases[t - 1])
         tokens = () if rebuilt is None else (rebuilt,)
         words[-t], biases[-t] = after((arrived[0], small[0]), *tokens)
-        words[t], biases[t] = after((arrived[1], small[1]), *tokens)
+        if t < half - 1:
+            words[t], biases[t] = after((arrived[1], small[1]), *tokens)
+        else:
+            opposite = [(order[i], order[(i + half) % count]) for i in range(count)]
+            far_bias = lax.ppermute(biases[0], "lat", opposite)
+            words[t], biases[t], biases[half] = after((arrived[1], small[1], far_bias), *tokens)
         if t == 1:
             (shift,) = after((dec_bias.reshape(1, width),), words[1])
-            rows = centre(acts, to_core(acts), shift)
+            rows = centre(acts, to_core(acts), shift, core_0)
         for group in ((-t, t),) if t > 1 else ((0,), (-t, t)):
             blocks = [words[step] for step in group]
             shifts = [biases[step] for step in group]
@@ -351,10 +359,9 @@
             dtype = jnp.bfloat16 if t == half - 1 and group[-1] == t else jnp.float32
             rebuilt = decode([codes[step] for step in group], blocks, rebuilt, dtype)
 
-    middle = half_blocks * rows_each
     swapped = to_core(rebuilt)
     last = to_right(words[1 - half][:cut]), to_left(words[half - 1][cut:])
-    *last, biases[half] = after((*last, to_right(biases[1 - half])), rebuilt)
+    last = after(last, rebuilt)
     words[half] = jnp.concatenate(last)
     other_words = to_core(words[half])
     preacts = jnp.einsum("rd,ld->rl", rows, words[half], preferred_element_type=jnp.float32)
@@ -365,12 +372,9 @@
     codes[half], sigmas[half] = lax.optimization_barrier((code, sigma))
     other_codes = to_core(codes[half])
 
-    def in_my_order(x):
-        return jnp.concatenate([x[middle:], x[:middle]])
-
-    errors = rebuilt.astype(jnp.float32) + in_my_order(swapped).astype(jnp.float32)
+    errors = rebuilt.astype(jnp.float32) + swapped.astype(jnp.float32)
     errors = errors - rows.astype(jnp.float32)
-    for code, word in ((codes[half], words[half]), (in_my_order(other_codes), other_words)):
+    for code, word in ((codes[half], words[half]), (other_codes, other_words)):
         errors = errors + jnp.einsum("rl,ld->rd", code, word, preferred_element_type=jnp.float32)
     errors = errors.astype(jnp.bfloat16)
 
@@ -395,11 +399,9 @@
         up = tuple(to_right(join(ahead, came, k)) for k, came in enumerate(up))
         down = tuple(to_left(join(behind, came, k)) for k, came in enumerate(down))
     mine = grads_of(0, tokens[0])
-    parts = []
-    for k in range(2):
-        part = mine[k * cut : (k + 1) * cut] + up[k].astype(jnp.float32) + down[k].astype(jnp.float32)
-        parts.append(part / block_rows)
-    return jnp.concatenate(parts).astype(jnp.bfloat16)
+    for came in (up, down):
+        mine = mine + jnp.concatenate(came).astype(jnp.float32)
+    return (mine / block_rows).astype(jnp.bfloat16)
 
 
 def solution(mesh):

time: 177 us -> 177 us (level)
  Pallas kernels: 49.1 us -> 38.7 us
  waiting for transfers between devices: 86.3 us -> 93.2 us
  starting transfers between devices: 32.5 us -> 36.6 us
    ppermute x15 -> x14, starting transfers between devices: 26 us -> 14.8 us  [to_right(): return lax.ppermute(x, 'lat', right_pairs)]
    ppermute x14, starting transfers between devices: 5.76 us -> 16.6 us  [to_left(): return lax.ppermute(x, 'lat', left_pairs)]
    pallas_call x35, Pallas kernels: 49.1 us -> 38.7 us  [local_call(): pl.pallas_call(kernel, grid=grid, in_specs=in_specs, out_specs=out_specs,...]
    ppermute x15 -> x14, waiting for transfers between devices: 82 us -> 88.8 us  [to_right(): return lax.ppermute(x, 'lat', right_pairs)]
    ppermute x0 -> x1, starting transfers between devices: none -> 4.46 us  [ring_body(): far_bias = lax.ppermute(biases[0], 'lat', opposite)]
  transfers between devices with their start and end apart: 33 -> 33, of which waited for: 15 -> 16; matrix products, arithmetic and copies ran while one was open for 1% -> 1% of each run, Pallas kernels for 28% -> 22%
where the time goes in v8:
time: 177 us
  waiting for transfers between devices  93.2 us (53%)
  Pallas kernels  38.7 us (22%)
  starting transfers between devices  36.6 us (21%)
  matrix products  4.34 us (2%)
    ppermute x14, waiting for transfers between devices, to_right(): return lax.ppermute(x, 'lat', right_pairs)  88.8 us
    pallas_call x35, Pallas kernels, local_call(): pl.pallas_call(kernel, grid=grid, in_specs=in_specs, out_specs=out_specs,...  38.7 us
    ppermute x14, starting transfers between devices, to_left(): return lax.ppermute(x, 'lat', left_pairs)  16.6 us
    ppermute x14, starting transfers between devices, to_right(): return lax.ppermute(x, 'lat', right_pairs)  14.8 us
    ppermute x1, starting transfers between devices, ring_body(): far_bias = lax.ppermute(biases[0], 'lat', opposite)  4.46 us
  transfers between devices with their start and end apart: 33, of which 16 were waited for; matrix products, arithmetic and copies ran while one was open for 1% of the time, Pallas kernels for 22%

profile of v8, /device:TPU:0, one launch (start us, length us, event | category | flops | bytes accessed | tf_op | source)
XLA Modules:
  0.0 176.6 jit_solution(1906339016418713810)
XLA Ops:
  0.0 3.0 %collective-permute-start.3 = (bf16[128,4096]{1,0:T(8,128)(2,1)}, bf16[128,4096]{1,0:T(8,128)(2,1)S(1)}, u32[]{:S(2)}, u32[]{:S(2)}) collective-permute-start(bf16[128,4096]{1,0:T(8,128)(2,1)} %w_ref.1), channel_id=1, source_target_pairs={{0,4},{4,8},{8,12},{12,14},{14,10},{10,6},{6,2},{2,0},{1,5},{5,9},... | collective-permute-start | bytes 3145736 | tf_op jit(solution)/shard_map/ppermute | solution.py:315
  3.0 2.0 %collective-permute-start.4 = (bf16[1,128]{1,0:T(2,128)(2,1)}, bf16[1,128]{1,0:T(2,128)(2,1)S(1)}, u32[]{:S(2)}, u32[]{:S(2)}) collective-permute-start(bf16[1,128]{1,0:T(2,128)(2,1)} %bitcast.33), channel_id=1, source_target_pairs={{0,4},{4,8},{8,12},{12,14},{14,10},{10,6},{6,2},{2,0},{1,5},{5,9},... | collective-permute-start | bytes 776 | tf_op jit(solution)/shard_map/ppermute | solution.py:315
  5.1 21.3 %collective-permute-done.4.refs_1_ = bf16[1,128]{1,0:T(2,128)(2,1)S(1)} collective-permute-done((bf16[1,128]{1,0:T(2,128)(2,1)}, bf16[1,128]{1,0:T(2,128)(2,1)S(1)}, u32[]{:S(2)}, u32[]{:S(2)}) %collective-permute-start.4) | collective-permute-done | bytes 288 | tf_op jit(solution)/shard_map/ppermute | solution.py:315
  26.4 1.8 %collective-permute-start.5 = (bf16[128,4096]{1,0:T(8,128)(2,1)S(1)}, bf16[128,4096]{1,0:T(8,128)(2,1)}, u32[]{:S(2)}, u32[]{:S(2)}) collective-permute-start(bf16[128,4096]{1,0:T(8,128)(2,1)S(1)} %get-tuple-element.38.refs_0_.refs_2_.w_ref), channel_id=1, source_target_pairs={{0,4},{4,8},{8,12},{12,14},{14,10},{10,6},{6,2},{2,0},{1,5},{5,9},... | collective-permute-start | bytes 3145736 | tf_op jit(solution)/shard_map/ppermute | solution.py:315
  28.7 1.9 %collective-permute-start.6 = (bf16[1,128]{1,0:T(2,128)(2,1)S(1)}, bf16[1,128]{1,0:T(2,128)(2,1)S(1)}, u32[]{:S(2)}, u32[]{:S(2)}) collective-permute-start(bf16[1,128]{1,0:T(2,128)(2,1)S(1)} %get-tuple-element.39.refs_2_), channel_id=1, source_target_pairs={{0,4},{4,8},{8,12},{12,14},{14,10},{10,6},{6,2},{2,0},{1,5},{5,9},... | collective-permute-start | bytes 776 | tf_op jit(solution)/shard_map/ppermute | solution.py:315
  32.0 2.3 %shard_map.57.x_ref = bf16[256,4096]{1,0:T(8,128)(2,1)S(1)} custom-call(bf16[128,4096]{1,0:T(8,128)(2,1)S(1)} %bitcast.32, bf16[128,4096]{1,0:T(8,128)(2,1)} %collective-permute-done.y_ref, bf16[1,4096]{1,0:T(2,128)(2,1)S(1)} %shard_map.56.b_ref, f32[1,128]{1,0:T(1,128)S(1)} %broadcast_in_dim.24.f_ref), custom_call_target="tpu_custom_call" | custom-call | tf_op jit(solution)/shard_map/pallas_call | solution.py:135
  38.4 2.1 %shard_map.62.refs_2_.refs_4_ = f32[256,4096]{1,0:T(8,128)S(1)} custom-call(bf16[256,128]{1,0:T(8,128)(2,1)S(1)} %get-tuple-element.41.refs_0_.c_ref, bf16[256,128]{1,0:T(8,128)(2,1)S(1)} %get-tuple-element.42.refs_1_.c_ref, bf16[128,4096]{1,0:T(8,128)(2,1)S(1)} %get-tuple-element.38.refs_0_.refs_2_.w_ref, ...), custom_call_target="tpu_custom_call", output_to_operand_aliasing={{}: (4, {})} | custom-call | tf_op jit(solution)/shard_map/pallas_call | solution.py:135
  40.5 10.3 %collective-permute-done.6.refs_1_ = bf16[1,128]{1,0:T(2,128)(2,1)S(1)} collective-permute-done((bf16[1,128]{1,0:T(2,128)(2,1)S(1)}, bf16[1,128]{1,0:T(2,128)(2,1)S(1)}, u32[]{:S(2)}, u32[]{:S(2)}) %collective-permute-start.6) | collective-permute-done | bytes 288 | tf_op jit(solution)/shard_map/ppermute | solution.py:315
  52.8 4.5 %collective-permute-start.13 = (bf16[1,128]{1,0:T(2,128)(2,1)S(1)}, bf16[1,128]{1,0:T(2,128)(2,1)S(1)}, u32[]{:S(2)}, u32[]{:S(2)}) collective-permute-start(bf16[1,128]{1,0:T(2,128)(2,1)S(1)} %bitcast.36), channel_id=1, source_target_pairs={{0,14},{4,10},{8,6},{12,2},{14,0},{10,4},{6,8},{2,12},{1,15},{5,11... | collective-permute-start | bytes 776 | tf_op jit(solution)/shard_map/ppermute | solution.py:348
  57.3 2.0 %collective-permute-start.12 = (bf16[1,128]{1,0:T(2,128)(2,1)S(1)}, bf16[1,128]{1,0:T(2,128)(2,1)S(1)}, u32[]{:S(2)}, u32[]{:S(2)}) collective-permute-start(bf16[1,128]{1,0:T(2,128)(2,1)S(1)} %get-tuple-element.46.refs_3_), channel_id=1, source_target_pairs={{4,0},{8,4},{12,8},{14,12},{10,14},{6,10},{2,6},{0,2},{5,1},{9,5},... | collective-permute-start | bytes 776 | tf_op jit(solution)/shard_map/ppermute | solution.py:318
  59.3 2.3 %shard_map.65 = (bf16[256,128]{1,0:T(8,128)(2,1)S(1)}, f32[256,128]{1,0:T(8,128)S(1)}, bf16[256,128]{1,0:T(8,128)(2,1)S(1)}, f32[256,128]{1,0:T(8,128)S(1)}) custom-call(bf16[256,4096]{1,0:T(8,128)(2,1)S(1)} %shard_map.57.x_ref, bf16[128,4096]{1,0:T(8,128)(2,1)} %get-tuple-element.43.refs_0_.refs_2_.w_ref, ...), custom_call_target="tpu_custom_call" | custom-call | tf_op jit(solution)/shard_map/pallas_call | solution.py:135
  61.6 2.7 %shard_map.66.refs_2_.refs_3_.refs_4_ = f32[256,4096]{1,0:T(8,128)S(1)} custom-call(bf16[256,128]{1,0:T(8,128)(2,1)S(1)} %get-tuple-element.47.refs_0_.c_ref, bf16[256,128]{1,0:T(8,128)(2,1)S(1)} %get-tuple-element.48.refs_1_.c_ref, bf16[128,4096]{1,0:T(8,128)(2,1)} %get-tuple-element.43.refs_0_.refs_2_.w_ref, ...), custom_call_target="tpu_custom_call", output_to_operand_aliasing={{}: (4, {})} | custom-call | tf_op jit(solution)/shard_map/pallas_call | solution.py:135
  64.3 10.1 %collective-permute-done.8.refs_1_ = bf16[1,128]{1,0:T(2,128)(2,1)S(1)} collective-permute-done((bf16[1,128]{1,0:T(2,128)(2,1)S(1)}, bf16[1,128]{1,0:T(2,128)(2,1)S(1)}, u32[]{:S(2)}, u32[]{:S(2)}) %collective-permute-start.8) | collective-permute-done | bytes 288 | tf_op jit(solution)/shard_map/ppermute | solution.py:315
  77.2 1.7 collective-permute-start.16
  80.3 2.0 %shard_map.70.refs_2_ = bf16[256,4096]{1,0:T(8,128)(2,1)S(1)} custom-call(bf16[256,128]{1,0:T(8,128)(2,1)S(1)} %get-tuple-element.53.refs_0_.c_ref, bf16[256,128]{1,0:T(8,128)(2,1)S(1)} %get-tuple-element.54.refs_1_.c_ref, bf16[128,4096]{1,0:T(8,128)(2,1)S(1)} %get-tuple-element.49.refs_0_.refs_2_.w_ref, ...), custom_call_target="tpu_custom_call" | custom-call | tf_op jit(solution)/shard_map/pallas_call | solution.py:135
  82.4 3.3 %collective-permute-done.15.refs_0_ = bf16[64,4096]{1,0:T(8,128)(2,1)S(1)} collective-permute-done((bf16[64,4096]{1,0:T(8,128)(2,1)S(1)}, bf16[64,4096]{1,0:T(8,128)(2,1)S(1)}, u32[]{:S(2)}, u32[]{:S(2)}) %collective-permute-start.15) | collective-permute-done | bytes 524320 | tf_op jit(solution)/shard_map/ppermute | solution.py:315
  85.6 2.1 %collective-permute-done.16.refs_1_ = bf16[64,4096]{1,0:T(8,128)(2,1)S(1)} collective-permute-done((bf16[64,4096]{1,0:T(8,128)(2,1)S(1)}, bf16[64,4096]{1,0:T(8,128)(2,1)S(1)}, u32[]{:S(2)}, u32[]{:S(2)}) %collective-permute-start.16) | collective-permute-done | bytes 524320 | tf_op jit(solution)/shard_map/ppermute | solution.py:318
  94.1 1.7 collective-permute-start.26
  101.7 1.7 collective-permute-start.28
  103.4 5.1 %collective-permute-done.19.refs_1_ = bf16[64,4096]{1,0:T(8,128)(2,1)S(1)} collective-permute-done((bf16[64,4096]{1,0:T(8,128)(2,1)S(1)}, bf16[64,4096]{1,0:T(8,128)(2,1)S(1)}, u32[]{:S(2)}, u32[]{:S(2)}) %collective-permute-start.19) | collective-permute-done | bytes 524320 | tf_op jit(solution)/shard_map/ppermute | solution.py:315
  109.5 1.7 collective-permute-start.27
  113.7 6.0 %collective-permute-done.23.refs_1_ = bf16[64,4096]{1,0:T(8,128)(2,1)S(1)} collective-permute-done((bf16[64,4096]{1,0:T(8,128)(2,1)S(1)}, bf16[64,4096]{1,0:T(8,128)(2,1)S(1)}, u32[]{:S(2)}, u32[]{:S(2)}) %collective-permute-start.23) | collective-permute-done | bytes 524320 | tf_op jit(solution)/shard_map/ppermute | solution.py:315
  120.4 2.0 %shard_map.98.s_ref = bf16[256,128]{1,0:T(8,128)(2,1)S(1)} custom-call(bf16[256,4096]{1,0:T(8,128)(2,1)S(1)} %add_convert_fusion.e_ref, bf16[128,4096]{1,0:T(8,128)(2,1)} %get-tuple-element.43.refs_0_.refs_2_.w_ref, f32[256,128]{1,0:T(8,128)S(1)} %shard_map.97.s_ref), custom_call_target="tpu_custom_call" | custom-call | flops 268435456 | bytes 3145728 | tf_op jit(solution)/shard_map/pallas_call | solution.py:135
  124.2 1.7 collective-permute-start.29
  125.9 5.1 %collective-permute-done.20.refs_1_ = bf16[64,4096]{1,0:T(8,128)(2,1)S(1)} collective-permute-done((bf16[64,4096]{1,0:T(8,128)(2,1)S(1)}, bf16[64,4096]{1,0:T(8,128)(2,1)S(1)}, u32[]{:S(2)}, u32[]{:S(2)}) %collective-permute-start.20) | collective-permute-done | bytes 524320 | tf_op jit(solution)/shard_map/ppermute | solution.py:315
  132.2 1.7 collective-permute-start.31
  136.4 5.8 %collective-permute-done.24.refs_1_ = bf16[64,4096]{1,0:T(8,128)(2,1)S(1)} collective-permute-done((bf16[64,4096]{1,0:T(8,128)(2,1)S(1)}, bf16[64,4096]{1,0:T(8,128)(2,1)S(1)}, u32[]{:S(2)}, u32[]{:S(2)}) %collective-permute-start.24) | collective-permute-done | bytes 524320 | tf_op jit(solution)/shard_map/ppermute | solution.py:315
  145.7 1.7 collective-permute-start.30
  147.5 6.0 %collective-permute-done.21.refs_1_ = bf16[64,4096]{1,0:T(8,128)(2,1)S(1)} collective-permute-done((bf16[64,4096]{1,0:T(8,128)(2,1)S(1)}, bf16[64,4096]{1,0:T(8,128)(2,1)S(1)}, u32[]{:S(2)}, u32[]{:S(2)}) %collective-permute-start.21) | collective-permute-done | bytes 524320 | tf_op jit(solution)/shard_map/ppermute | solution.py:315
  154.4 1.7 collective-permute-start.32
  158.7 6.0 %collective-permute-done.25 = bf16[64,4096]{1,0:T(8,128)(2,1)S(1)} collective-permute-done((bf16[64,4096]{1,0:T(8,128)(2,1)S(1)}, bf16[64,4096]{1,0:T(8,128)(2,1)S(1)}, u32[]{:S(2)}, u32[]{:S(2)}) %collective-permute-start.25) | collective-permute-done | bytes 524320 | tf_op jit(solution)/shard_map/ppermute | solution.py:315
  165.1 10.0 %collective-permute-done.22 = bf16[64,4096]{1,0:T(8,128)(2,1)S(1)} collective-permute-done((bf16[64,4096]{1,0:T(8,128)(2,1)S(1)}, bf16[64,4096]{1,0:T(8,128)(2,1)S(1)}, u32[]{:S(2)}, u32[]{:S(2)}) %collective-permute-start.22) | collective-permute-done | bytes 524320 | tf_op jit(solution)/shard_map/ppermute | solution.py:315
  (115 shorter events, 42.7 us)
Async XLA Ops:
  0.0 26.4 %collective-permute-start.3 = (bf16[128,4096]{1,0:T(8,128)(2,1)}, bf16[128,4096]{1,0:T(8,128)(2,1)S(1)}, u32[]{:S(2)}, u32[]{:S(2)}) collective-permute-start(bf16[128,4096]{1,0:T(8,128)(2,1)} %w_ref.1), channel_id=1, source_target_pairs={{0,4},{4,8},{8,12},{12,14},{14,10},{10,6},{6,2},{2,0},{1,5},{5,9},... | collective-permute-start | bytes 3145736 | tf_op jit(solution)/shard_map/ppermute | solution.py:315
  3.0 25.2 %collective-permute-start.1 = (bf16[128,4096]{1,0:T(8,128)(2,1)}, bf16[128,4096]{1,0:T(8,128)(2,1)S(1)}, u32[]{:S(2)}, u32[]{:S(2)}) collective-permute-start(bf16[128,4096]{1,0:T(8,128)(2,1)} %w_ref.1), channel_id=1, source_target_pairs={{4,0},{8,4},{12,8},{14,12},{10,14},{6,10},{2,6},{0,2},{5,1},{9,5},... | collective-permute-start | bytes 3145736 | tf_op jit(solution)/shard_map/ppermute | solution.py:318
  3.0 27.7 %collective-permute-start = (bf16[128,4096]{1,0:T(8,128)(2,1)}, bf16[128,4096]{1,0:T(8,128)(2,1)}, u32[]{:S(2)}, u32[]{:S(2)}) collective-permute-start(bf16[128,4096]{1,0:T(8,128)(2,1)} %bitcast.31), channel_id=1, source_target_pairs={{0,1},{1,0},{2,3},{3,2},{4,5},{5,4},{6,7},{7,6},{8,9},{9,8},{10,11... | collective-permute-start | bytes 3145736 | tf_op jit(solution)/shard_map/ppermute | solution.py:321
  3.0 23.3 %collective-permute-start.4 = (bf16[1,128]{1,0:T(2,128)(2,1)}, bf16[1,128]{1,0:T(2,128)(2,1)S(1)}, u32[]{:S(2)}, u32[]{:S(2)}) collective-permute-start(bf16[1,128]{1,0:T(2,128)(2,1)} %bitcast.33), channel_id=1, source_target_pairs={{0,4},{4,8},{8,12},{12,14},{14,10},{10,6},{6,2},{2,0},{1,5},{5,9},... | collective-permute-start | bytes 776 | tf_op jit(solution)/shard_map/ppermute | solution.py:315
  5.1 23.2 %collective-permute-start.2 = (bf16[1,128]{1,0:T(2,128)(2,1)}, bf16[1,128]{1,0:T(2,128)(2,1)S(1)}, u32[]{:S(2)}, u32[]{:S(2)}) collective-permute-start(bf16[1,128]{1,0:T(2,128)(2,1)} %bitcast.34), channel_id=1, source_target_pairs={{4,0},{8,4},{12,8},{14,12},{10,14},{6,10},{2,6},{0,2},{5,1},{9,5},... | collective-permute-start | bytes 776 | tf_op jit(solution)/shard_map/ppermute | solution.py:318
  26.4 24.4 %collective-permute-start.5 = (bf16[128,4096]{1,0:T(8,128)(2,1)S(1)}, bf16[128,4096]{1,0:T(8,128)(2,1)}, u32[]{:S(2)}, u32[]{:S(2)}) collective-permute-start(bf16[128,4096]{1,0:T(8,128)(2,1)S(1)} %get-tuple-element.38.refs_0_.refs_2_.w_ref), channel_id=1, source_target_pairs={{0,4},{4,8},{8,12},{12,14},{14,10},{10,6},{6,2},{2,0},{1,5},{5,9},... | collective-permute-start | bytes 3145736 | tf_op jit(solution)/shard_map/ppermute | solution.py:315
  28.2 24.1 %collective-permute-start.9 = (bf16[128,4096]{1,0:T(8,128)(2,1)S(1)}, bf16[128,4096]{1,0:T(8,128)(2,1)S(1)}, u32[]{:S(2)}, u32[]{:S(2)}) collective-permute-start(bf16[128,4096]{1,0:T(8,128)(2,1)S(1)} %get-tuple-element.36.refs_1_.refs_3_.w_ref), channel_id=1, source_target_pairs={{4,0},{8,4},{12,8},{14,12},{10,14},{6,10},{2,6},{0,2},{5,1},{9,5},... | collective-permute-start | bytes 3145736 | tf_op jit(solution)/shard_map/ppermute | solution.py:318
  28.7 22.1 %collective-permute-start.6 = (bf16[1,128]{1,0:T(2,128)(2,1)S(1)}, bf16[1,128]{1,0:T(2,128)(2,1)S(1)}, u32[]{:S(2)}, u32[]{:S(2)}) collective-permute-start(bf16[1,128]{1,0:T(2,128)(2,1)S(1)} %get-tuple-element.39.refs_2_), channel_id=1, source_target_pairs={{0,4},{4,8},{8,12},{12,14},{14,10},{10,6},{6,2},{2,0},{1,5},{5,9},... | collective-permute-start | bytes 776 | tf_op jit(solution)/shard_map/ppermute | solution.py:315
  30.6 21.7 %collective-permute-start.10 = (bf16[1,128]{1,0:T(2,128)(2,1)S(1)}, bf16[1,128]{1,0:T(2,128)(2,1)S(1)}, u32[]{:S(2)}, u32[]{:S(2)}) collective-permute-start(bf16[1,128]{1,0:T(2,128)(2,1)S(1)} %get-tuple-element.40.refs_3_), channel_id=1, source_target_pairs={{4,0},{8,4},{12,8},{14,12},{10,14},{6,10},{2,6},{0,2},{5,1},{9,5},... | collective-permute-start | bytes 776 | tf_op jit(solution)/shard_map/ppermute | solution.py:318
  50.8 23.6 %collective-permute-start.7 = (bf16[128,4096]{1,0:T(8,128)(2,1)}, bf16[128,4096]{1,0:T(8,128)(2,1)S(1)}, u32[]{:S(2)}, u32[]{:S(2)}) collective-permute-start(bf16[128,4096]{1,0:T(8,128)(2,1)} %get-tuple-element.43.refs_0_.refs_2_.w_ref), channel_id=1, source_target_pairs={{0,4},{4,8},{8,12},{12,14},{14,10},{10,6},{6,2},{2,0},{1,5},{5,9},... | collective-permute-start | bytes 3145736 | tf_op jit(solution)/shard_map/ppermute | solution.py:315
  52.3 24.8 %collective-permute-start.11 = (bf16[128,4096]{1,0:T(8,128)(2,1)S(1)}, bf16[128,4096]{1,0:T(8,128)(2,1)S(1)}, u32[]{:S(2)}, u32[]{:S(2)}) collective-permute-start(bf16[128,4096]{1,0:T(8,128)(2,1)S(1)} %get-tuple-element.45.refs_1_.refs_3_.w_ref), channel_id=1, source_target_pairs={{4,0},{8,4},{12,8},{14,12},{10,14},{6,10},{2,6},{0,2},{5,1},{9,5},... | collective-permute-start | bytes 3145736 | tf_op jit(solution)/shard_map/ppermute | solution.py:318
  52.8 24.3 %collective-permute-start.13 = (bf16[1,128]{1,0:T(2,128)(2,1)S(1)}, bf16[1,128]{1,0:T(2,128)(2,1)S(1)}, u32[]{:S(2)}, u32[]{:S(2)}) collective-permute-start(bf16[1,128]{1,0:T(2,128)(2,1)S(1)} %bitcast.36), channel_id=1, source_target_pairs={{0,14},{4,10},{8,6},{12,2},{14,0},{10,4},{6,8},{2,12},{1,15},{5,11... | collective-permute-start | bytes 776 | tf_op jit(solution)/shard_map/ppermute | solution.py:348
  57.3 17.1 %collective-permute-start.8 = (bf16[1,128]{1,0:T(2,128)(2,1)S(1)}, bf16[1,128]{1,0:T(2,128)(2,1)S(1)}, u32[]{:S(2)}, u32[]{:S(2)}) collective-permute-start(bf16[1,128]{1,0:T(2,128)(2,1)S(1)} %get-tuple-element.44.refs_2_), channel_id=1, source_target_pairs={{0,4},{4,8},{8,12},{12,14},{14,10},{10,6},{6,2},{2,0},{1,5},{5,9},... | collective-permute-start | bytes 776 | tf_op jit(solution)/shard_map/ppermute | solution.py:315
  57.3 19.8 %collective-permute-start.12 = (bf16[1,128]{1,0:T(2,128)(2,1)S(1)}, bf16[1,128]{1,0:T(2,128)(2,1)S(1)}, u32[]{:S(2)}, u32[]{:S(2)}) collective-permute-start(bf16[1,128]{1,0:T(2,128)(2,1)S(1)} %get-tuple-element.46.refs_3_), channel_id=1, source_target_pairs={{4,0},{8,4},{12,8},{14,12},{10,14},{6,10},{2,6},{0,2},{5,1},{9,5},... | collective-permute-start | bytes 776 | tf_op jit(solution)/shard_map/ppermute | solution.py:318
  74.5 11.2 %collective-permute-start.15 = (bf16[64,4096]{1,0:T(8,128)(2,1)S(1)}, bf16[64,4096]{1,0:T(8,128)(2,1)S(1)}, u32[]{:S(2)}, u32[]{:S(2)}) collective-permute-start(bf16[64,4096]{1,0:T(8,128)(2,1)S(1)} %slice.16), channel_id=1, source_target_pairs={{0,4},{4,8},{8,12},{12,14},{14,10},{10,6},{6,2},{2,0},{1,5},{5,9},... | collective-permute-start | bytes 1572872 | tf_op jit(solution)/shard_map/ppermute | solution.py:315
  77.2 10.6 %collective-permute-start.16 = (bf16[64,4096]{1,0:T(8,128)(2,1)S(1)}, bf16[64,4096]{1,0:T(8,128)(2,1)S(1)}, u32[]{:S(2)}, u32[]{:S(2)}) collective-permute-start(bf16[64,4096]{1,0:T(8,128)(2,1)S(1)} %slice.17), channel_id=1, source_target_pairs={{4,0},{8,4},{12,8},{14,12},{10,14},{6,10},{2,6},{0,2},{5,1},{9,5},... | collective-permute-start | bytes 1572872 | tf_op jit(solution)/shard_map/ppermute | solution.py:318
  82.3 8.4 %collective-permute-start.14 = (bf16[256,4096]{1,0:T(8,128)(2,1)S(1)}, bf16[256,4096]{1,0:T(8,128)(2,1)S(1)}, u32[]{:S(2)}, u32[]{:S(2)}) collective-permute-start(bf16[256,4096]{1,0:T(8,128)(2,1)S(1)} %shard_map.70.refs_2_), channel_id=1, source_target_pairs={{0,1},{1,0},{2,3},{3,2},{4,5},{5,4},{6,7},{7,6},{8,9},{9,8},{10,11... | collective-permute-start | bytes 6291464 | tf_op jit(solution)/shard_map/ppermute | solution.py:321
  87.8 2.8 %collective-permute-start.18 = (bf16[128,4096]{1,0:T(8,128)(2,1)S(1)}, bf16[128,4096]{1,0:T(8,128)(2,1)S(1)}, u32[]{:S(2)}, u32[]{:S(2)}) collective-permute-start(bf16[128,4096]{1,0:T(8,128)(2,1)S(1)} %constant_dynamic-update-slice_fusion), channel_id=1, source_target_pairs={{0,1},{1,0},{2,3},{3,2},{4,5},{5,4},{6,7},{7,6},{8,9},{9,8},{10,11... | collective-permute-start | bytes 3145736 | tf_op jit(solution)/shard_map/ppermute | solution.py:321
  93.7 14.8 %collective-permute-start.19 = (bf16[64,4096]{1,0:T(8,128)(2,1)S(1)}, bf16[64,4096]{1,0:T(8,128)(2,1)S(1)}, u32[]{:S(2)}, u32[]{:S(2)}) collective-permute-start(bf16[64,4096]{1,0:T(8,128)(2,1)S(1)} %get-tuple-element.68), channel_id=1, source_target_pairs={{0,4},{4,8},{8,12},{12,14},{14,10},{10,6},{6,2},{2,0},{1,5},{5,9},... | collective-permute-start | bytes 1572872 | tf_op jit(solution)/shard_map/ppermute | solution.py:315
  94.1 15.1 %collective-permute-start.26 = (bf16[64,4096]{1,0:T(8,128)(2,1)S(1)}, bf16[64,4096]{1,0:T(8,128)(2,1)S(1)}, u32[]{:S(2)}, u32[]{:S(2)}) collective-permute-start(bf16[64,4096]{1,0:T(8,128)(2,1)S(1)} %get-tuple-element.67), channel_id=1, source_target_pairs={{4,0},{8,4},{12,8},{14,12},{10,14},{6,10},{2,6},{0,2},{5,1},{9,5},... | collective-permute-start | bytes 1572872 | tf_op jit(solution)/shard_map/ppermute | solution.py:318
  98.5 21.2 %collective-permute-start.23 = (bf16[64,4096]{1,0:T(8,128)(2,1)S(1)}, bf16[64,4096]{1,0:T(8,128)(2,1)S(1)}, u32[]{:S(2)}, u32[]{:S(2)}) collective-permute-start(bf16[64,4096]{1,0:T(8,128)(2,1)S(1)} %shard_map.87), channel_id=1, source_target_pairs={{0,4},{4,8},{8,12},{12,14},{14,10},{10,6},{6,2},{2,0},{1,5},{5,9},... | collective-permute-start | bytes 1572872 | tf_op jit(solution)/shard_map/ppermute | solution.py:315
  101.7 22.2 %collective-permute-start.28 = (bf16[64,4096]{1,0:T(8,128)(2,1)S(1)}, bf16[64,4096]{1,0:T(8,128)(2,1)S(1)}, u32[]{:S(2)}, u32[]{:S(2)}) collective-permute-start(bf16[64,4096]{1,0:T(8,128)(2,1)S(1)} %shard_map.100), channel_id=1, source_target_pairs={{4,0},{8,4},{12,8},{14,12},{10,14},{6,10},{2,6},{0,2},{5,1},{9,5},... | collective-permute-start | bytes 1572872 | tf_op jit(solution)/shard_map/ppermute | solution.py:318
  108.8 22.2 %collective-permute-start.20 = (bf16[64,4096]{1,0:T(8,128)(2,1)S(1)}, bf16[64,4096]{1,0:T(8,128)(2,1)S(1)}, u32[]{:S(2)}, u32[]{:S(2)}) collective-permute-start(bf16[64,4096]{1,0:T(8,128)(2,1)S(1)} %shard_map.78), channel_id=1, source_target_pairs={{0,4},{4,8},{8,12},{12,14},{14,10},{10,6},{6,2},{2,0},{1,5},{5,9},... | collective-permute-start | bytes 1572872 | tf_op jit(solution)/shard_map/ppermute | solution.py:315
  109.5 22.4 %collective-permute-start.27 = (bf16[64,4096]{1,0:T(8,128)(2,1)S(1)}, bf16[64,4096]{1,0:T(8,128)(2,1)S(1)}, u32[]{:S(2)}, u32[]{:S(2)}) collective-permute-start(bf16[64,4096]{1,0:T(8,128)(2,1)S(1)} %shard_map.93), channel_id=1, source_target_pairs={{4,0},{8,4},{12,8},{14,12},{10,14},{6,10},{2,6},{0,2},{5,1},{9,5},... | collective-permute-start | bytes 1572872 | tf_op jit(solution)/shard_map/ppermute | solution.py:318
  120.0 22.2 %collective-permute-start.24 = (bf16[64,4096]{1,0:T(8,128)(2,1)S(1)}, bf16[64,4096]{1,0:T(8,128)(2,1)S(1)}, u32[]{:S(2)}, u32[]{:S(2)}) collective-permute-start(bf16[64,4096]{1,0:T(8,128)(2,1)S(1)} %shard_map.88), channel_id=1, source_target_pairs={{0,4},{4,8},{8,12},{12,14},{14,10},{10,6},{6,2},{2,0},{1,5},{5,9},... | collective-permute-start | bytes 1572872 | tf_op jit(solution)/shard_map/ppermute | solution.py:315
  124.2 21.3 %collective-permute-start.29 = (bf16[64,4096]{1,0:T(8,128)(2,1)S(1)}, bf16[64,4096]{1,0:T(8,128)(2,1)S(1)}, u32[]{:S(2)}, u32[]{:S(2)}) collective-permute-start(bf16[64,4096]{1,0:T(8,128)(2,1)S(1)} %shard_map.101), channel_id=1, source_target_pairs={{4,0},{8,4},{12,8},{14,12},{10,14},{6,10},{2,6},{0,2},{5,1},{9,5},... | collective-permute-start | bytes 1572872 | tf_op jit(solution)/shard_map/ppermute | solution.py:318
  131.3 22.2 %collective-permute-start.21 = (bf16[64,4096]{1,0:T(8,128)(2,1)S(1)}, bf16[64,4096]{1,0:T(8,128)(2,1)S(1)}, u32[]{:S(2)}, u32[]{:S(2)}) collective-permute-start(bf16[64,4096]{1,0:T(8,128)(2,1)S(1)} %shard_map.79), channel_id=1, source_target_pairs={{0,4},{4,8},{8,12},{12,14},{14,10},{10,6},{6,2},{2,0},{1,5},{5,9},... | collective-permute-start | bytes 1572872 | tf_op jit(solution)/shard_map/ppermute | solution.py:315
  132.2 22.0 %collective-permute-start.31 = (bf16[64,4096]{1,0:T(8,128)(2,1)S(1)}, bf16[64,4096]{1,0:T(8,128)(2,1)S(1)}, u32[]{:S(2)}, u32[]{:S(2)}) collective-permute-start(bf16[64,4096]{1,0:T(8,128)(2,1)S(1)} %shard_map.103), channel_id=1, source_target_pairs={{4,0},{8,4},{12,8},{14,12},{10,14},{6,10},{2,6},{0,2},{5,1},{9,5},... | collective-permute-start | bytes 1572872 | tf_op jit(solution)/shard_map/ppermute | solution.py:318
  142.5 22.2 %collective-permute-start.25 = (bf16[64,4096]{1,0:T(8,128)(2,1)S(1)}, bf16[64,4096]{1,0:T(8,128)(2,1)S(1)}, u32[]{:S(2)}, u32[]{:S(2)}) collective-permute-start(bf16[64,4096]{1,0:T(8,128)(2,1)S(1)} %shard_map.89), channel_id=1, source_target_pairs={{0,4},{4,8},{8,12},{12,14},{14,10},{10,6},{6,2},{2,0},{1,5},{5,9},... | collective-permute-start | bytes 1572872 | tf_op jit(solution)/shard_map/ppermute | solution.py:315
  145.7 19.3 %collective-permute-start.30 = (bf16[64,4096]{1,0:T(8,128)(2,1)S(1)}, bf16[64,4096]{1,0:T(8,128)(2,1)S(1)}, u32[]{:S(2)}, u32[]{:S(2)}) collective-permute-start(bf16[64,4096]{1,0:T(8,128)(2,1)S(1)} %shard_map.102), channel_id=1, source_target_pairs={{4,0},{8,4},{12,8},{14,12},{10,14},{6,10},{2,6},{0,2},{5,1},{9,5},... | collective-permute-start | bytes 1572872 | tf_op jit(solution)/shard_map/ppermute | solution.py:318
  153.7 21.4 %collective-permute-start.22 = (bf16[64,4096]{1,0:T(8,128)(2,1)S(1)}, bf16[64,4096]{1,0:T(8,128)(2,1)S(1)}, u32[]{:S(2)}, u32[]{:S(2)}) collective-permute-start(bf16[64,4096]{1,0:T(8,128)(2,1)S(1)} %shard_map.86), channel_id=1, source_target_pairs={{0,4},{4,8},{8,12},{12,14},{14,10},{10,6},{6,2},{2,0},{1,5},{5,9},... | collective-permute-start | bytes 1572872 | tf_op jit(solution)/shard_map/ppermute | solution.py:315
  154.4 20.8 %collective-permute-start.32 = (bf16[64,4096]{1,0:T(8,128)(2,1)S(1)}, bf16[64,4096]{1,0:T(8,128)(2,1)S(1)}, u32[]{:S(2)}, u32[]{:S(2)}) collective-permute-start(bf16[64,4096]{1,0:T(8,128)(2,1)S(1)} %shard_map.104), channel_id=1, source_target_pairs={{4,0},{8,4},{12,8},{14,12},{10,14},{6,10},{2,6},{0,2},{5,1},{9,5},... | collective-permute-start | bytes 1572872 | tf_op jit(solution)/shard_map/ppermute | solution.py:318
  (6 other events, 64.9 us)

commit v9 on v8

--- a/solution.py
+++ b/solution.py
@@ -212,7 +212,7 @@
     )
 
 
-def decode(codes, words, total, dtype):
+def decode(codes, words, total, dtype, rows=None):
     n, width = len(words), words[0].shape[1]
     tile = width // TILES
 
@@ -223,10 +223,13 @@
             part = one if part is None else part + one
         rest = refs[2 * n :]
         part = part if len(rest) == 1 else part + rest[0][...]
+        if rows is not None:
+            part = part - 0.5 * rest[1][...].astype(jnp.float32)
         rest[-1][...] = part.astype(dtype)
 
     out = jax.ShapeDtypeStruct((codes[0].shape[0], width), dtype)
     args = (*codes, *words) if total is None else (*codes, *words, total)
+    args += () if rows is None else (rows,)
     specs = [whole(c) for c in codes] + [columns(w, tile) for w in words]
     specs += [columns(out, tile)] * (len(args) - 2 * n)
     aliases = {2 * n: 0} if total is not None and total.dtype == dtype else None
@@ -356,8 +359,9 @@
             out = encode(rows, blocks, shifts, listed, [steps.index(step) for step in group])
             for k, step in enumerate(group):
                 codes[step], sigmas[step] = out[2 * k : 2 * k + 2]
-            dtype = jnp.bfloat16 if t == half - 1 and group[-1] == t else jnp.float32
-            rebuilt = decode([codes[step] for step in group], blocks, rebuilt, dtype)
+            final = t == half - 1 and group[-1] == t
+            dtype, less = (jnp.bfloat16, rows) if final else (jnp.float32, None)
+            rebuilt = decode([codes[step] for step in group], blocks, rebuilt, dtype, less)
 
     swapped = to_core(rebuilt)
     last = to_right(words[1 - half][:cut]), to_left(words[half - 1][cut:])
@@ -373,7 +377,6 @@
     other_codes = to_core(codes[half])
 
     errors = rebuilt.astype(jnp.float32) + swapped.astype(jnp.float32)
-    errors = errors - rows.astype(jnp.float32)
     for code, word in ((codes[half], words[half]), (other_codes, other_words)):
         errors = errors + jnp.einsum("rl,ld->rd", code, word, preferred_element_type=jnp.float32)
     errors = errors.astype(jnp.bfloat16)

time: 177 us -> 177 us (level)
  no operation moved by 1% of the time
where the time goes in v9:
time: 177 us; the launch traced here: 176 us
  waiting for transfers between devices  92.9 us (52%)
  Pallas kernels  38.9 us (22%)
  starting transfers between devices  36.6 us (21%)
  matrix products  4.14 us (2%)
    ppermute x14, waiting for transfers between devices, to_right(): return lax.ppermute(x, 'lat', right_pairs)  88.6 us
    pallas_call x35, Pallas kernels, local_call(): pl.pallas_call(kernel, grid=grid, in_specs=in_specs, out_specs=out_specs,...  38.9 us
    ppermute x14, starting transfers between devices, to_left(): return lax.ppermute(x, 'lat', left_pairs)  16.8 us
    ppermute x14, starting transfers between devices, to_right(): return lax.ppermute(x, 'lat', right_pairs)  14.6 us
    ppermute x1, starting transfers between devices, ring_body(): far_bias = lax.ppermute(biases[0], 'lat', opposite)  4.46 us
  transfers between devices with their start and end apart: 33, of which 16 were waited for; matrix products, arithmetic and copies ran while one was open for 1% of the time, Pallas kernels for 22%

profile of v9, /device:TPU:0, one launch (start us, length us, event | category | flops | bytes accessed | tf_op | source)
XLA Modules:
  0.0 176.3 jit_solution(4713703225809449163)
XLA Ops:
  0.0 3.0 %collective-permute-start.3 = (bf16[128,4096]{1,0:T(8,128)(2,1)}, bf16[128,4096]{1,0:T(8,128)(2,1)S(1)}, u32[]{:S(2)}, u32[]{:S(2)}) collective-permute-start(bf16[128,4096]{1,0:T(8,128)(2,1)} %w_ref.1), channel_id=1, source_target_pairs={{0,4},{4,8},{8,12},{12,14},{14,10},{10,6},{6,2},{2,0},{1,5},{5,9},... | collective-permute-start | bytes 3145736 | tf_op jit(solution)/shard_map/ppermute | solution.py:318
  3.0 2.0 %collective-permute-start.4 = (bf16[1,128]{1,0:T(2,128)(2,1)}, bf16[1,128]{1,0:T(2,128)(2,1)S(1)}, u32[]{:S(2)}, u32[]{:S(2)}) collective-permute-start(bf16[1,128]{1,0:T(2,128)(2,1)} %bitcast.33), channel_id=1, source_target_pairs={{0,4},{4,8},{8,12},{12,14},{14,10},{10,6},{6,2},{2,0},{1,5},{5,9},... | collective-permute-start | bytes 776 | tf_op jit(solution)/shard_map/ppermute | solution.py:318
  5.1 21.3 %collective-permute-done.4.refs_1_ = bf16[1,128]{1,0:T(2,128)(2,1)S(1)} collective-permute-done((bf16[1,128]{1,0:T(2,128)(2,1)}, bf16[1,128]{1,0:T(2,128)(2,1)S(1)}, u32[]{:S(2)}, u32[]{:S(2)}) %collective-permute-start.4) | collective-permute-done | bytes 288 | tf_op jit(solution)/shard_map/ppermute | solution.py:318
  26.4 1.8 %collective-permute-start.5 = (bf16[128,4096]{1,0:T(8,128)(2,1)S(1)}, bf16[128,4096]{1,0:T(8,128)(2,1)}, u32[]{:S(2)}, u32[]{:S(2)}) collective-permute-start(bf16[128,4096]{1,0:T(8,128)(2,1)S(1)} %get-tuple-element.38.refs_0_.refs_2_.w_ref), channel_id=1, source_target_pairs={{0,4},{4,8},{8,12},{12,14},{14,10},{10,6},{6,2},{2,0},{1,5},{5,9},... | collective-permute-start | bytes 3145736 | tf_op jit(solution)/shard_map/ppermute | solution.py:318
  28.7 1.9 %collective-permute-start.6 = (bf16[1,128]{1,0:T(2,128)(2,1)S(1)}, bf16[1,128]{1,0:T(2,128)(2,1)S(1)}, u32[]{:S(2)}, u32[]{:S(2)}) collective-permute-start(bf16[1,128]{1,0:T(2,128)(2,1)S(1)} %get-tuple-element.39.refs_2_), channel_id=1, source_target_pairs={{0,4},{4,8},{8,12},{12,14},{14,10},{10,6},{6,2},{2,0},{1,5},{5,9},... | collective-permute-start | bytes 776 | tf_op jit(solution)/shard_map/ppermute | solution.py:318
  32.0 2.3 %shard_map.57.x_ref.refs_5_ = bf16[256,4096]{1,0:T(8,128)(2,1)S(1)} custom-call(bf16[128,4096]{1,0:T(8,128)(2,1)S(1)} %bitcast.32, bf16[128,4096]{1,0:T(8,128)(2,1)} %collective-permute-done.y_ref, bf16[1,4096]{1,0:T(2,128)(2,1)S(1)} %shard_map.56.b_ref, f32[1,128]{1,0:T(1,128)S(1)} %broadcast_in_dim.24.f_ref), custom_call_target="tpu_custom_call" | custom-call | tf_op jit(solution)/shard_map/pallas_call | solution.py:135
  38.4 2.1 %shard_map.62.refs_2_.refs_4_ = f32[256,4096]{1,0:T(8,128)S(1)} custom-call(bf16[256,128]{1,0:T(8,128)(2,1)S(1)} %get-tuple-element.41.refs_0_.c_ref, bf16[256,128]{1,0:T(8,128)(2,1)S(1)} %get-tuple-element.42.refs_1_.c_ref, bf16[128,4096]{1,0:T(8,128)(2,1)S(1)} %get-tuple-element.38.refs_0_.refs_2_.w_ref, ...), custom_call_target="tpu_custom_call", output_to_operand_aliasing={{}: (4, {})} | custom-call | tf_op jit(solution)/shard_map/pallas_call | solution.py:135
  40.5 10.3 %collective-permute-done.6.refs_1_ = bf16[1,128]{1,0:T(2,128)(2,1)S(1)} collective-permute-done((bf16[1,128]{1,0:T(2,128)(2,1)S(1)}, bf16[1,128]{1,0:T(2,128)(2,1)S(1)}, u32[]{:S(2)}, u32[]{:S(2)}) %collective-permute-start.6) | collective-permute-done | bytes 288 | tf_op jit(solution)/shard_map/ppermute | solution.py:318
  52.8 4.5 %collective-permute-start.13 = (bf16[1,128]{1,0:T(2,128)(2,1)S(1)}, bf16[1,128]{1,0:T(2,128)(2,1)S(1)}, u32[]{:S(2)}, u32[]{:S(2)}) collective-permute-start(bf16[1,128]{1,0:T(2,128)(2,1)S(1)} %bitcast.36), channel_id=1, source_target_pairs={{0,14},{4,10},{8,6},{12,2},{14,0},{10,4},{6,8},{2,12},{1,15},{5,11... | collective-permute-start | bytes 776 | tf_op jit(solution)/shard_map/ppermute | solution.py:351
  57.3 2.0 %collective-permute-start.12 = (bf16[1,128]{1,0:T(2,128)(2,1)S(1)}, bf16[1,128]{1,0:T(2,128)(2,1)S(1)}, u32[]{:S(2)}, u32[]{:S(2)}) collective-permute-start(bf16[1,128]{1,0:T(2,128)(2,1)S(1)} %get-tuple-element.46.refs_3_), channel_id=1, source_target_pairs={{4,0},{8,4},{12,8},{14,12},{10,14},{6,10},{2,6},{0,2},{5,1},{9,5},... | collective-permute-start | bytes 776 | tf_op jit(solution)/shard_map/ppermute | solution.py:321
  59.3 2.3 %shard_map.65 = (bf16[256,128]{1,0:T(8,128)(2,1)S(1)}, f32[256,128]{1,0:T(8,128)S(1)}, bf16[256,128]{1,0:T(8,128)(2,1)S(1)}, f32[256,128]{1,0:T(8,128)S(1)}) custom-call(bf16[256,4096]{1,0:T(8,128)(2,1)S(1)} %shard_map.57.x_ref.refs_5_, bf16[128,4096]{1,0:T(8,128)(2,1)} %get-tuple-element.43.refs_0_.refs_2_.w_ref, ...), custom_call_target="tpu_custom_call" | custom-call | tf_op jit(solution)/shard_map/pallas_call | solution.py:135
  61.6 2.7 %shard_map.66.refs_2_.refs_3_.refs_4_ = f32[256,4096]{1,0:T(8,128)S(1)} custom-call(bf16[256,128]{1,0:T(8,128)(2,1)S(1)} %get-tuple-element.47.refs_0_.c_ref, bf16[256,128]{1,0:T(8,128)(2,1)S(1)} %get-tuple-element.48.refs_1_.c_ref, bf16[128,4096]{1,0:T(8,128)(2,1)} %get-tuple-element.43.refs_0_.refs_2_.w_ref, ...), custom_call_target="tpu_custom_call", output_to_operand_aliasing={{}: (4, {})} | custom-call | tf_op jit(solution)/shard_map/pallas_call | solution.py:135
  64.4 10.1 %collective-permute-done.8.refs_1_ = bf16[1,128]{1,0:T(2,128)(2,1)S(1)} collective-permute-done((bf16[1,128]{1,0:T(2,128)(2,1)S(1)}, bf16[1,128]{1,0:T(2,128)(2,1)S(1)}, u32[]{:S(2)}, u32[]{:S(2)}) %collective-permute-start.8) | collective-permute-done | bytes 288 | tf_op jit(solution)/shard_map/ppermute | solution.py:318
  77.2 1.7 collective-permute-start.16
  80.3 2.1 %shard_map.70.refs_2_ = bf16[256,4096]{1,0:T(8,128)(2,1)S(1)} custom-call(bf16[256,128]{1,0:T(8,128)(2,1)S(1)} %get-tuple-element.53.refs_0_.c_ref, bf16[256,128]{1,0:T(8,128)(2,1)S(1)} %get-tuple-element.54.refs_1_.c_ref, bf16[128,4096]{1,0:T(8,128)(2,1)S(1)} %get-tuple-element.49.refs_0_.refs_2_.w_ref, ...), custom_call_target="tpu_custom_call" | custom-call | tf_op jit(solution)/shard_map/pallas_call | solution.py:135
  82.5 3.1 %collective-permute-done.15.refs_0_ = bf16[64,4096]{1,0:T(8,128)(2,1)S(1)} collective-permute-done((bf16[64,4096]{1,0:T(8,128)(2,1)S(1)}, bf16[64,4096]{1,0:T(8,128)(2,1)S(1)}, u32[]{:S(2)}, u32[]{:S(2)}) %collective-permute-start.15) | collective-permute-done | bytes 524320 | tf_op jit(solution)/shard_map/ppermute | solution.py:318
  85.6 2.1 %collective-permute-done.16.refs_1_ = bf16[64,4096]{1,0:T(8,128)(2,1)S(1)} collective-permute-done((bf16[64,4096]{1,0:T(8,128)(2,1)S(1)}, bf16[64,4096]{1,0:T(8,128)(2,1)S(1)}, u32[]{:S(2)}, u32[]{:S(2)}) %collective-permute-start.16) | collective-permute-done | bytes 524320 | tf_op jit(solution)/shard_map/ppermute | solution.py:321
  93.8 1.7 collective-permute-start.26
  101.5 1.7 collective-permute-start.28
  103.2 5.1 %collective-permute-done.19.refs_1_ = bf16[64,4096]{1,0:T(8,128)(2,1)S(1)} collective-permute-done((bf16[64,4096]{1,0:T(8,128)(2,1)S(1)}, bf16[64,4096]{1,0:T(8,128)(2,1)S(1)}, u32[]{:S(2)}, u32[]{:S(2)}) %collective-permute-start.19) | collective-permute-done | bytes 524320 | tf_op jit(solution)/shard_map/ppermute | solution.py:318
  109.2 1.7 collective-permute-start.27
  113.5 6.0 %collective-permute-done.23.refs_1_ = bf16[64,4096]{1,0:T(8,128)(2,1)S(1)} collective-permute-done((bf16[64,4096]{1,0:T(8,128)(2,1)S(1)}, bf16[64,4096]{1,0:T(8,128)(2,1)S(1)}, u32[]{:S(2)}, u32[]{:S(2)}) %collective-permute-start.23) | collective-permute-done | bytes 524320 | tf_op jit(solution)/shard_map/ppermute | solution.py:318
  120.2 2.0 %shard_map.98.s_ref = bf16[256,128]{1,0:T(8,128)(2,1)S(1)} custom-call(bf16[256,4096]{1,0:T(8,128)(2,1)S(1)} %add_convert_fusion.e_ref, bf16[128,4096]{1,0:T(8,128)(2,1)} %get-tuple-element.43.refs_0_.refs_2_.w_ref, f32[256,128]{1,0:T(8,128)S(1)} %shard_map.97.s_ref), custom_call_target="tpu_custom_call" | custom-call | flops 268435456 | bytes 3145728 | tf_op jit(solution)/shard_map/pallas_call | solution.py:135
  123.9 1.7 collective-permute-start.29
  125.6 5.1 %collective-permute-done.20.refs_1_ = bf16[64,4096]{1,0:T(8,128)(2,1)S(1)} collective-permute-done((bf16[64,4096]{1,0:T(8,128)(2,1)S(1)}, bf16[64,4096]{1,0:T(8,128)(2,1)S(1)}, u32[]{:S(2)}, u32[]{:S(2)}) %collective-permute-start.20) | collective-permute-done | bytes 524320 | tf_op jit(solution)/shard_map/ppermute | solution.py:318
  131.7 1.9 %collective-permute-start.31 = (bf16[64,4096]{1,0:T(8,128)(2,1)S(1)}, bf16[64,4096]{1,0:T(8,128)(2,1)S(1)}, u32[]{:S(2)}, u32[]{:S(2)}) collective-permute-start(bf16[64,4096]{1,0:T(8,128)(2,1)S(1)} %shard_map.103), channel_id=1, source_target_pairs={{4,0},{8,4},{12,8},{14,12},{10,14},{6,10},{2,6},{0,2},{5,1},{9,5},... | collective-permute-start | bytes 1572872 | tf_op jit(solution)/shard_map/ppermute | solution.py:321
  136.2 5.8 %collective-permute-done.24.refs_1_ = bf16[64,4096]{1,0:T(8,128)(2,1)S(1)} collective-permute-done((bf16[64,4096]{1,0:T(8,128)(2,1)S(1)}, bf16[64,4096]{1,0:T(8,128)(2,1)S(1)}, u32[]{:S(2)}, u32[]{:S(2)}) %collective-permute-start.24) | collective-permute-done | bytes 524320 | tf_op jit(solution)/shard_map/ppermute | solution.py:318
  145.5 1.7 collective-permute-start.30
  147.2 6.0 %collective-permute-done.21.refs_1_ = bf16[64,4096]{1,0:T(8,128)(2,1)S(1)} collective-permute-done((bf16[64,4096]{1,0:T(8,128)(2,1)S(1)}, bf16[64,4096]{1,0:T(8,128)(2,1)S(1)}, u32[]{:S(2)}, u32[]{:S(2)}) %collective-permute-start.21) | collective-permute-done | bytes 524320 | tf_op jit(solution)/shard_map/ppermute | solution.py:318
  154.2 1.7 collective-permute-start.32
  158.4 6.0 %collective-permute-done.25 = bf16[64,4096]{1,0:T(8,128)(2,1)S(1)} collective-permute-done((bf16[64,4096]{1,0:T(8,128)(2,1)S(1)}, bf16[64,4096]{1,0:T(8,128)(2,1)S(1)}, u32[]{:S(2)}, u32[]{:S(2)}) %collective-permute-start.25) | collective-permute-done | bytes 524320 | tf_op jit(solution)/shard_map/ppermute | solution.py:318
  164.8 10.0 %collective-permute-done.22 = bf16[64,4096]{1,0:T(8,128)(2,1)S(1)} collective-permute-done((bf16[64,4096]{1,0:T(8,128)(2,1)S(1)}, bf16[64,4096]{1,0:T(8,128)(2,1)S(1)}, u32[]{:S(2)}, u32[]{:S(2)}) %collective-permute-start.22) | collective-permute-done | bytes 524320 | tf_op jit(solution)/shard_map/ppermute | solution.py:318
  (115 shorter events, 42.3 us)
Async XLA Ops:
  0.0 26.4 %collective-permute-start.3 = (bf16[128,4096]{1,0:T(8,128)(2,1)}, bf16[128,4096]{1,0:T(8,128)(2,1)S(1)}, u32[]{:S(2)}, u32[]{:S(2)}) collective-permute-start(bf16[128,4096]{1,0:T(8,128)(2,1)} %w_ref.1), channel_id=1, source_target_pairs={{0,4},{4,8},{8,12},{12,14},{14,10},{10,6},{6,2},{2,0},{1,5},{5,9},... | collective-permute-start | bytes 3145736 | tf_op jit(solution)/shard_map/ppermute | solution.py:318
  3.0 25.2 %collective-permute-start.1 = (bf16[128,4096]{1,0:T(8,128)(2,1)}, bf16[128,4096]{1,0:T(8,128)(2,1)S(1)}, u32[]{:S(2)}, u32[]{:S(2)}) collective-permute-start(bf16[128,4096]{1,0:T(8,128)(2,1)} %w_ref.1), channel_id=1, source_target_pairs={{4,0},{8,4},{12,8},{14,12},{10,14},{6,10},{2,6},{0,2},{5,1},{9,5},... | collective-permute-start | bytes 3145736 | tf_op jit(solution)/shard_map/ppermute | solution.py:321
  3.0 27.7 %collective-permute-start = (bf16[128,4096]{1,0:T(8,128)(2,1)}, bf16[128,4096]{1,0:T(8,128)(2,1)}, u32[]{:S(2)}, u32[]{:S(2)}) collective-permute-start(bf16[128,4096]{1,0:T(8,128)(2,1)} %bitcast.31), channel_id=1, source_target_pairs={{0,1},{1,0},{2,3},{3,2},{4,5},{5,4},{6,7},{7,6},{8,9},{9,8},{10,11... | collective-permute-start | bytes 3145736 | tf_op jit(solution)/shard_map/ppermute | solution.py:324
  3.0 23.3 %collective-permute-start.4 = (bf16[1,128]{1,0:T(2,128)(2,1)}, bf16[1,128]{1,0:T(2,128)(2,1)S(1)}, u32[]{:S(2)}, u32[]{:S(2)}) collective-permute-start(bf16[1,128]{1,0:T(2,128)(2,1)} %bitcast.33), channel_id=1, source_target_pairs={{0,4},{4,8},{8,12},{12,14},{14,10},{10,6},{6,2},{2,0},{1,5},{5,9},... | collective-permute-start | bytes 776 | tf_op jit(solution)/shard_map/ppermute | solution.py:318
  5.1 23.2 %collective-permute-start.2 = (bf16[1,128]{1,0:T(2,128)(2,1)}, bf16[1,128]{1,0:T(2,128)(2,1)S(1)}, u32[]{:S(2)}, u32[]{:S(2)}) collective-permute-start(bf16[1,128]{1,0:T(2,128)(2,1)} %bitcast.34), channel_id=1, source_target_pairs={{4,0},{8,4},{12,8},{14,12},{10,14},{6,10},{2,6},{0,2},{5,1},{9,5},... | collective-permute-start | bytes 776 | tf_op jit(solution)/shard_map/ppermute | solution.py:321
  26.4 24.4 %collective-permute-start.5 = (bf16[128,4096]{1,0:T(8,128)(2,1)S(1)}, bf16[128,4096]{1,0:T(8,128)(2,1)}, u32[]{:S(2)}, u32[]{:S(2)}) collective-permute-start(bf16[128,4096]{1,0:T(8,128)(2,1)S(1)} %get-tuple-element.38.refs_0_.refs_2_.w_ref), channel_id=1, source_target_pairs={{0,4},{4,8},{8,12},{12,14},{14,10},{10,6},{6,2},{2,0},{1,5},{5,9},... | collective-permute-start | bytes 3145736 | tf_op jit(solution)/shard_map/ppermute | solution.py:318
  28.2 24.1 %collective-permute-start.9 = (bf16[128,4096]{1,0:T(8,128)(2,1)S(1)}, bf16[128,4096]{1,0:T(8,128)(2,1)S(1)}, u32[]{:S(2)}, u32[]{:S(2)}) collective-permute-start(bf16[128,4096]{1,0:T(8,128)(2,1)S(1)} %get-tuple-element.36.refs_1_.refs_3_.w_ref), channel_id=1, source_target_pairs={{4,0},{8,4},{12,8},{14,12},{10,14},{6,10},{2,6},{0,2},{5,1},{9,5},... | collective-permute-start | bytes 3145736 | tf_op jit(solution)/shard_map/ppermute | solution.py:321
  28.7 22.1 %collective-permute-start.6 = (bf16[1,128]{1,0:T(2,128)(2,1)S(1)}, bf16[1,128]{1,0:T(2,128)(2,1)S(1)}, u32[]{:S(2)}, u32[]{:S(2)}) collective-permute-start(bf16[1,128]{1,0:T(2,128)(2,1)S(1)} %get-tuple-element.39.refs_2_), channel_id=1, source_target_pairs={{0,4},{4,8},{8,12},{12,14},{14,10},{10,6},{6,2},{2,0},{1,5},{5,9},... | collective-permute-start | bytes 776 | tf_op jit(solution)/shard_map/ppermute | solution.py:318
  30.6 21.7 %collective-permute-start.10 = (bf16[1,128]{1,0:T(2,128)(2,1)S(1)}, bf16[1,128]{1,0:T(2,128)(2,1)S(1)}, u32[]{:S(2)}, u32[]{:S(2)}) collective-permute-start(bf16[1,128]{1,0:T(2,128)(2,1)S(1)} %get-tuple-element.40.refs_3_), channel_id=1, source_target_pairs={{4,0},{8,4},{12,8},{14,12},{10,14},{6,10},{2,6},{0,2},{5,1},{9,5},... | collective-permute-start | bytes 776 | tf_op jit(solution)/shard_map/ppermute | solution.py:321
  50.8 23.6 %collective-permute-start.7 = (bf16[128,4096]{1,0:T(8,128)(2,1)}, bf16[128,4096]{1,0:T(8,128)(2,1)S(1)}, u32[]{:S(2)}, u32[]{:S(2)}) collective-permute-start(bf16[128,4096]{1,0:T(8,128)(2,1)} %get-tuple-element.43.refs_0_.refs_2_.w_ref), channel_id=1, source_target_pairs={{0,4},{4,8},{8,12},{12,14},{14,10},{10,6},{6,2},{2,0},{1,5},{5,9},... | collective-permute-start | bytes 3145736 | tf_op jit(solution)/shard_map/ppermute | solution.py:318
  52.3 24.8 %collective-permute-start.11 = (bf16[128,4096]{1,0:T(8,128)(2,1)S(1)}, bf16[128,4096]{1,0:T(8,128)(2,1)S(1)}, u32[]{:S(2)}, u32[]{:S(2)}) collective-permute-start(bf16[128,4096]{1,0:T(8,128)(2,1)S(1)} %get-tuple-element.45.refs_1_.refs_3_.w_ref), channel_id=1, source_target_pairs={{4,0},{8,4},{12,8},{14,12},{10,14},{6,10},{2,6},{0,2},{5,1},{9,5},... | collective-permute-start | bytes 3145736 | tf_op jit(solution)/shard_map/ppermute | solution.py:321
  52.8 24.3 %collective-permute-start.13 = (bf16[1,128]{1,0:T(2,128)(2,1)S(1)}, bf16[1,128]{1,0:T(2,128)(2,1)S(1)}, u32[]{:S(2)}, u32[]{:S(2)}) collective-permute-start(bf16[1,128]{1,0:T(2,128)(2,1)S(1)} %bitcast.36), channel_id=1, source_target_pairs={{0,14},{4,10},{8,6},{12,2},{14,0},{10,4},{6,8},{2,12},{1,15},{5,11... | collective-permute-start | bytes 776 | tf_op jit(solution)/shard_map/ppermute | solution.py:351
  57.3 17.1 %collective-permute-start.8 = (bf16[1,128]{1,0:T(2,128)(2,1)S(1)}, bf16[1,128]{1,0:T(2,128)(2,1)S(1)}, u32[]{:S(2)}, u32[]{:S(2)}) collective-permute-start(bf16[1,128]{1,0:T(2,128)(2,1)S(1)} %get-tuple-element.44.refs_2_), channel_id=1, source_target_pairs={{0,4},{4,8},{8,12},{12,14},{14,10},{10,6},{6,2},{2,0},{1,5},{5,9},... | collective-permute-start | bytes 776 | tf_op jit(solution)/shard_map/ppermute | solution.py:318
  57.3 19.8 %collective-permute-start.12 = (bf16[1,128]{1,0:T(2,128)(2,1)S(1)}, bf16[1,128]{1,0:T(2,128)(2,1)S(1)}, u32[]{:S(2)}, u32[]{:S(2)}) collective-permute-start(bf16[1,128]{1,0:T(2,128)(2,1)S(1)} %get-tuple-element.46.refs_3_), channel_id=1, source_target_pairs={{4,0},{8,4},{12,8},{14,12},{10,14},{6,10},{2,6},{0,2},{5,1},{9,5},... | collective-permute-start | bytes 776 | tf_op jit(solution)/shard_map/ppermute | solution.py:321
  74.5 11.2 %collective-permute-start.15 = (bf16[64,4096]{1,0:T(8,128)(2,1)S(1)}, bf16[64,4096]{1,0:T(8,128)(2,1)S(1)}, u32[]{:S(2)}, u32[]{:S(2)}) collective-permute-start(bf16[64,4096]{1,0:T(8,128)(2,1)S(1)} %slice.16), channel_id=1, source_target_pairs={{0,4},{4,8},{8,12},{12,14},{14,10},{10,6},{6,2},{2,0},{1,5},{5,9},... | collective-permute-start | bytes 1572872 | tf_op jit(solution)/shard_map/ppermute | solution.py:318
  77.2 10.6 %collective-permute-start.16 = (bf16[64,4096]{1,0:T(8,128)(2,1)S(1)}, bf16[64,4096]{1,0:T(8,128)(2,1)S(1)}, u32[]{:S(2)}, u32[]{:S(2)}) collective-permute-start(bf16[64,4096]{1,0:T(8,128)(2,1)S(1)} %slice.17), channel_id=1, source_target_pairs={{4,0},{8,4},{12,8},{14,12},{10,14},{6,10},{2,6},{0,2},{5,1},{9,5},... | collective-permute-start | bytes 1572872 | tf_op jit(solution)/shard_map/ppermute | solution.py:321
  82.5 8.2 %collective-permute-start.14 = (bf16[256,4096]{1,0:T(8,128)(2,1)S(1)}, bf16[256,4096]{1,0:T(8,128)(2,1)S(1)}, u32[]{:S(2)}, u32[]{:S(2)}) collective-permute-start(bf16[256,4096]{1,0:T(8,128)(2,1)S(1)} %shard_map.70.refs_2_), channel_id=1, source_target_pairs={{0,1},{1,0},{2,3},{3,2},{4,5},{5,4},{6,7},{7,6},{8,9},{9,8},{10,11... | collective-permute-start | bytes 6291464 | tf_op jit(solution)/shard_map/ppermute | solution.py:324
  87.9 2.8 %collective-permute-start.18 = (bf16[128,4096]{1,0:T(8,128)(2,1)S(1)}, bf16[128,4096]{1,0:T(8,128)(2,1)S(1)}, u32[]{:S(2)}, u32[]{:S(2)}) collective-permute-start(bf16[128,4096]{1,0:T(8,128)(2,1)S(1)} %constant_dynamic-update-slice_fusion), channel_id=1, source_target_pairs={{0,1},{1,0},{2,3},{3,2},{4,5},{5,4},{6,7},{7,6},{8,9},{9,8},{10,11... | collective-permute-start | bytes 3145736 | tf_op jit(solution)/shard_map/ppermute | solution.py:324
  93.4 14.8 %collective-permute-start.19 = (bf16[64,4096]{1,0:T(8,128)(2,1)S(1)}, bf16[64,4096]{1,0:T(8,128)(2,1)S(1)}, u32[]{:S(2)}, u32[]{:S(2)}) collective-permute-start(bf16[64,4096]{1,0:T(8,128)(2,1)S(1)} %get-tuple-element.68), channel_id=1, source_target_pairs={{0,4},{4,8},{8,12},{12,14},{14,10},{10,6},{6,2},{2,0},{1,5},{5,9},... | collective-permute-start | bytes 1572872 | tf_op jit(solution)/shard_map/ppermute | solution.py:318
  93.8 15.1 %collective-permute-start.26 = (bf16[64,4096]{1,0:T(8,128)(2,1)S(1)}, bf16[64,4096]{1,0:T(8,128)(2,1)S(1)}, u32[]{:S(2)}, u32[]{:S(2)}) collective-permute-start(bf16[64,4096]{1,0:T(8,128)(2,1)S(1)} %get-tuple-element.67), channel_id=1, source_target_pairs={{4,0},{8,4},{12,8},{14,12},{10,14},{6,10},{2,6},{0,2},{5,1},{9,5},... | collective-permute-start | bytes 1572872 | tf_op jit(solution)/shard_map/ppermute | solution.py:321
  98.3 21.2 %collective-permute-start.23 = (bf16[64,4096]{1,0:T(8,128)(2,1)S(1)}, bf16[64,4096]{1,0:T(8,128)(2,1)S(1)}, u32[]{:S(2)}, u32[]{:S(2)}) collective-permute-start(bf16[64,4096]{1,0:T(8,128)(2,1)S(1)} %shard_map.87), channel_id=1, source_target_pairs={{0,4},{4,8},{8,12},{12,14},{14,10},{10,6},{6,2},{2,0},{1,5},{5,9},... | collective-permute-start | bytes 1572872 | tf_op jit(solution)/shard_map/ppermute | solution.py:318
  101.5 22.2 %collective-permute-start.28 = (bf16[64,4096]{1,0:T(8,128)(2,1)S(1)}, bf16[64,4096]{1,0:T(8,128)(2,1)S(1)}, u32[]{:S(2)}, u32[]{:S(2)}) collective-permute-start(bf16[64,4096]{1,0:T(8,128)(2,1)S(1)} %shard_map.100), channel_id=1, source_target_pairs={{4,0},{8,4},{12,8},{14,12},{10,14},{6,10},{2,6},{0,2},{5,1},{9,5},... | collective-permute-start | bytes 1572872 | tf_op jit(solution)/shard_map/ppermute | solution.py:321
  108.5 22.2 %collective-permute-start.20 = (bf16[64,4096]{1,0:T(8,128)(2,1)S(1)}, bf16[64,4096]{1,0:T(8,128)(2,1)S(1)}, u32[]{:S(2)}, u32[]{:S(2)}) collective-permute-start(bf16[64,4096]{1,0:T(8,128)(2,1)S(1)} %shard_map.78), channel_id=1, source_target_pairs={{0,4},{4,8},{8,12},{12,14},{14,10},{10,6},{6,2},{2,0},{1,5},{5,9},... | collective-permute-start | bytes 1572872 | tf_op jit(solution)/shard_map/ppermute | solution.py:318
  109.2 22.2 %collective-permute-start.27 = (bf16[64,4096]{1,0:T(8,128)(2,1)S(1)}, bf16[64,4096]{1,0:T(8,128)(2,1)S(1)}, u32[]{:S(2)}, u32[]{:S(2)}) collective-permute-start(bf16[64,4096]{1,0:T(8,128)(2,1)S(1)} %shard_map.93), channel_id=1, source_target_pairs={{4,0},{8,4},{12,8},{14,12},{10,14},{6,10},{2,6},{0,2},{5,1},{9,5},... | collective-permute-start | bytes 1572872 | tf_op jit(solution)/shard_map/ppermute | solution.py:321
  119.8 22.2 %collective-permute-start.24 = (bf16[64,4096]{1,0:T(8,128)(2,1)S(1)}, bf16[64,4096]{1,0:T(8,128)(2,1)S(1)}, u32[]{:S(2)}, u32[]{:S(2)}) collective-permute-start(bf16[64,4096]{1,0:T(8,128)(2,1)S(1)} %shard_map.88), channel_id=1, source_target_pairs={{0,4},{4,8},{8,12},{12,14},{14,10},{10,6},{6,2},{2,0},{1,5},{5,9},... | collective-permute-start | bytes 1572872 | tf_op jit(solution)/shard_map/ppermute | solution.py:318
  123.9 21.3 %collective-permute-start.29 = (bf16[64,4096]{1,0:T(8,128)(2,1)S(1)}, bf16[64,4096]{1,0:T(8,128)(2,1)S(1)}, u32[]{:S(2)}, u32[]{:S(2)}) collective-permute-start(bf16[64,4096]{1,0:T(8,128)(2,1)S(1)} %shard_map.101), channel_id=1, source_target_pairs={{4,0},{8,4},{12,8},{14,12},{10,14},{6,10},{2,6},{0,2},{5,1},{9,5},... | collective-permute-start | bytes 1572872 | tf_op jit(solution)/shard_map/ppermute | solution.py:321
  131.0 22.2 %collective-permute-start.21 = (bf16[64,4096]{1,0:T(8,128)(2,1)S(1)}, bf16[64,4096]{1,0:T(8,128)(2,1)S(1)}, u32[]{:S(2)}, u32[]{:S(2)}) collective-permute-start(bf16[64,4096]{1,0:T(8,128)(2,1)S(1)} %shard_map.79), channel_id=1, source_target_pairs={{0,4},{4,8},{8,12},{12,14},{14,10},{10,6},{6,2},{2,0},{1,5},{5,9},... | collective-permute-start | bytes 1572872 | tf_op jit(solution)/shard_map/ppermute | solution.py:318
  131.7 22.2 %collective-permute-start.31 = (bf16[64,4096]{1,0:T(8,128)(2,1)S(1)}, bf16[64,4096]{1,0:T(8,128)(2,1)S(1)}, u32[]{:S(2)}, u32[]{:S(2)}) collective-permute-start(bf16[64,4096]{1,0:T(8,128)(2,1)S(1)} %shard_map.103), channel_id=1, source_target_pairs={{4,0},{8,4},{12,8},{14,12},{10,14},{6,10},{2,6},{0,2},{5,1},{9,5},... | collective-permute-start | bytes 1572872 | tf_op jit(solution)/shard_map/ppermute | solution.py:321
  142.3 22.2 %collective-permute-start.25 = (bf16[64,4096]{1,0:T(8,128)(2,1)S(1)}, bf16[64,4096]{1,0:T(8,128)(2,1)S(1)}, u32[]{:S(2)}, u32[]{:S(2)}) collective-permute-start(bf16[64,4096]{1,0:T(8,128)(2,1)S(1)} %shard_map.89), channel_id=1, source_target_pairs={{0,4},{4,8},{8,12},{12,14},{14,10},{10,6},{6,2},{2,0},{1,5},{5,9},... | collective-permute-start | bytes 1572872 | tf_op jit(solution)/shard_map/ppermute | solution.py:318
  145.5 19.3 %collective-permute-start.30 = (bf16[64,4096]{1,0:T(8,128)(2,1)S(1)}, bf16[64,4096]{1,0:T(8,128)(2,1)S(1)}, u32[]{:S(2)}, u32[]{:S(2)}) collective-permute-start(bf16[64,4096]{1,0:T(8,128)(2,1)S(1)} %shard_map.102), channel_id=1, source_target_pairs={{4,0},{8,4},{12,8},{14,12},{10,14},{6,10},{2,6},{0,2},{5,1},{9,5},... | collective-permute-start | bytes 1572872 | tf_op jit(solution)/shard_map/ppermute | solution.py:321
  153.5 21.4 %collective-permute-start.22 = (bf16[64,4096]{1,0:T(8,128)(2,1)S(1)}, bf16[64,4096]{1,0:T(8,128)(2,1)S(1)}, u32[]{:S(2)}, u32[]{:S(2)}) collective-permute-start(bf16[64,4096]{1,0:T(8,128)(2,1)S(1)} %shard_map.86), channel_id=1, source_target_pairs={{0,4},{4,8},{8,12},{12,14},{14,10},{10,6},{6,2},{2,0},{1,5},{5,9},... | collective-permute-start | bytes 1572872 | tf_op jit(solution)/shard_map/ppermute | solution.py:318
  154.2 20.7 %collective-permute-start.32 = (bf16[64,4096]{1,0:T(8,128)(2,1)S(1)}, bf16[64,4096]{1,0:T(8,128)(2,1)S(1)}, u32[]{:S(2)}, u32[]{:S(2)}) collective-permute-start(bf16[64,4096]{1,0:T(8,128)(2,1)S(1)} %shard_map.104), channel_id=1, source_target_pairs={{4,0},{8,4},{12,8},{14,12},{10,14},{6,10},{2,6},{0,2},{5,1},{9,5},... | collective-permute-start | bytes 1572872 | tf_op jit(solution)/shard_map/ppermute | solution.py:321
  (6 other events, 64.9 us)
